TPU v7x, 32 devices: a whole 2x2x4 slice. The times are simulated.
32 devices in a mesh: dp: 8 (over z, y), mp: 4 (over x, core).
Axes of the slice: x: 2, y: 2, z: 4, core: 2. Of those that a mesh axis runs over, the one named last changes fastest.
Arguments:
- tokens: bfloat16 [64, 8192], P('dp'), may hold values from -1000 to 1000
- norm_gain: float32 [8192], replicated, may hold values from 0.5 to 1.5
- target: bfloat16 [64, 8192], P(None, 'mp'), may hold values from -6 to 6
- w_gate: bfloat16 [8192, 24576], P('mp', 'dp'), may hold values from -0.0625 to 0.0625
- w_up: bfloat16 [8192, 24576], P('mp', 'dp'), may hold values from -0.0625 to 0.0625
- v_gate: bfloat16 [8192, 24576], P('mp', 'dp'), may hold values from -6 to 6
- w_down: bfloat16 [24576, 8192], P('dp', 'mp'), may hold values from -0.0390625 to 0.0390625
- v_down: bfloat16 [24576, 8192], P('dp', 'mp'), may hold values from -6 to 6
Outputs:
- gate_score: bfloat16 [8192, 24576], P('mp', 'dp')
- down_score: bfloat16 [24576, 8192], P('dp', 'mp')
All inputs are finite; a program needn't handle non-finite values.
Results may differ from a plain program's by a relative error of at most 0.0083.
Values may be sent and summed in bfloat16 or wider, within the bound.
No kernel may reach another device: no remote copies, remote signals or barrier semaphores. Data moves between devices by JAX's collectives and lax.ppermute only.
A program may use at most 256 MiB of HBM per device.

v0:
```python
import jax
import jax.numpy as jnp
from jax import lax
from jax.sharding import PartitionSpec as P

epsilon = 1e-06


def contract_rows(left_op, right_op):
    return lax.dot_general(
        left_op, right_op, (((0,), (0,)), ((), ())), preferred_element_type=jnp.float32
    )


def contract_cols(left_op, right_op):
    return lax.dot_general(
        left_op, right_op, (((1,), (1,)), ((), ())), preferred_element_type=jnp.float32
    )


def silu_parts(gate_pre):
    sigmoid_gate = jax.nn.sigmoid(gate_pre)
    activation = gate_pre * sigmoid_gate
    slope_gate = sigmoid_gate * (1.0 + gate_pre * (1.0 - sigmoid_gate))
    curvature = sigmoid_gate * (1.0 - sigmoid_gate) * (2.0 + gate_pre * (1.0 - 2.0 * sigmoid_gate))
    return (activation, slope_gate, curvature)


def per_device(tokens, norm_gain, target, w_gate, w_up, v_gate, w_down, v_down):
    feature_count = tokens.shape[1]
    col_width = w_gate.shape[0]
    col_first = lax.axis_index("mp") * col_width
    tokens_f = tokens.astype(jnp.float32)
    squares = jnp.sum(tokens_f * tokens_f, axis=1, keepdims=True)
    normed_rows = (tokens_f * lax.rsqrt(squares / feature_count + epsilon) * norm_gain).astype(
        jnp.bfloat16
    )
    local_cols = lax.dynamic_slice_in_dim(normed_rows, col_first, col_width, 1)
    normed = lax.all_gather(local_cols, "dp", axis=0, tiled=True)
    gate_part = jnp.dot(normed, w_gate, preferred_element_type=jnp.float32)
    up_part = jnp.dot(normed, w_up, preferred_element_type=jnp.float32)
    tangent_part = jnp.dot(normed, v_gate, preferred_element_type=jnp.float32)
    gate_pre, up_value, tangent = lax.psum((gate_part, up_part, tangent_part), "mp")
    activation, slope_gate, curvature = silu_parts(gate_pre)
    hidden = (activation * up_value).astype(jnp.bfloat16)
    hidden_tan = (slope_gate * up_value * tangent).astype(jnp.bfloat16)
    token_count = normed.shape[0]
    out_part = jnp.dot(hidden, w_down, preferred_element_type=jnp.float32)
    out_tan_part = jnp.dot(hidden_tan, w_down, preferred_element_type=jnp.float32) + jnp.dot(
        hidden, v_down, preferred_element_type=jnp.float32
    )
    output, output_tan = lax.psum((out_part, out_tan_part), "dp")
    residual = ((output - target.astype(jnp.float32)) / token_count).astype(jnp.bfloat16)
    residual_tan = (output_tan / token_count).astype(jnp.bfloat16)
    down_hess = contract_rows(hidden_tan, residual) + contract_rows(hidden, residual_tan)
    back_part = contract_cols(residual, w_down)
    back_tan_part = contract_cols(residual_tan, w_down) + contract_cols(residual, v_down)
    back_grad, back_tangent = lax.psum((back_part, back_tan_part), "mp")
    combined = (
        back_tangent * up_value * slope_gate + back_grad * up_value * curvature * tangent
    ).astype(jnp.bfloat16)
    gate_hess = contract_rows(normed, combined)
    gate_score = (v_gate.astype(jnp.float32) * gate_hess).astype(jnp.bfloat16)
    down_score = (v_down.astype(jnp.float32) * down_hess).astype(jnp.bfloat16)
    return (gate_score, down_score)


def solution(mesh):
    in_specs = (
        P("dp", None),
        P(),
        P(None, "mp"),
        P("mp", "dp"),
        P("mp", "dp"),
        P("mp", "dp"),
        P("dp", "mp"),
        P("dp", "mp"),
    )
    out_specs = (P("mp", "dp"), P("dp", "mp"))
    return jax.shard_map(
        per_device, mesh=mesh, in_specs=in_specs, out_specs=out_specs, check_vma=False
    )
```

profile of v0, /device:TPU:0, one launch (start us, length us, event | category | flops | bytes accessed | tf_op | source)
XLA Modules:
  0.0 306.7 jit_solution(11053444251053752353)
XLA Ops:
  7.2 0.0 all-reduce.11.cloned.1.call-start
  7.2 0.9 convert_element_type.37
  8.1 1.1 multiply_reduce_fusion
  9.2 0.0 copy-start
  9.2 0.9 dynamic-slice
  10.1 0.1 fusion.13
  10.2 32.6 %all_gather.3 = bf16[64,2048]{1,0:T(8,128)(2,1)S(1)} all-gather(bf16[8,2048]{1,0:T(8,128)(2,1)S(1)} %fusion.13), channel_id=1, replica_groups=mesh['dp'=8,'mp'=4] {'dp'}, dimensions={0}, use_global_device_ids=true | all-gather | bytes 294912 | tf_op jit(solution)/shard_map/all_gather | solution.py:39
  42.8 0.0 slice-start.6
  42.8 0.0 slice-start.7
  42.8 7.9 %fusion.18 = f32[64,3072]{1,0:T(8,128)} fusion(bf16[64,2048]{1,0:T(8,128)(2,1)S(1)} %all_gather.3, bf16[2048,3072]{1,0:T(8,128)(2,1)} %param.11), kind=kOutput, calls=%fused_computation.30 | convolution fusion | flops 805306368 | bytes 13631488 | tf_op jit(solution)/shard_map/dot_general | solution.py:40
  50.7 0.0 copy-done
  50.7 0.0 slice-start.8
  50.7 3.2 %fusion.19 = f32[64,3072]{1,0:T(8,128)} fusion(bf16[64,2048]{1,0:T(8,128)(2,1)S(1)} %all_gather.3, bf16[2048,3072]{1,0:T(8,128)(2,1)S(1)} %copy-done), kind=kOutput, calls=%fused_computation.31 | convolution fusion | flops 805306368 | bytes 13631488 | tf_op jit(solution)/shard_map/dot_general | solution.py:41
  53.9 0.0 slice-done.6
  53.9 0.0 slice-done.7
  53.9 0.0 slice-done.8
  53.9 3.2 %fusion.20 = f32[64,3072]{1,0:T(8,128)} fusion(bf16[64,2048]{1,0:T(8,128)(2,1)S(1)} %all_gather.3, bf16[2048,3072]{1,0:T(8,128)(2,1)S(1)} %bitcast.26), kind=kOutput, calls=%fused_computation.32 | convolution fusion | flops 805306368 | bytes 13631488 | tf_op jit(solution)/shard_map/dot_general | solution.py:42
  57.1 0.0 all-reduce.11.cloned.1.call-update
  57.1 0.0 all-reduce.7.cloned.1.call-start
  57.2 57.1 %all-reduce.11.cloned.1.call-done = (f32[64,3072]{1,0:T(8,128)}, f32[64,3072]{1,0:T(8,128)}, f32[64,3072]{1,0:T(8,128)}) async-done(((f32[64,3072]{1,0:T(8,128)}, f32[64,3072]{1,0:T(8,128)}, f32[64,3072]{1,0:T(8,128)}), (f32[64,3072]{1,0:T(8,128)}, f32[64,3072]{1,0:T(8,128)}, f32[64,3072]{1,0:T(8,128)})) %all-reduce.11.cloned.1.call-update) | async-done | bytes 2359312 | tf_op jit(solution)/shard_map/psum | solution.py:43
  114.3 2.0 multiply_convert_fusion.3
  116.3 0.0 slice-start.3
  116.3 0.0 slice-start.4
  116.3 7.0 %fusion.21 = f32[64,2048]{1,0:T(8,128)S(1)} fusion(bf16[64,3072]{1,0:T(8,128)(2,1)S(1)} %get-tuple-element.9, bf16[3072,2048]{1,0:T(8,128)(2,1)} %param.14), kind=kOutput, calls=%fused_computation.33 | convolution fusion | flops 805306368 | bytes 13500416 | tf_op jit(solution)/shard_map/dot_general | solution.py:49
  123.3 0.0 slice-start.5
  123.4 7.8 %fusion.22 = f32[64,2048]{1,0:T(8,128)} fusion(bf16[64,3072]{1,0:T(8,128)(2,1)S(1)} %get-tuple-element.10, bf16[3072,2048]{1,0:T(8,128)(2,1)} %param.14), kind=kOutput, calls=%fused_computation.34 | convolution fusion | flops 805306368 | bytes 13500416 | tf_op jit(solution)/shard_map/dot_general | solution.py:48
  131.2 0.0 slice-done.3
  131.2 0.0 slice-done.4
  131.2 0.0 slice-done.5
  131.2 0.0 copy-start.5
  131.2 3.1 %convolution_add_fusion.1 = f32[64,2048]{1,0:T(8,128)} fusion(f32[64,2048]{1,0:T(8,128)S(1)} %fusion.21, bf16[64,3072]{1,0:T(8,128)(2,1)S(1)} %get-tuple-element.10, bf16[3072,2048]{1,0:T(8,128)(2,1)S(1)} %bitcast.24), kind=kOutput, calls=%fused_computation.3 | convolution fusion | flops 805437440 | bytes 14024704 | tf_op jit(solution)/shard_map/dot_general | solution.py:49
  134.3 0.0 all-reduce.7.cloned.1.call-update
  134.3 0.2 all-reduce.9.cloned.1.call-start
  134.6 78.4 %all-reduce.7.cloned.1.call-done = (f32[64,2048]{1,0:T(8,128)}, f32[64,2048]{1,0:T(8,128)}) async-done(((f32[64,2048]{1,0:T(8,128)}, f32[64,2048]{1,0:T(8,128)}), (f32[64,2048]{1,0:T(8,128)}, f32[64,2048]{1,0:T(8,128)})) %all-reduce.7.cloned.1.call-update) | async-done | bytes 1048592 | tf_op jit(solution)/shard_map/psum | solution.py:52
  213.0 0.0 copy-done.5
  213.0 1.1 multiply_convert_fusion.4
  214.1 0.0 slice-start
  214.1 0.0 slice-start.1
  214.1 10.5 %fusion.24 = f32[3072,2048]{1,0:T(8,128)} fusion(bf16[64,3072]{1,0:T(8,128)(2,1)S(1)} %get-tuple-element.9, bf16[64,2048]{1,0:T(8,128)(2,1)S(1)} %multiply_convert_fusion.4), kind=kOutput, calls=%fused_computation.36 | convolution fusion | flops 805306368 | bytes 25821184 | tf_op jit(solution)/shard_map/dot_general | solution.py:10
  224.6 0.0 slice-start.2
  224.6 0.0 copy-start.4
  224.6 9.5 %fusion.23 = f32[64,3072]{1,0:T(8,128)} fusion(bf16[64,2048]{1,0:T(8,128)(2,1)S(1)} %multiply_convert_fusion.4, bf16[3072,2048]{1,0:T(8,128)(2,1)} %param.14), kind=kOutput, calls=%fused_computation.35 | convolution fusion | flops 805306368 | bytes 13631488 | tf_op jit(solution)/shard_map/dot_general | solution.py:16
  234.1 0.0 slice-done
  234.2 0.0 slice-done.1
  234.2 0.0 slice-done.2
  234.2 0.0 copy-done.4
  234.2 3.9 %fusion.11 = f32[64,3072]{1,0:T(8,128)S(1)} fusion(bf16[3072,2048]{1,0:T(8,128)(2,1)S(1)} %bitcast.22, f32[64,2048]{1,0:T(8,128)S(1)} %copy-done.4), kind=kOutput, calls=%fused_computation.21 | convolution fusion | flops 805568512 | bytes 13893632 | tf_op jit(solution)/shard_map/dot_general | solution.py:16
  238.1 9.5 %convolution_add_fusion = f32[64,3072]{1,0:T(8,128)} fusion(f32[64,3072]{1,0:T(8,128)S(1)} %fusion.11, bf16[64,2048]{1,0:T(8,128)(2,1)S(1)} %multiply_convert_fusion.4, bf16[3072,2048]{1,0:T(8,128)(2,1)} %param.15), kind=kOutput, calls=%fused_computation.2 | convolution fusion | flops 805502976 | bytes 14417920 | tf_op jit(solution)/shard_map/dot_general | solution.py:16
  247.6 0.0 all-reduce.9.cloned.1.call-update
  247.6 0.0 copy-start.1
  247.6 0.0 copy-start.2
  247.6 0.0 copy-start.3
  247.6 18.9 %multiply_convert_fusion = bf16[3072,2048]{1,0:T(8,128)(2,1)} fusion(f32[3072,2048]{1,0:T(8,128)} %fusion.24, bf16[3072,2048]{1,0:T(8,128)(2,1)} %param.15, bf16[64,3072]{1,0:T(8,128)(2,1)S(1)} %get-tuple-element.10, f32[64,2048]{1,0:T(8,128)S(1)} %copy-done.4), kind=kOutput, calls=%fused_computation | convolution fusion | flops 830734336 | bytes 51249152 | tf_op jit(solution)/shard_map/dot_general | solution.py:10
  266.6 23.7 %all-reduce.9.cloned.1.call-done = (f32[64,3072]{1,0:T(8,128)}, f32[64,3072]{1,0:T(8,128)}) async-done(((f32[64,3072]{1,0:T(8,128)}, f32[64,3072]{1,0:T(8,128)}), (f32[64,3072]{1,0:T(8,128)}, f32[64,3072]{1,0:T(8,128)})) %all-reduce.9.cloned.1.call-update) | async-done | bytes 1572880 | tf_op jit(solution)/shard_map/psum | solution.py:58
  290.3 0.0 copy-done.1
  290.3 0.0 copy-done.2
  290.3 0.0 copy-done.3
  290.3 9.8 %multiply_convert_fusion.1 = bf16[2048,3072]{1,0:T(8,128)(2,1)} fusion(bf16[2048,3072]{1,0:T(8,128)(2,1)} %param.13, bf16[64,2048]{1,0:T(8,128)(2,1)S(1)} %all_gather.3, f32[64,3072]{1,0:T(8,128)S(1)} %copy-done.1, f32[64,3072]{1,0:T(8,128)S(1)} %copy-done.2, f32[64,3072]{1,0:T(8,128)} %get-tuple-element.4, f32[64,3072]{1,0:T(8,128)S(1)} %copy-done.3, ...), kind=kOutput, calls=%fused_computation.1 | convolution fusion | flops 828112896 | bytes 29360128 | tf_op jit(solution)/shard_map/dot_general | solution.py:10
  (4 shorter events, 0.0 us)
Async XLA Ops:
  7.2 107.2 %all-reduce.11.cloned.1.call-start = ((), (), s32[]{:S(2)}) async-start(), calls=%async_computation.2 | async-start | bytes 4718592 | tf_op jit(solution)/shard_map/psum | solution.py:43
  9.2 41.5 %copy-start = (bf16[2048,3072]{1,0:T(8,128)(2,1)S(1)}, bf16[2048,3072]{1,0:T(8,128)(2,1)}, u32[]{:S(2)}) copy-start(bf16[2048,3072]{1,0:T(8,128)(2,1)} %param.12) | copy-start | bytes 37748740
  42.8 11.1 %slice-start.6 = ((s8[12582912]{0:T(1024)(128)(4,1)}), s8[4194304]{0:T(1024)(128)(4,1)S(1)}, s32[]{:S(2)}) async-start(s8[12582912]{0:T(1024)(128)(4,1)} %bitcast.25), calls=%async_computation.9 | async-start | bytes 8388608
  42.8 11.1 %slice-start.7 = ((s8[12582912]{0:T(1024)(128)(4,1)}), s8[4194304]{0:T(1024)(128)(4,1)S(1)}, s32[]{:S(2)}) async-start(s8[12582912]{0:T(1024)(128)(4,1)} %bitcast.25), calls=%async_computation.10 | async-start | bytes 8388608
  50.7 3.2 %slice-start.8 = ((s8[12582912]{0:T(1024)(128)(4,1)}), s8[4194304]{0:T(1024)(128)(4,1)S(1)}, s32[]{:S(2)}) async-start(s8[12582912]{0:T(1024)(128)(4,1)} %bitcast.25), calls=%async_computation.11 | async-start | bytes 8388608
  57.1 155.8 %all-reduce.7.cloned.1.call-start = ((), (), s32[]{:S(2)}) async-start(), calls=%async_computation | async-start | bytes 2097152 | tf_op jit(solution)/shard_map/psum | solution.py:52
  116.3 14.9 %slice-start.3 = ((s8[12582912]{0:T(1024)(128)(4,1)}), s8[4194304]{0:T(1024)(128)(4,1)S(1)}, s32[]{:S(2)}) async-start(s8[12582912]{0:T(1024)(128)(4,1)} %bitcast.23), calls=%async_computation.6 | async-start | bytes 8388608
  116.3 14.9 %slice-start.4 = ((s8[12582912]{0:T(1024)(128)(4,1)}), s8[4194304]{0:T(1024)(128)(4,1)S(1)}, s32[]{:S(2)}) async-start(s8[12582912]{0:T(1024)(128)(4,1)} %bitcast.23), calls=%async_computation.7 | async-start | bytes 8388608
  123.3 7.8 %slice-start.5 = ((s8[12582912]{0:T(1024)(128)(4,1)}), s8[4194304]{0:T(1024)(128)(4,1)S(1)}, s32[]{:S(2)}) async-start(s8[12582912]{0:T(1024)(128)(4,1)} %bitcast.23), calls=%async_computation.8 | async-start | bytes 8388608
  131.2 81.8 %copy-start.5 = (bf16[64,2048]{1,0:T(8,128)(2,1)S(1)}, bf16[64,2048]{1,0:T(8,128)(2,1)}, u32[]{:S(2)}) copy-start(bf16[64,2048]{1,0:T(8,128)(2,1)} %param.10) | copy-start | bytes 786436
  134.3 156.0 %all-reduce.9.cloned.1.call-start = ((), (), s32[]{:S(2)}) async-start(), calls=%async_computation.1 | async-start | bytes 3145728 | tf_op jit(solution)/shard_map/psum | solution.py:58
  214.1 20.0 %slice-start = ((s8[12582912]{0:T(1024)(128)(4,1)}), s8[4194304]{0:T(1024)(128)(4,1)S(1)}, s32[]{:S(2)}) async-start(s8[12582912]{0:T(1024)(128)(4,1)} %bitcast.21), calls=%async_computation.3 | async-start | bytes 8388608
  214.1 20.0 %slice-start.1 = ((s8[12582912]{0:T(1024)(128)(4,1)}), s8[4194304]{0:T(1024)(128)(4,1)S(1)}, s32[]{:S(2)}) async-start(s8[12582912]{0:T(1024)(128)(4,1)} %bitcast.21), calls=%async_computation.4 | async-start | bytes 8388608
  224.6 9.5 %slice-start.2 = ((s8[12582912]{0:T(1024)(128)(4,1)}), s8[4194304]{0:T(1024)(128)(4,1)S(1)}, s32[]{:S(2)}) async-start(s8[12582912]{0:T(1024)(128)(4,1)} %bitcast.21), calls=%async_computation.5 | async-start | bytes 8388608
  224.6 9.5 %copy-start.4 = (f32[64,2048]{1,0:T(8,128)S(1)}, f32[64,2048]{1,0:T(8,128)}, u32[]{:S(2)}) copy-start(f32[64,2048]{1,0:T(8,128)} %get-tuple-element.3) | copy-start | bytes 1572868
  247.6 42.7 %copy-start.1 = (f32[64,3072]{1,0:T(8,128)S(1)}, f32[64,3072]{1,0:T(8,128)}, u32[]{:S(2)}) copy-start(f32[64,3072]{1,0:T(8,128)} %get-tuple-element.6) | copy-start | bytes 2359300
  247.6 42.7 %copy-start.2 = (f32[64,3072]{1,0:T(8,128)S(1)}, f32[64,3072]{1,0:T(8,128)}, u32[]{:S(2)}) copy-start(f32[64,3072]{1,0:T(8,128)} %get-tuple-element.7) | copy-start | bytes 2359300
  247.6 42.7 %copy-start.3 = (f32[64,3072]{1,0:T(8,128)S(1)}, f32[64,3072]{1,0:T(8,128)}, u32[]{:S(2)}) copy-start(f32[64,3072]{1,0:T(8,128)} %get-tuple-element.8) | copy-start | bytes 2359300
Sparse Core Ops, SparseCore 0:
  57.3 57.0 all-reduce.10
  134.4 78.4 all-reduce.6
  247.7 42.5 all-reduce.8
where the time goes:
time: 307 us
  waiting for transfers between devices  159 us (52%)
  matrix products  94.4 us (31%)
  blocking collectives  32.6 us (11%)
  between operations  13.9 us (5%)
  other arithmetic  5.18 us (2%)
    psum x1, waiting for transfers between devices, per_device(): output, output_tan = lax.psum((out_part, out_tan_part), 'dp')  78.4 us
    psum x1, waiting for transfers between devices, per_device(): lax.psum((gate_part, up_part, tangent_part), 'mp')  57.1 us
    dot_general x3, matrix products, contract_rows(): lax.dot_general(left_op, right_op, (((0,), (0,)), ((), ())), preferred_el...  39.3 us
    all_gather x1, blocking collectives, per_device(): normed = lax.all_gather(local_cols, 'dp', axis=0, tiled=True)  32.6 us
    psum x1, waiting for transfers between devices, per_device(): back_grad, back_tangent = lax.psum((back_part, back_tan_part), 'mp')  23.7 us
    dot_general x3, matrix products, contract_cols(): lax.dot_general(left_op, right_op, (((1,), (1,)), ((), ())), preferred_el...  22.9 us
    dot_general x1, matrix products, per_device(): gate_part = jnp.dot(normed, w_gate, preferred_element_type=jnp.float32)  7.9 us
    dot_general x1, matrix products, per_device(): out_part = jnp.dot(hidden, w_down, preferred_element_type=jnp.float32)  7.82 us
  transfers between devices with their start and end apart: 3, of which 3 were waited for; matrix products, arithmetic and copies ran while one was open for 6% of the time, Pallas kernels for 0%

commit v1 on v0

v1 whole, which is shorter than its diff:
```python
import jax
import jax.numpy as jnp
from jax import lax
from jax.sharding import PartitionSpec as P

epsilon = 1e-06
bf16 = jnp.bfloat16
f32 = jnp.float32


def contract_rows(left_op, right_op):
    return lax.dot_general(
        left_op, right_op, (((0,), (0,)), ((), ())), preferred_element_type=f32
    )


def contract_cols(left_op, right_op):
    return lax.dot_general(
        left_op, right_op, (((1,), (1,)), ((), ())), preferred_element_type=f32
    )


def silu_parts(gate_pre):
    sigmoid_gate = jax.nn.sigmoid(gate_pre)
    activation = gate_pre * sigmoid_gate
    slope_gate = sigmoid_gate * (1.0 + gate_pre * (1.0 - sigmoid_gate))
    curvature = sigmoid_gate * (1.0 - sigmoid_gate) * (2.0 + gate_pre * (1.0 - 2.0 * sigmoid_gate))
    return (activation, slope_gate, curvature)


def swap_core(value):
    return lax.ppermute(value, "mp", [(i, i ^ 1) for i in range(4)])


def swap_chip(value):
    return lax.ppermute(value, "mp", [(i, i ^ 2) for i in range(4)])


def reduce_mp(parts, core):
    half = parts.shape[1] // 2
    keep = lax.dynamic_slice_in_dim(parts, core * half, half, 1)
    send = lax.dynamic_slice_in_dim(parts, (1 - core) * half, half, 1).astype(bf16)
    chip_sum = keep + swap_core(send).astype(f32)
    return chip_sum + swap_chip(chip_sum.astype(bf16)).astype(f32)


def gather_core(mine, core):
    other = swap_core(mine)
    low = jnp.where(core == 0, mine, other)
    high = jnp.where(core == 0, other, mine)
    return jnp.concatenate([low, high], axis=1)


def gather_dp(block, dp):
    copies = jnp.broadcast_to(block[None], (dp,) + block.shape)
    return lax.all_to_all(copies, "dp", 0, 0, tiled=True)


def per_device(dp, tokens, norm_gain, target, w_gate, w_up, v_gate, w_down, v_down):
    feature_count = tokens.shape[1]
    own = tokens.shape[0]
    token_count = own * dp
    col_width = w_gate.shape[0]
    mp_id = lax.axis_index("mp")
    dp_id = lax.axis_index("dp")
    core = mp_id % 2
    col_first = mp_id * col_width
    tokens_f = tokens.astype(f32)
    squares = jnp.sum(tokens_f * tokens_f, axis=1, keepdims=True)
    normed_rows = (tokens_f * lax.rsqrt(squares / feature_count + epsilon) * norm_gain).astype(bf16)
    local_cols = lax.dynamic_slice_in_dim(normed_rows, col_first, col_width, 1)
    normed = gather_dp(local_cols, dp).reshape(token_count, col_width)
    gate_part = jnp.dot(normed, w_gate, preferred_element_type=f32)
    up_part = jnp.dot(normed, w_up, preferred_element_type=f32)
    tangent_part = jnp.dot(normed, v_gate, preferred_element_type=f32)
    gate_pre, up_value, tangent = reduce_mp(jnp.stack([gate_part, up_part, tangent_part]), core)
    activation, slope_gate, curvature = silu_parts(gate_pre)
    hidden_half = (activation * up_value).astype(bf16)
    hidden_tan_half = (slope_gate * up_value * tangent).astype(bf16)
    both = gather_core(jnp.stack([hidden_half, hidden_tan_half]), core)
    hidden, hidden_tan = both[0], both[1]
    out_part = jnp.dot(hidden, w_down, preferred_element_type=f32)
    out_tan_part = jnp.dot(hidden_tan, w_down, preferred_element_type=f32) + jnp.dot(
        hidden, v_down, preferred_element_type=f32
    )
    pieces = jnp.stack(
        [out_part.reshape(dp, own, col_width), out_tan_part.reshape(dp, own, col_width)], axis=1
    ).astype(bf16)
    arrived = lax.all_to_all(pieces, "dp", 0, 0, tiled=True).astype(f32)
    totals = jnp.sum(arrived, axis=0)
    target_rows = lax.dynamic_slice_in_dim(target, dp_id * own, own, 0)
    residual_rows = ((totals[0] - target_rows.astype(f32)) / token_count).astype(bf16)
    residual_tan_rows = (totals[1] / token_count).astype(bf16)
    spread = gather_dp(jnp.stack([residual_rows, residual_tan_rows]), dp)
    residual = spread[:, 0].reshape(token_count, col_width)
    residual_tan = spread[:, 1].reshape(token_count, col_width)
    back_part = contract_cols(residual, w_down)
    back_tan_part = contract_cols(residual_tan, w_down) + contract_cols(residual, v_down)
    back_grad, back_tangent = reduce_mp(jnp.stack([back_part, back_tan_part]), core)
    down_hess = contract_rows(hidden_tan, residual) + contract_rows(hidden, residual_tan)
    down_score = (v_down.astype(f32) * down_hess).astype(bf16)
    combined_half = (
        back_tangent * up_value * slope_gate + back_grad * up_value * curvature * tangent
    ).astype(bf16)
    combined = gather_core(combined_half[None], core)[0]
    gate_hess = contract_rows(normed, combined)
    gate_score = (v_gate.astype(f32) * gate_hess).astype(bf16)
    return (gate_score, down_score)


def solution(mesh):
    dp = mesh.shape["dp"]
    in_specs = (
        P("dp", None),
        P(),
        P(None, "mp"),
        P("mp", "dp"),
        P("mp", "dp"),
        P("mp", "dp"),
        P("dp", "mp"),
        P("dp", "mp"),
    )
    out_specs = (P("mp", "dp"), P("dp", "mp"))

    def body(*args):
        return per_device(dp, *args)

    return jax.shard_map(body, mesh=mesh, in_specs=in_specs, out_specs=out_specs, check_vma=False)
```

time: 307 us -> 176 us (0.57)
  waiting for transfers between devices: 159 us -> 43.1 us
  blocking collectives: 32.6 us -> 18.3 us
  starting transfers between devices: 0.3 us -> 14.2 us
  between operations: 13.9 us -> 1 us
  matrix products: 94.4 us -> 86.7 us
  local copies, waits for them, and re-layouts: 0.93 us -> 6.16 us
    psum x3 -> x0, waiting for transfers between devices: 159 us -> none  [the longest x1 78.4 us: per_device(): output, output_tan = lax.psum((out_part, out_tan_part), 'dp')]
    all_gather x1 -> x0, blocking collectives: 32.6 us -> none  [per_device(): normed = lax.all_gather(local_cols, 'dp', axis=0, tiled=True)]
    all_to_all x0 -> x2, waiting for transfers between devices: none -> 23.8 us  [the longest x1 14.9 us: per_device(): arrived = lax.all_to_all(pieces, 'dp', 0, 0, tiled=True).astype(f32)]
    ppermute x0 -> x6, waiting for transfers between devices: none -> 19.3 us  [the longest x2 13.9 us: swap_chip(): return lax.ppermute(value, 'mp', [(i, i ^ 2) for i in range(4)])]
    all_to_all x0 -> x1, blocking collectives: none -> 18.3 us  [gather_dp(): return lax.all_to_all(copies, 'dp', 0, 0, tiled=True)]
    all_to_all x0 -> x2, starting transfers between devices: none -> 10.9 us  [the longest x1 7.28 us: gather_dp(): return lax.all_to_all(copies, 'dp', 0, 0, tiled=True)]
    dot_general x6, matrix products: 32.2 us -> 28 us  [the longest x1 7.04 us: per_device(): out_part = jnp.dot(hidden, w_down, preferred_element_type=f32)]
    dot_general x3, matrix products: 39.3 us -> 35.4 us  [contract_rows(): lax.dot_general(left_op, right_op, (((0,), (0,)), ((), ())), preferred_el...]
  transfers between devices with their start and end apart: 3 -> 8, of which waited for: 3 -> 6; matrix products, arithmetic and copies ran while one was open for 6% -> 15% of each run, Pallas kernels for 0% -> 0%
where the time goes in v1:
time: 176 us
  matrix products  86.7 us (49%)
  waiting for transfers between devices  43.1 us (24%)
  blocking collectives  18.3 us (10%)
  starting transfers between devices  14.2 us (8%)
  local copies, waits for them, and re-layouts  6.16 us (4%)
  other arithmetic  6.08 us (3%)
    dot_general x3, matrix products, contract_rows(): lax.dot_general(left_op, right_op, (((0,), (0,)), ((), ())), preferred_el...  35.4 us
    dot_general x3, matrix products, contract_cols(): lax.dot_general(left_op, right_op, (((1,), (1,)), ((), ())), preferred_el...  23.4 us
    all_to_all x1, blocking collectives, gather_dp(): return lax.all_to_all(copies, 'dp', 0, 0, tiled=True)  18.3 us
    all_to_all x1, waiting for transfers between devices, per_device(): arrived = lax.all_to_all(pieces, 'dp', 0, 0, tiled=True).astype(f32)  14.9 us
    ppermute x2, waiting for transfers between devices, swap_chip(): return lax.ppermute(value, 'mp', [(i, i ^ 2) for i in range(4)])  13.9 us
    all_to_all x1, waiting for transfers between devices, gather_dp(): return lax.all_to_all(copies, 'dp', 0, 0, tiled=True)  8.92 us
    all_to_all x1, starting transfers between devices, gather_dp(): return lax.all_to_all(copies, 'dp', 0, 0, tiled=True)  7.28 us
    dot_general x1, matrix products, per_device(): out_part = jnp.dot(hidden, w_down, preferred_element_type=f32)  7.04 us
  transfers between devices with their start and end apart: 8, of which 6 were waited for; matrix products, arithmetic and copies ran while one was open for 15% of the time, Pallas kernels for 0%

profile of v1, /device:TPU:0, one launch (start us, length us, event | category | flops | bytes accessed | tf_op | source)
XLA Modules:
  0.0 175.5 jit_solution(685798894885447621)
XLA Ops:
  0.6 0.9 convert_element_type.69
  1.6 1.1 multiply_reduce_fusion
  2.7 0.7 dynamic-slice
  3.4 0.1 fusion.43
  3.4 0.7 broadcast_in_dim.4
  4.2 7.3 %all-to-all-start = ((bf16[8,8,2048]{2,1,0:T(8,128)(2,1)}), bf16[8,8,2048]{2,1,0:T(8,128)(2,1)S(1)}, u32[]{:S(2)}, u32[]{:S(2)}) async-start(bf16[8,8,2048]{2,1,0:T(8,128)(2,1)} %broadcast_in_dim.4), calls=%async_computation | async-start | bytes 524288 | tf_op jit(solution)/shard_map/all_to_all | solution.py:56
  11.4 8.9 %all-to-all-done = bf16[8,8,2048]{2,1,0:T(8,128)(2,1)S(1)} async-done(((bf16[8,8,2048]{2,1,0:T(8,128)(2,1)}), bf16[8,8,2048]{2,1,0:T(8,128)(2,1)S(1)}, u32[]{:S(2)}, u32[]{:S(2)}) %all-to-all-start) | async-done | bytes 262176 | tf_op jit(solution)/shard_map/all_to_all | solution.py:56
  20.4 7.0 %convolution_bitcast_fusion.1 = f32[1,64,3072]{2,1,0:T(8,128)S(1)} fusion(bf16[2048,3072]{1,0:T(8,128)(2,1)} %param.13, bf16[8,8,2048]{2,1,0:T(8,128)(2,1)S(1)} %all-to-all-done), kind=kOutput, calls=%fused_computation.7 | convolution fusion | flops 805306368 | bytes 13631488 | tf_op jit(solution)/shard_map/dot_general | solution.py:75
  27.4 1.2 copy-done
  28.6 2.3 %convolution_bitcast_fusion.2 = f32[1,64,3072]{2,1,0:T(8,128)S(1)} fusion(bf16[2048,3072]{1,0:T(8,128)(2,1)S(1)} %copy-done, bf16[8,8,2048]{2,1,0:T(8,128)(2,1)S(1)} %all-to-all-done), kind=kOutput, calls=%fused_computation.8 | convolution fusion | flops 805306368 | bytes 13631488 | tf_op jit(solution)/shard_map/dot_general | solution.py:74
  30.9 0.0 copy-done.3
  30.9 0.0 slice-done.6
  30.9 0.1 slice-done.7
  31.0 1.4 slice-done.8
  32.4 2.3 %convolution_bitcast_fusion.3 = f32[1,64,3072]{2,1,0:T(8,128)S(1)} fusion(bf16[2048,3072]{1,0:T(8,128)(2,1)S(1)} %bitcast.79, bf16[8,8,2048]{2,1,0:T(8,128)(2,1)S(1)} %all-to-all-done), kind=kOutput, calls=%fused_computation.9 | convolution fusion | flops 805306368 | bytes 13631488 | tf_op jit(solution)/shard_map/dot_general | solution.py:73
  34.7 0.2 pad_maximum_fusion
  35.0 0.1 dynamic-slice_convert_fusion
  35.1 0.1 collective-permute-start
  35.1 2.0 %collective-permute-done = bf16[3,32,3072]{2,1,0:T(8,128)(2,1)S(1)} collective-permute-done((bf16[3,32,3072]{2,1,0:T(8,128)(2,1)S(1)}, bf16[3,32,3072]{2,1,0:T(8,128)(2,1)S(1)}, u32[]{:S(2)}, u32[]{:S(2)}) %collective-permute-start) | collective-permute-done | bytes 589856 | tf_op jit(solution)/shard_map/ppermute | solution.py:32
  37.1 0.1 fusion.15
  37.2 1.6 collective-permute-start.1
  38.8 13.9 %collective-permute-done.1 = bf16[3,32,3072]{2,1,0:T(8,128)(2,1)S(1)} collective-permute-done((bf16[3,32,3072]{2,1,0:T(8,128)(2,1)S(1)}, bf16[3,32,3072]{2,1,0:T(8,128)(2,1)S(1)}, u32[]{:S(2)}, u32[]{:S(2)}) %collective-permute-start.1) | collective-permute-done | bytes 589856 | tf_op jit(solution)/shard_map/ppermute | solution.py:36
  52.7 0.2 convert_add_fusion
  52.9 0.0 copy-start.4
  52.9 1.0 copy-done.4
  53.9 0.2 multiply_convert_fusion.3
  54.1 0.1 collective-permute-start.2
  54.2 1.7 collective-permute-done.2
  55.9 0.1 broadcast_select_fusion
  56.0 0.0 copy-start.1
  56.0 0.0 slice-start
  56.0 0.0 slice-start.1
  56.0 7.0 %fusion.7 = bf16[8,1,8,2048]{3,2,0,1:T(8,128)(2,1)S(1)} fusion(bf16[3072,2048]{1,0:T(8,128)(2,1)} %param.14, bf16[2,32,3072]{2,1,0:T(8,128)(2,1)S(1)} %get-tuple-element.5, bf16[2,32,3072]{2,1,0:T(8,128)(2,1)S(1)} %get-tuple-element.4), kind=kOutput, calls=%fused_computation.14 | convolution fusion | flops 806223872 | bytes 13631488 | tf_op jit(solution)/shard_map/dot_general | solution.py:82
  63.1 0.0 slice-start.2
  63.1 7.0 %fusion.30 = f32[64,2048]{1,0:T(8,128)S(1)} fusion(bf16[3072,2048]{1,0:T(8,128)(2,1)} %param.15, bf16[2,32,3072]{2,1,0:T(8,128)(2,1)S(1)} %get-tuple-element.5, bf16[2,32,3072]{2,1,0:T(8,128)(2,1)S(1)} %get-tuple-element.4), kind=kOutput, calls=%fused_computation.54 | convolution fusion | flops 806092800 | bytes 13893632 | tf_op jit(solution)/shard_map/dot_general | solution.py:83
  70.1 0.0 copy-done.1
  70.1 0.0 slice-done
  70.1 0.0 slice-done.1
  70.1 0.0 slice-done.2
  70.2 2.3 %fusion.10 = bf16[8,1,8,2048]{3,2,0,1:T(8,128)(2,1)S(1)} fusion(f32[64,2048]{1,0:T(8,128)S(1)} %fusion.30, bf16[3072,2048]{1,0:T(8,128)(2,1)S(1)} %bitcast.75, bf16[2,32,3072]{2,1,0:T(8,128)(2,1)S(1)} %get-tuple-element.4, bf16[2,32,3072]{2,1,0:T(8,128)(2,1)S(1)} %get-tuple-element.5), kind=kOutput, calls=%fused_computation.15 | convolution fusion | flops 806354944 | bytes 14155776 | tf_op jit(solution)/shard_map/dot_general | solution.py:83
  72.5 0.1 pad_maximum_fusion.1
  72.5 0.8 copy.10
  73.3 3.6 %all-to-all-start.1 = ((bf16[8,2,8,2048]{3,2,1,0:T(8,128)(2,1)}), bf16[8,2,8,2048]{3,2,1,0:T(8,128)(2,1)S(1)}, u32[]{:S(2)}, u32[]{:S(2)}) async-start(bf16[8,2,8,2048]{3,2,1,0:T(8,128)(2,1)} %copy.10), calls=%async_computation.1 | async-start | bytes 1048576 | tf_op jit(solution)/shard_map/all_to_all | solution.py:89
  76.9 14.9 %all-to-all-done.1 = bf16[8,2,8,2048]{3,2,1,0:T(8,128)(2,1)S(1)} async-done(((bf16[8,2,8,2048]{3,2,1,0:T(8,128)(2,1)}), bf16[8,2,8,2048]{3,2,1,0:T(8,128)(2,1)S(1)}, u32[]{:S(2)}, u32[]{:S(2)}) %all-to-all-start.1) | async-done | bytes 524320 | tf_op jit(solution)/shard_map/all_to_all | solution.py:89
  91.8 0.1 convert_reduce_fusion
  91.9 0.8 fusion.46
  92.8 18.3 %all_to_all.15 = bf16[8,2,8,2048]{3,2,1,0:T(8,128)(2,1)S(1)} all-to-all(bf16[8,2,8,2048]{3,2,1,0:T(8,128)(2,1)S(1)} %broadcast_in_dim.5), channel_id=1, replica_groups=mesh['dp'=8,'mp'=4] {'dp'}, dimensions={0} | all-to-all | bytes 1048576 | tf_op jit(solution)/shard_map/all_to_all | solution.py:56
  111.0 9.6 %fusion.37 = f32[64,3072]{1,0:T(8,128)} fusion(bf16[3072,2048]{1,0:T(8,128)(2,1)} %param.14, bf16[8,2,8,2048]{3,2,1,0:T(8,128)(2,1)S(1)} %all_to_all.15), kind=kOutput, calls=%fused_computation.69 | convolution fusion | flops 805306368 | bytes 13631488 | tf_op jit(solution)/shard_map/dot_general | solution.py:18
  120.7 8.6 %convolution_bitcast_fusion = f32[1,64,3072]{2,1,0:T(8,128)S(1)} fusion(bf16[3072,2048]{1,0:T(8,128)(2,1)} %param.14, bf16[8,2,8,2048]{3,2,1,0:T(8,128)(2,1)S(1)} %all_to_all.15), kind=kOutput, calls=%fused_computation.6 | convolution fusion | flops 805306368 | bytes 13631488 | tf_op jit(solution)/shard_map/dot_general | solution.py:18
  129.4 5.1 %fusion.2 = f32[1,64,3072]{2,1,0:T(8,128)S(1)} fusion(f32[64,3072]{1,0:T(8,128)} %fusion.37, bf16[3072,2048]{1,0:T(8,128)(2,1)S(1)} %bitcast.77, bf16[8,2,8,2048]{3,2,1,0:T(8,128)(2,1)S(1)} %all_to_all.15), kind=kOutput, calls=%fused_computation.5 | convolution fusion | flops 805502976 | bytes 14417920 | tf_op jit(solution)/shard_map/dot_general | solution.py:18
  134.5 0.1 collective-permute-start.3
  134.6 1.7 collective-permute-done.3
  136.3 0.1 fusion.50
  136.4 0.0 copy-start.5
  136.4 1.6 collective-permute-start.4
  138.0 11.1 %fusion.28 = f32[3072,2048]{1,0:T(8,128)} fusion(bf16[8,2,8,2048]{3,2,1,0:T(8,128)(2,1)} %copy-done.6, bf16[2,32,3072]{2,1,0:T(8,128)(2,1)S(1)} %copy-done.2, bf16[2,32,3072]{2,1,0:T(8,128)(2,1)S(1)} %get-tuple-element.4), kind=kOutput, calls=%fused_computation.52 | convolution fusion | flops 806092800 | bytes 26214400 | tf_op jit(solution)/shard_map/dot_general | solution.py:12
  149.0 0.0 collective-permute-done.4
  149.0 0.1 convert_add_fusion.2
  149.1 1.0 fusion.22
  150.1 0.0 collective-permute-start.5
  150.1 14.9 %multiply_convert_fusion = bf16[3072,2048]{1,0:T(8,128)(2,1)} fusion(f32[3072,2048]{1,0:T(8,128)} %fusion.28, bf16[3072,2048]{1,0:T(8,128)(2,1)S(1)} %bitcast.77, bf16[8,2,8,2048]{3,2,1,0:T(8,128)(2,1)} %copy-done.6, bf16[2,32,3072]{2,1,0:T(8,128)(2,1)S(1)} %get-tuple-element.4, bf16[2,32,3072]{2,1,0:T(8,128)(2,1)} %copy-done.1), kind=kOutput, calls=%fused_computation | convolution fusion | flops 831258624 | bytes 51380224 | tf_op jit(solution)/shard_map/dot_general | solution.py:12
  165.1 0.0 collective-permute-done.5
  165.1 1.1 broadcast_select_fusion.3
  166.1 9.4 %multiply_convert_fusion.1 = bf16[2048,3072]{1,0:T(8,128)(2,1)} fusion(bf16[2048,3072]{1,0:T(8,128)(2,1)} %param.13, bf16[1,32,3072]{2,1,0:T(8,128)(2,1)S(1)} %get-tuple-element.7, bf16[1,32,3072]{2,1,0:T(8,128)(2,1)S(1)} %get-tuple-element.6, bf16[8,8,2048]{2,1,0:T(8,128)(2,1)} %copy-done.3), kind=kOutput, calls=%fused_computation.1 | convolution fusion | flops 824967168 | bytes 25821184 | tf_op jit(solution)/shard_map/dot_general | solution.py:12
  (25 shorter events, 0.2 us)
Async XLA Ops:
  4.2 16.2 %all-to-all-start = ((bf16[8,8,2048]{2,1,0:T(8,128)(2,1)}), bf16[8,8,2048]{2,1,0:T(8,128)(2,1)S(1)}, u32[]{:S(2)}, u32[]{:S(2)}) async-start(bf16[8,8,2048]{2,1,0:T(8,128)(2,1)} %broadcast_in_dim.4), calls=%async_computation | async-start | bytes 524288 | tf_op jit(solution)/shard_map/all_to_all | solution.py:56
  20.4 10.6 %copy-start.3 = (bf16[8,8,2048]{2,1,0:T(8,128)(2,1)}, bf16[8,8,2048]{2,1,0:T(8,128)(2,1)S(1)}, u32[]{:S(2)}) copy-start(bf16[8,8,2048]{2,1,0:T(8,128)(2,1)S(1)} %all-to-all-done) | copy-start | bytes 786436
  20.4 8.2 %copy-start = (bf16[2048,3072]{1,0:T(8,128)(2,1)S(1)}, bf16[2048,3072]{1,0:T(8,128)(2,1)}, u32[]{:S(2)}) copy-start(bf16[2048,3072]{1,0:T(8,128)(2,1)} %param.12) | copy-start | bytes 37748740
  20.4 10.6 %slice-start.6 = ((s8[12582912]{0:T(1024)(128)(4,1)}), s8[4194304]{0:T(1024)(128)(4,1)S(1)}, s32[]{:S(2)}) async-start(s8[12582912]{0:T(1024)(128)(4,1)} %bitcast.78), calls=%async_computation.9 | async-start | bytes 8388608
  20.4 10.6 %slice-start.7 = ((s8[12582912]{0:T(1024)(128)(4,1)}), s8[4194304]{0:T(1024)(128)(4,1)S(1)}, s32[]{:S(2)}) async-start(s8[12582912]{0:T(1024)(128)(4,1)} %bitcast.78), calls=%async_computation.10 | async-start | bytes 8388608
  28.6 3.8 %slice-start.8 = ((s8[12582912]{0:T(1024)(128)(4,1)}), s8[4194304]{0:T(1024)(128)(4,1)S(1)}, s32[]{:S(2)}) async-start(s8[12582912]{0:T(1024)(128)(4,1)} %bitcast.78), calls=%async_computation.11 | async-start | bytes 8388608
  35.1 2.1 %collective-permute-start = (bf16[3,32,3072]{2,1,0:T(8,128)(2,1)S(1)}, bf16[3,32,3072]{2,1,0:T(8,128)(2,1)S(1)}, u32[]{:S(2)}, u32[]{:S(2)}) collective-permute-start(bf16[3,32,3072]{2,1,0:T(8,128)(2,1)S(1)} %dynamic-slice_convert_fusion), channel_id=1, source_target_pairs={{0,1},{1,0},{2,3},{3,2},{4,5},{5,4},{6,7},{7,6},{8,9},{9,8},{10,11... | collective-permute-start | bytes 1769480 | tf_op jit(solution)/shard_map/ppermute | solution.py:32
  37.2 15.4 %collective-permute-start.1 = (bf16[3,32,3072]{2,1,0:T(8,128)(2,1)S(1)}, bf16[3,32,3072]{2,1,0:T(8,128)(2,1)S(1)}, u32[]{:S(2)}, u32[]{:S(2)}) collective-permute-start(bf16[3,32,3072]{2,1,0:T(8,128)(2,1)S(1)} %fusion.15), channel_id=1, source_target_pairs={{0,2},{1,3},{2,0},{3,1},{4,6},{5,7},{6,4},{7,5},{8,10},{9,11},{10,... | collective-permute-start | bytes 1769480 | tf_op jit(solution)/shard_map/ppermute | solution.py:36
  52.9 1.0 copy-start.4
  54.1 1.8 %collective-permute-start.2 = (bf16[2,32,3072]{2,1,0:T(8,128)(2,1)S(1)}, bf16[2,32,3072]{2,1,0:T(8,128)(2,1)S(1)}, u32[]{:S(2)}, u32[]{:S(2)}) collective-permute-start(bf16[2,32,3072]{2,1,0:T(8,128)(2,1)S(1)} %pad_maximum_fusion.3), channel_id=1, source_target_pairs={{0,1},{1,0},{2,3},{3,2},{4,5},{5,4},{6,7},{7,6},{8,9},{9,8},{10,11... | collective-permute-start | bytes 1179656 | tf_op jit(solution)/shard_map/ppermute | solution.py:32
  56.0 14.1 %copy-start.1 = (bf16[2,32,3072]{2,1,0:T(8,128)(2,1)}, bf16[2,32,3072]{2,1,0:T(8,128)(2,1)S(1)}, u32[]{:S(2)}) copy-start(bf16[2,32,3072]{2,1,0:T(8,128)(2,1)S(1)} %get-tuple-element.5) | copy-start | bytes 1179652
  56.0 14.1 %slice-start = ((s8[12582912]{0:T(1024)(128)(4,1)}), s8[4194304]{0:T(1024)(128)(4,1)S(1)}, s32[]{:S(2)}) async-start(s8[12582912]{0:T(1024)(128)(4,1)} %bitcast.74), calls=%async_computation.3 | async-start | bytes 8388608
  56.0 14.1 %slice-start.1 = ((s8[12582912]{0:T(1024)(128)(4,1)}), s8[4194304]{0:T(1024)(128)(4,1)S(1)}, s32[]{:S(2)}) async-start(s8[12582912]{0:T(1024)(128)(4,1)} %bitcast.74), calls=%async_computation.4 | async-start | bytes 8388608
  63.1 7.1 %slice-start.2 = ((s8[12582912]{0:T(1024)(128)(4,1)}), s8[4194304]{0:T(1024)(128)(4,1)S(1)}, s32[]{:S(2)}) async-start(s8[12582912]{0:T(1024)(128)(4,1)} %bitcast.74), calls=%async_computation.5 | async-start | bytes 8388608
  73.3 18.5 %all-to-all-start.1 = ((bf16[8,2,8,2048]{3,2,1,0:T(8,128)(2,1)}), bf16[8,2,8,2048]{3,2,1,0:T(8,128)(2,1)S(1)}, u32[]{:S(2)}, u32[]{:S(2)}) async-start(bf16[8,2,8,2048]{3,2,1,0:T(8,128)(2,1)} %copy.10), calls=%async_computation.1 | async-start | bytes 1048576 | tf_op jit(solution)/shard_map/all_to_all | solution.py:89
  111.0 18.3 %copy-start.6 = (bf16[8,2,8,2048]{3,2,1,0:T(8,128)(2,1)}, bf16[8,2,8,2048]{3,2,1,0:T(8,128)(2,1)S(1)}, u32[]{:S(2)}) copy-start(bf16[8,2,8,2048]{3,2,1,0:T(8,128)(2,1)S(1)} %all_to_all.15) | copy-start | bytes 1572868
  111.0 18.3 %slice-start.3 = ((s8[12582912]{0:T(1024)(128)(4,1)}), s8[4194304]{0:T(1024)(128)(4,1)S(1)}, s32[]{:S(2)}) async-start(s8[12582912]{0:T(1024)(128)(4,1)} %bitcast.76), calls=%async_computation.6 | async-start | bytes 8388608
  111.0 18.3 %slice-start.4 = ((s8[12582912]{0:T(1024)(128)(4,1)}), s8[4194304]{0:T(1024)(128)(4,1)S(1)}, s32[]{:S(2)}) async-start(s8[12582912]{0:T(1024)(128)(4,1)} %bitcast.76), calls=%async_computation.7 | async-start | bytes 8388608
  120.7 8.7 %slice-start.5 = ((s8[12582912]{0:T(1024)(128)(4,1)}), s8[4194304]{0:T(1024)(128)(4,1)S(1)}, s32[]{:S(2)}) async-start(s8[12582912]{0:T(1024)(128)(4,1)} %bitcast.76), calls=%async_computation.8 | async-start | bytes 8388608
  129.4 8.6 %copy-start.2 = (bf16[2,32,3072]{2,1,0:T(8,128)(2,1)S(1)}, bf16[2,32,3072]{2,1,0:T(8,128)(2,1)}, u32[]{:S(2)}) copy-start(bf16[2,32,3072]{2,1,0:T(8,128)(2,1)} %copy-done.1) | copy-start | bytes 1179652
  134.5 1.8 %collective-permute-start.3 = (bf16[2,32,3072]{2,1,0:T(8,128)(2,1)S(1)}, bf16[2,32,3072]{2,1,0:T(8,128)(2,1)S(1)}, u32[]{:S(2)}, u32[]{:S(2)}) collective-permute-start(bf16[2,32,3072]{2,1,0:T(8,128)(2,1)S(1)} %fusion.12), channel_id=1, source_target_pairs={{0,1},{1,0},{2,3},{3,2},{4,5},{5,4},{6,7},{7,6},{8,9},{9,8},{10,11... | collective-permute-start | bytes 1179656 | tf_op jit(solution)/shard_map/ppermute | solution.py:32
  136.4 12.7 %copy-start.5 = (f32[3,32,3072]{2,1,0:T(8,128)S(1)}, f32[3,32,3072]{2,1,0:T(8,128)}, u32[]{:S(2)}) copy-start(f32[3,32,3072]{2,1,0:T(8,128)} %copy-done.4) | copy-start | bytes 3538948
  136.4 12.6 %collective-permute-start.4 = (bf16[2,32,3072]{2,1,0:T(8,128)(2,1)S(1)}, bf16[2,32,3072]{2,1,0:T(8,128)(2,1)S(1)}, u32[]{:S(2)}, u32[]{:S(2)}) collective-permute-start(bf16[2,32,3072]{2,1,0:T(8,128)(2,1)S(1)} %fusion.50), channel_id=1, source_target_pairs={{0,2},{1,3},{2,0},{3,1},{4,6},{5,7},{6,4},{7,5},{8,10},{9,11},{10,... | collective-permute-start | bytes 1179656 | tf_op jit(solution)/shard_map/ppermute | solution.py:36
  150.1 14.9 %collective-permute-start.5 = (bf16[1,32,3072]{2,1,0:T(8,128)(2,1)}, bf16[1,32,3072]{2,1,0:T(8,128)(2,1)}, u32[]{:S(2)}, u32[]{:S(2)}) collective-permute-start(bf16[1,32,3072]{2,1,0:T(8,128)(2,1)} %fusion.22), channel_id=1, source_target_pairs={{0,1},{1,0},{2,3},{3,2},{4,5},{5,4},{6,7},{7,6},{8,9},{9,8},{10,11... | collective-permute-start | bytes 589832 | tf_op jit(solution)/shard_map/ppermute | solution.py:32

commit v2 on v0

v2 whole, which is shorter than its diff:
```python
import functools
import jax
import jax.numpy as jnp
from jax import lax
from jax.experimental import pallas as pl
from jax.experimental.pallas import tpu as pltpu
from jax.sharding import PartitionSpec as P

epsilon = 1e-06
bf16 = jnp.bfloat16
f32 = jnp.float32
MIB = 1024 * 1024
IN_VMEM = pl.BlockSpec(memory_space=pltpu.VMEM)
IN_HBM = pl.BlockSpec(memory_space=pltpu.HBM)


def block_of(extent, most):
    size = most
    while extent % size:
        size -= 128
    return size


def params(mebibytes):
    return pltpu.CompilerParams(vmem_limit_bytes=mebibytes * MIB)


def cost(flops, bytes_accessed):
    return pl.CostEstimate(flops=flops, bytes_accessed=bytes_accessed, transcendentals=0)


def dot(left, right, left_dim, right_dim):
    return lax.dot_general(
        left, right, (((left_dim,), (right_dim,)), ((), ())), preferred_element_type=f32
    )


def held(value):
    return pltpu.with_memory_space_constraint(value, pltpu.VMEM)


def kept_out(value):
    return pltpu.with_memory_space_constraint(value, pltpu.HBM)


def silu_parts(gate_pre):
    sigmoid_gate = jax.nn.sigmoid(gate_pre)
    activation = gate_pre * sigmoid_gate
    slope_gate = sigmoid_gate * (1.0 + gate_pre * (1.0 - sigmoid_gate))
    curvature = sigmoid_gate * (1.0 - sigmoid_gate) * (2.0 + gate_pre * (1.0 - 2.0 * sigmoid_gate))
    return (activation, slope_gate, curvature)


def swap_core(value):
    return lax.ppermute(value, "mp", [(i, i ^ 1) for i in range(4)])


def swap_chip(value):
    return lax.ppermute(value, "mp", [(i, i ^ 2) for i in range(4)])


def load_call(weights, after, name):
    n = len(weights)
    parts = 4

    def body(*refs):
        sources, targets, sems = refs[:n], refs[n + 1 : 2 * n + 1], refs[-1]
        copies = []
        for i in range(n):
            rows = sources[i].shape[0] // parts
            for j in range(parts):
                span = pl.ds(j * rows, rows)
                copies.append(
                    pltpu.make_async_copy(
                        sources[i].at[span], targets[i].at[span], sems.at[i, j]
                    )
                )
        for copy in copies:
            copy.start()
        for copy in copies:
            copy.wait()

    size = sum(w.size * 2 for w in weights)
    return pl.pallas_call(
        body,
        in_specs=[IN_HBM] * n + [pl.BlockSpec(memory_space=pl.ANY)],
        out_specs=[IN_VMEM] * n,
        out_shape=[pltpu.VMEM(w.shape, w.dtype) for w in weights],
        scratch_shapes=[pltpu.SemaphoreType.DMA((n, parts))],
        compiler_params=params(1),
        cost_estimate=cost(0, 2 * size),
        name=name,
    )(*[kept_out(w) for w in weights], after)


def norm_call(tokens, norm_gain, copies, col_width):
    own, features = tokens.shape

    def body(tokens_ref, gain_ref, out_ref, scaled):
        tokens_f = tokens_ref[...].astype(f32)
        squares = jnp.sum(tokens_f * tokens_f, axis=1, keepdims=True)
        scaled[...] = tokens_f * lax.rsqrt(squares / features + epsilon) * gain_ref[...]
        first = pl.multiple_of(lax.axis_index("mp") * col_width, col_width)
        mine = scaled[:, pl.ds(first, col_width)].astype(bf16)
        for i in range(copies):
            out_ref[i] = mine

    return pl.pallas_call(
        body,
        out_shape=jax.ShapeDtypeStruct((copies, own, col_width), bf16),
        scratch_shapes=[pltpu.VMEM((own, features), f32)],
        compiler_params=params(8),
        name="norm_rows",
    )(tokens, norm_gain.reshape(1, features))


def gate_call(normed, w_gate, w_up, v_gate, chunk, chunks):
    count, depth = normed.shape
    half = count // 2
    width = w_gate.shape[1] // chunks
    block = block_of(width, 256)
    first = chunk * (width // block)

    def body(normed_ref, gate_ref, up_ref, tan_ref, keep_ref, send_ref):
        upper = lax.axis_index("mp") % 2 == 1
        for i, weight in enumerate((gate_ref, up_ref, tan_ref)):
            part = dot(normed_ref[...], weight[...], 1, 0)
            low, high = part[:half], part[half:]
            keep_ref[i] = jnp.where(upper, high, low)
            send_ref[i] = jnp.where(upper, low, high).astype(bf16)

    weight_spec = pl.BlockSpec((depth, block), lambda i: (0, first + i))
    part_spec = pl.BlockSpec((3, half, block), lambda i: (0, 0, i))
    return pl.pallas_call(
        body,
        grid=(width // block,),
        in_specs=[pl.BlockSpec((count, depth), lambda i: (0, 0)), weight_spec, weight_spec, weight_spec],
        out_specs=[part_spec, part_spec],
        out_shape=[
            jax.ShapeDtypeStruct((3, half, width), f32),
            jax.ShapeDtypeStruct((3, half, width), bf16),
        ],
        compiler_params=params(20),
        cost_estimate=cost(6 * count * depth * width, 6 * depth * width),
        name="gate_products",
    )(normed, *[kept_out(w) for w in (w_gate, w_up, v_gate)])


def hidden_call(chip_sum, arrived, after):
    shape = chip_sum.shape[1:]
    width = shape[1]
    block = block_of(width, 512)

    def body(sum_ref, arrived_ref, after_ref, mine_ref, factor_ref):
        for j in range(width // block):
            span = slice(j * block, (j + 1) * block)
            gate_pre, up_value, tangent = [
                sum_ref[i, :, span] + arrived_ref[i, :, span].astype(f32) for i in range(3)
            ]
            activation, slope_gate, curvature = silu_parts(gate_pre)
            mine_ref[0, :, span] = (activation * up_value).astype(bf16)
            mine_ref[1, :, span] = (slope_gate * up_value * tangent).astype(bf16)
            factor_ref[0, :, span] = up_value * slope_gate
            factor_ref[1, :, span] = up_value * curvature * tangent

    return pl.pallas_call(
        body,
        in_specs=[IN_VMEM, IN_VMEM, pl.BlockSpec(memory_space=pl.ANY)],
        out_specs=[IN_VMEM] * 2,
        out_shape=[
            jax.ShapeDtypeStruct((2,) + shape, bf16),
            jax.ShapeDtypeStruct((2,) + shape, f32),
        ],
        compiler_params=params(8),
        cost_estimate=cost(0, 30 * shape[0] * width),
        name="hidden_units",
    )(chip_sum, arrived, after)


def down_call(mine, other, w_down, v_down):
    half, rows = mine.shape[1:]
    count = 2 * half
    features = w_down.shape[1]
    block = block_of(features, 512)

    def body(mine_ref, other_ref, w_ref, v_ref, out_ref, left):
        for i in range(2):
            left[i * count : i * count + half] = mine_ref[i]
            left[i * count + half : (i + 1) * count] = other_ref[i]
        for j in range(features // block):
            span = slice(j * block, (j + 1) * block)
            both = dot(left[...], w_ref[:, span], 1, 0)
            out_ref[0, :, span] = both[:count].astype(bf16)
            out_ref[1, :, span] = (both[count:] + dot(left[:count], v_ref[:, span], 1, 0)).astype(bf16)

    return pl.pallas_call(
        body,
        in_specs=[IN_VMEM] * 4,
        out_specs=IN_VMEM,
        out_shape=jax.ShapeDtypeStruct((2, count, features), bf16),
        scratch_shapes=[pltpu.VMEM((2 * count, rows), bf16)],
        compiler_params=params(12),
        cost_estimate=cost(6 * count * rows * features, 4 * rows * features),
        name="down_products",
    )(mine, other, held(w_down), held(v_down))


def back_call(residuals, w_down, v_down):
    count, features = residuals.shape[1:]
    half = count // 2
    rows = w_down.shape[0]
    block = block_of(rows, 512)

    def body(res_ref, w_ref, v_ref, keep_ref, send_ref, right):
        right[...] = res_ref[...].reshape(2 * count, features).T
        for j in range(rows // block):
            span = slice(j * block, (j + 1) * block)
            both = dot(w_ref[span, :], right[...], 1, 0)
            tangent = both[:, count:] + dot(v_ref[span, :], right[:, :count], 1, 0)
            for i, part in enumerate((both[:, :count].T, tangent.T)):
                keep_ref[i, :, span] = part[:half]
                send_ref[i, :, span] = part[half:].astype(bf16)

    return pl.pallas_call(
        body,
        in_specs=[IN_VMEM] * 3,
        out_specs=[IN_VMEM] * 2,
        out_shape=[
            jax.ShapeDtypeStruct((2, half, rows), f32),
            jax.ShapeDtypeStruct((2, half, rows), bf16),
        ],
        scratch_shapes=[pltpu.VMEM((features, 2 * count), bf16)],
        compiler_params=params(12),
        cost_estimate=cost(6 * count * rows * features, 4 * rows * features),
        name="back_products",
    )(residuals, held(w_down), held(v_down))


def down_score_call(mine, other, residuals, v_down):
    half, rows = mine.shape[1:]
    count = 2 * half
    features = v_down.shape[1]
    block = block_of(rows, 512)
    steps = rows // block

    def body(mine_ref, other_ref, res_ref, v_ref, out_ref, buffer, sems):
        copies = []
        for j in range(steps):
            span = slice(j * block, (j + 1) * block)
            if j >= 2:
                copies[j - 2].wait()
            left = jnp.concatenate(
                [mine_ref[1, :, span], other_ref[1, :, span], mine_ref[0, :, span], other_ref[0, :, span]],
                axis=0,
            )
            hess = dot(left, res_ref[...].reshape(2 * count, features), 0, 0)
            buffer[j % 2] = (v_ref[span, :].astype(f32) * hess).astype(bf16)
            copies.append(
                pltpu.make_async_copy(
                    buffer.at[j % 2], out_ref.at[pl.ds(j * block, block)], sems.at[j % 2]
                )
            )
            copies[j].start()
        for copy in copies[-2:]:
            copy.wait()

    return pl.pallas_call(
        body,
        in_specs=[IN_VMEM] * 4,
        out_specs=IN_HBM,
        out_shape=jax.ShapeDtypeStruct((rows, features), bf16),
        scratch_shapes=[
            pltpu.VMEM((2, block, features), bf16),
            pltpu.SemaphoreType.DMA((2,)),
        ],
        compiler_params=params(16),
        cost_estimate=cost(4 * count * rows * features, 4 * rows * features),
        name="down_score",
    )(mine, other, residuals, held(v_down))


def combine_call(chip_sum, arrived, factors, after):
    half, width = chip_sum.shape[1:]
    block = block_of(width, 512)

    def body(sum_ref, arrived_ref, factor_ref, after_ref, out_ref):
        for j in range(width // block):
            span = slice(j * block, (j + 1) * block)
            back_grad, back_tangent = [
                sum_ref[i, :, span] + arrived_ref[i, :, span].astype(f32) for i in range(2)
            ]
            out_ref[:, span] = (
                back_tangent * factor_ref[0, :, span] + back_grad * factor_ref[1, :, span]
            ).astype(bf16)

    return pl.pallas_call(
        body,
        in_specs=[IN_VMEM] * 3 + [pl.BlockSpec(memory_space=pl.ANY)],
        out_specs=IN_VMEM,
        out_shape=jax.ShapeDtypeStruct((half, width), bf16),
        compiler_params=params(8),
        cost_estimate=cost(0, 22 * half * width),
        name="combined",
    )(chip_sum, arrived, factors, after)


def gate_score_call(normed, mine, other, v_gate):
    count, depth = normed.shape
    half = count // 2
    width = v_gate.shape[1]
    block = block_of(width, 512)
    steps = width // block

    def body(normed_ref, mine_ref, other_ref, v_ref, out_ref, buffer, sems):
        upper = lax.axis_index("mp") % 2 == 1
        copies = []
        for j in range(steps):
            span = slice(j * block, (j + 1) * block)
            if j >= 2:
                copies[j - 2].wait()
            low = jnp.where(upper, other_ref[:, span], mine_ref[:, span])
            high = jnp.where(upper, mine_ref[:, span], other_ref[:, span])
            hess = dot(normed_ref[...], jnp.concatenate([low, high], axis=0), 0, 0)
            buffer[j % 2] = (v_ref[:, span].astype(f32) * hess).astype(bf16)
            copies.append(
                pltpu.make_async_copy(
                    buffer.at[j % 2], out_ref.at[:, pl.ds(j * block, block)], sems.at[j % 2]
                )
            )
            copies[j].start()
        for copy in copies[-2:]:
            copy.wait()

    return pl.pallas_call(
        body,
        in_specs=[IN_VMEM] * 4,
        out_specs=IN_HBM,
        out_shape=jax.ShapeDtypeStruct((depth, width), bf16),
        scratch_shapes=[
            pltpu.VMEM((2, depth, block), bf16),
            pltpu.SemaphoreType.DMA((2,)),
        ],
        compiler_params=params(16),
        cost_estimate=cost(2 * count * depth * width, 4 * depth * width),
        name="gate_score",
    )(normed, mine, other, v_gate)


def bits():
    index = lax.axis_index("dp")
    return index % 2, (index // 2) % 2


def swap_dp(value, bit):
    return lax.ppermute(value, "dp", [(i, i ^ bit) for i in range(8)])


def piece_call(mine, other, w_down, v_down, away, dtype):
    half, rows = mine.shape[1:]
    count = 2 * half
    features = w_down.shape[1]
    piece = features // 8

    def body(mine_ref, other_ref, w_ref, v_ref, a_ref, b_ref, left):
        y, z = bits()
        for i in range(2):
            left[i * count : i * count + half] = mine_ref[i]
            left[i * count + half : (i + 1) * count] = other_ref[i]
        for out_ref, base, outer, inner in ((a_ref, 0, y, z), (b_ref, 4, z, y)):
            group = 1 - outer if away else outer
            for k, low in enumerate((1 - inner, inner)):
                first = pl.multiple_of((base + 2 * group + low) * piece, piece)
                both = dot(left[...], w_ref[:, pl.ds(first, piece)], 1, 0)
                tangent = both[count:] + dot(left[:count], v_ref[:, pl.ds(first, piece)], 1, 0)
                out_ref[k, 0] = both[:count].astype(dtype)
                out_ref[k, 1] = tangent.astype(dtype)

    shape = jax.ShapeDtypeStruct((2, 2, count, piece), dtype)
    return pl.pallas_call(
        body,
        in_specs=[IN_VMEM] * 4,
        out_specs=[IN_VMEM] * 2,
        out_shape=[shape, shape],
        scratch_shapes=[pltpu.VMEM((2 * count, rows), bf16)],
        compiler_params=params(8),
        cost_estimate=cost(3 * count * rows * features, 2 * rows * features),
        name="pieces_away" if away else "pieces_home",
    )(mine, other, held(w_down), held(v_down))


def residual_call(sums, arrived, target):
    count, features = target.shape
    half = count // 2
    piece = features // 8

    def body(sums_ref, arrived_ref, target_ref, a_ref, b_ref):
        y, z = bits()
        upper = lax.axis_index("mp") % 2 == 1
        for i, (out_ref, outer, inner) in enumerate(((a_ref, y, z), (b_ref, z, y))):
            first = pl.multiple_of((4 * i + 2 * outer + inner) * piece, piece)
            wanted = target_ref[:, pl.ds(first, piece)].astype(f32)
            low, high = wanted[:half], wanted[half:]
            wanted = jnp.concatenate(
                [jnp.where(upper, high, low), jnp.where(upper, low, high)], axis=0
            )
            out_ref[0] = ((sums_ref[i, 0] + arrived_ref[i, 0].astype(f32) - wanted) / count).astype(bf16)
            out_ref[1] = ((sums_ref[i, 1] + arrived_ref[i, 1].astype(f32)) / count).astype(bf16)

    shape = jax.ShapeDtypeStruct((2, count, piece), bf16)
    return pl.pallas_call(
        body,
        in_specs=[IN_VMEM] * 3,
        out_specs=[IN_VMEM] * 2,
        out_shape=[shape, shape],
        compiler_params=params(4),
        cost_estimate=cost(0, 8 * 2 * count * piece),
        name="residuals",
    )(sums, arrived, target)


def back_first_call(a_pieces, b_pieces, w_down, v_down):
    count, piece = a_pieces.shape[2:]
    rows = w_down.shape[0]
    block = block_of(rows, 512)

    def body(a_ref, b_ref, w_ref, v_ref, out_ref, right):
        y, z = bits()
        for i, (ref, inner) in enumerate(((a_ref, z), (b_ref, y))):
            for k, low in enumerate((inner, 1 - inner)):
                first = pl.multiple_of((2 * i + low) * piece, piece)
                right[pl.ds(first, piece), :] = ref[k].reshape(2 * count, piece).T
        starts = [
            pl.multiple_of(2 * piece * y, 2 * piece),
            pl.multiple_of(2 * piece * (2 + z), 2 * piece),
        ]
        for j in range(rows // block):
            span = slice(j * block, (j + 1) * block)
            total = jnp.zeros((block, 2 * count), f32)
            tangent = jnp.zeros((block, count), f32)
            for i, first in enumerate(starts):
                part = right[2 * i * piece : 2 * (i + 1) * piece]
                total += dot(w_ref[span, pl.ds(first, 2 * piece)], part, 1, 0)
                tangent += dot(v_ref[span, pl.ds(first, 2 * piece)], part[:, :count], 1, 0)
            out_ref[span] = jnp.concatenate([total[:, :count], total[:, count:] + tangent], axis=1)

    return pl.pallas_call(
        body,
        in_specs=[IN_VMEM] * 4,
        out_specs=IN_VMEM,
        out_shape=jax.ShapeDtypeStruct((rows, 2 * count), f32),
        scratch_shapes=[pltpu.VMEM((4 * piece, 2 * count), bf16)],
        compiler_params=params(8),
        cost_estimate=cost(12 * count * rows * piece, 8 * rows * piece),
        name="back_first",
    )(a_pieces, b_pieces, held(w_down), held(v_down))


def back_second_call(a_pieces, b_pieces, a_far, b_far, first_part, w_down, v_down):
    count, piece = a_pieces.shape[2:]
    half = count // 2
    rows, features = w_down.shape
    block = block_of(rows, 512)

    def body(a_ref, b_ref, a_far_ref, b_far_ref, part_ref, w_ref, v_ref, keep_ref, send_ref, res_ref, right):
        y, z = bits()
        for i, (ref, far_ref, outer, inner) in enumerate(((a_ref, a_far_ref, y, z), (b_ref, b_far_ref, z, y))):
            for k, low in enumerate((inner, 1 - inner)):
                first = pl.multiple_of((2 * i + low) * piece, piece)
                right[pl.ds(first, piece), :] = far_ref[k].reshape(2 * count, piece).T
                near = pl.multiple_of((4 * i + 2 * outer + low) * piece, piece)
                far = pl.multiple_of((4 * i + 2 * (1 - outer) + low) * piece, piece)
                for t in range(2):
                    res_ref[t, :, pl.ds(near, piece)] = ref[k, t]
                    res_ref[t, :, pl.ds(far, piece)] = far_ref[k, t]
        starts = [
            pl.multiple_of(2 * piece * (1 - y), 2 * piece),
            pl.multiple_of(2 * piece * (3 - z), 2 * piece),
        ]
        for j in range(rows // block):
            span = slice(j * block, (j + 1) * block)
            total = part_ref[span]
            tangent = jnp.zeros((block, count), f32)
            for i, first in enumerate(starts):
                part = right[2 * i * piece : 2 * (i + 1) * piece]
                total += dot(w_ref[span, pl.ds(first, 2 * piece)], part, 1, 0)
                tangent += dot(v_ref[span, pl.ds(first, 2 * piece)], part[:, :count], 1, 0)
            for i, value in enumerate((total[:, :count].T, (total[:, count:] + tangent).T)):
                keep_ref[i, :, span] = value[:half]
                send_ref[i, :, span] = value[half:].astype(bf16)

    return pl.pallas_call(
        body,
        in_specs=[IN_VMEM] * 7,
        out_specs=[IN_VMEM] * 3,
        out_shape=[
            jax.ShapeDtypeStruct((2, half, rows), f32),
            jax.ShapeDtypeStruct((2, half, rows), bf16),
            jax.ShapeDtypeStruct((2, count, features), bf16),
        ],
        scratch_shapes=[pltpu.VMEM((4 * piece, 2 * count), bf16)],
        compiler_params=params(8),
        cost_estimate=cost(12 * count * rows * piece, 8 * rows * piece),
        name="back_second",
    )(a_pieces, b_pieces, a_far, b_far, first_part, held(w_down), held(v_down))


def middle_tree(mine, other, target, w_down, v_down):
    a_send, b_send = piece_call(mine, other, w_down, v_down, True, bf16)
    a_recv, b_recv = swap_dp(a_send, 1), swap_dp(b_send, 2)
    a_home, b_home = piece_call(mine, other, w_down, v_down, False, f32)
    a_sum = a_home + a_recv.astype(f32)
    b_sum = b_home + b_recv.astype(f32)
    a_recv, b_recv = swap_dp(a_sum[0].astype(bf16), 2), swap_dp(b_sum[0].astype(bf16), 1)
    sums = jnp.stack([a_sum[1] + a_recv.astype(f32), b_sum[1] + b_recv.astype(f32)])
    arrived = swap_dp(sums.astype(bf16), 4)
    a_res, b_res = residual_call(sums, arrived, target)
    a_pieces = jnp.stack([a_res, swap_dp(a_res, 2)])
    b_pieces = jnp.stack([b_res, swap_dp(b_res, 1)])
    a_far, b_far = swap_dp(a_pieces, 1), swap_dp(b_pieces, 2)
    first_part = back_first_call(a_pieces, b_pieces, w_down, v_down)
    return back_second_call(a_pieces, b_pieces, a_far, b_far, first_part, w_down, v_down)


def middle_direct(dp, mine, other, target, w_down, v_down):
    half = mine.shape[1]
    count = 2 * half
    own = count // dp
    features = w_down.shape[1]
    out_parts = down_call(mine, other, w_down, v_down)
    pieces = out_parts.reshape(2, dp, own, features).swapaxes(0, 1)
    arrived = lax.all_to_all(pieces, "dp", 0, 0, tiled=True).astype(f32)
    totals = jnp.sum(arrived, axis=0)
    core = lax.axis_index("mp") % 2
    first_row = (lax.axis_index("dp") * own + core * half) % count
    target_rows = lax.dynamic_slice_in_dim(target, first_row, own, 0)
    residual_rows = ((totals[0] - target_rows.astype(f32)) / count).astype(bf16)
    residual_tan_rows = (totals[1] / count).astype(bf16)
    rows = jnp.stack([residual_rows, residual_tan_rows])
    spread = lax.all_to_all(
        jnp.broadcast_to(rows[None], (dp,) + rows.shape), "dp", 0, 0, tiled=True
    )
    residuals = spread.swapaxes(0, 1).reshape(2, count, features)
    keep, send = back_call(residuals, w_down, v_down)
    return keep, send, residuals


def per_device(dp, tokens, norm_gain, target, w_gate, w_up, v_gate, w_down, v_down):
    own = tokens.shape[0]
    count = own * dp
    col_width = w_gate.shape[0]
    copies = norm_call(tokens, norm_gain, dp, col_width)
    normed = lax.all_to_all(copies, "dp", 0, 0, tiled=True).reshape(count, col_width)
    keep, send = gate_call(normed, w_gate, w_up, v_gate, 0, 1)
    chip_sum = keep + swap_core(send).astype(f32)
    chip_send = chip_sum.astype(bf16)
    w_down, v_down = load_call([w_down, v_down], chip_send, "load_down")
    mine, factors = hidden_call(chip_sum, swap_chip(chip_send), held(v_down))
    other = swap_core(mine)
    if dp == 8:
        keep, send, residuals = middle_tree(mine, other, target, w_down, v_down)
    else:
        keep, send, residuals = middle_direct(dp, mine, other, target, w_down, v_down)
    chip_sum = keep + swap_core(send).astype(f32)
    arrived = swap_chip(chip_sum.astype(bf16))
    down_score = down_score_call(mine, other, residuals, v_down)
    combined = combine_call(chip_sum, arrived, factors, down_score)
    gate_score = gate_score_call(normed, combined, swap_core(combined), v_gate)
    return (gate_score, down_score)


def solution(mesh):
    in_specs = (
        P("dp", None),
        P(),
        P(None, "mp"),
        P("mp", "dp"),
        P("mp", "dp"),
        P("mp", "dp"),
        P("dp", "mp"),
        P("dp", "mp"),
    )
    out_specs = (P("mp", "dp"), P("dp", "mp"))
    return jax.shard_map(
        functools.partial(per_device, mesh.shape["dp"]),
        mesh=mesh,
        in_specs=in_specs,
        out_specs=out_specs,
        check_vma=False,
    )
```

time: 307 us -> 118 us (0.38)
  waiting for transfers between devices: 159 us -> 31.1 us
  matrix products: 94.4 us -> 0 us
  Pallas kernels: 0 us -> 52.5 us
  blocking collectives: 32.6 us -> 16 us
  between operations: 13.9 us -> 1.01 us
  starting transfers between devices: 0.3 us -> 9.89 us
  local copies, waits for them, and re-layouts: 0.93 us -> 6.83 us
  other arithmetic: 5.18 us -> 0.4 us
    psum x3 -> x0, waiting for transfers between devices: 159 us -> none  [the longest x1 78.4 us: per_device(): output, output_tan = lax.psum((out_part, out_tan_part), 'dp')]
    dot_general x12 -> x0, matrix products: 94.4 us -> none  [the longest x3 39.3 us: contract_rows(): lax.dot_general(left_op, right_op, (((0,), (0,)), ((), ())), preferred_el...]
    pallas_call x0 -> x12, Pallas kernels: none -> 52.5 us  [the longest x1 17.5 us: gate_call(): pl.pallas_call(body, grid=(width // block,), in_specs=[pl.BlockSpec((coun...]
    all_gather x1 -> x0, blocking collectives: 32.6 us -> none  [per_device(): normed = lax.all_gather(local_cols, 'dp', axis=0, tiled=True)]
    ppermute x0 -> x15, waiting for transfers between devices: none -> 31.1 us  [the longest x9 16.2 us: swap_dp(): return lax.ppermute(value, 'dp', [(i, i ^ bit) for i in range(8)])]
    all_to_all x0 -> x1, blocking collectives: none -> 16 us  [per_device(): lax.all_to_all(copies, 'dp', 0, 0, tiled=True).reshape(count, col_width)]
    ppermute x0 -> x15, starting transfers between devices: none -> 9.89 us  [the longest x9 6.53 us: swap_dp(): return lax.ppermute(value, 'dp', [(i, i ^ bit) for i in range(8)])]
    unnamed x30 -> x14, local copies, waits for them, and re-layouts: 0.08 us -> 6.81 us
  transfers between devices with their start and end apart: 3 -> 15, of which waited for: 3 -> 12; matrix products, arithmetic and copies ran while one was open for 6% -> 0% of each run, Pallas kernels for 0% -> 18%
where the time goes in v2:
time: 118 us
  Pallas kernels  52.5 us (44%)
  waiting for transfers between devices  31.1 us (26%)
  blocking collectives  16 us (14%)
  starting transfers between devices  9.89 us (8%)
  local copies, waits for them, and re-layouts  6.83 us (6%)
    pallas_call x1, Pallas kernels, gate_call(): pl.pallas_call(body, grid=(width // block,), in_specs=[pl.BlockSpec((coun...  17.5 us
    ppermute x9, waiting for transfers between devices, swap_dp(): return lax.ppermute(value, 'dp', [(i, i ^ bit) for i in range(8)])  16.2 us
    all_to_all x1, blocking collectives, per_device(): lax.all_to_all(copies, 'dp', 0, 0, tiled=True).reshape(count, col_width)  16 us
    pallas_call x1, Pallas kernels, load_call(): pl.pallas_call(body, in_specs=[IN_HBM] * n + [pl.BlockSpec(memory_space=p...  8.3 us
    ppermute x2, waiting for transfers between devices, swap_chip(): return lax.ppermute(value, 'mp', [(i, i ^ 2) for i in range(4)])  8.07 us
    pallas_call x1, Pallas kernels, down_score_call(): pl.pallas_call(body, in_specs=[IN_VMEM] * 4, out_specs=IN_HBM, out_shape=...  7.18 us
    pallas_call x1, Pallas kernels, gate_score_call(): pl.pallas_call(body, in_specs=[IN_VMEM] * 4, out_specs=IN_HBM, out_shape=...  6.93 us
    ppermute x4, waiting for transfers between devices, swap_core(): return lax.ppermute(value, 'mp', [(i, i ^ 1) for i in range(4)])  6.84 us
  transfers between devices with their start and end apart: 15, of which 12 were waited for; matrix products, arithmetic and copies ran while one was open for 0% of the time, Pallas kernels for 18%

profile of v2, /device:TPU:0, one launch (start us, length us, event | category | flops | bytes accessed | tf_op | source)
XLA Modules:
  0.0 117.8 jit_solution(707911487290486091)
XLA Ops:
  0.6 0.0 copy-start.2
  0.6 0.9 copy-done.2
  1.5 0.0 copy-start.3
  1.5 0.8 copy-done.3
  2.3 0.2 norm_rows.1
  2.5 16.0 %all_to_all.5 = bf16[8,8,2048]{2,1,0:T(8,128)(2,1)S(1)} all-to-all(bf16[8,8,2048]{2,1,0:T(8,128)(2,1)S(1)} %norm_rows.1), channel_id=1, replica_groups=mesh['dp'=8,'mp'=4] {'dp'}, dimensions={0} | all-to-all | bytes 524288 | tf_op jit(solution)/shard_map/all_to_all | solution.py:552
  18.5 17.5 %gate_products.1 = (f32[3,32,3072]{2,1,0:T(8,128)S(1)}, bf16[3,32,3072]{2,1,0:T(8,128)(2,1)S(1)}) custom-call(bf16[64,2048]{1,0:T(8,128)(2,1)S(1)} %bitcast.28, bf16[2048,3072]{1,0:T(8,128)(2,1)} %gate_ref.1, bf16[2048,3072]{1,0:T(8,128)(2,1)} %up_ref.1, bf16[2048,3072]{1,0:T(8,128)(2,1)} %v_ref.1), custom_call_target="tpu_custom_call" | custom-call | flops 2415919104 | bytes 37748736 | tf_op jit(solution)/shard_map/gate_products/pallas_call | solution.py:134
  36.1 0.1 collective-permute-start
  36.1 2.0 %collective-permute-done = bf16[3,32,3072]{2,1,0:T(8,128)(2,1)S(1)} collective-permute-done((bf16[3,32,3072]{2,1,0:T(8,128)(2,1)S(1)}, bf16[3,32,3072]{2,1,0:T(8,128)(2,1)S(1)}, u32[]{:S(2)}, u32[]{:S(2)}) %collective-permute-start) | collective-permute-done | bytes 589856 | tf_op jit(solution)/shard_map/ppermute | solution.py:55
  38.1 0.2 fusion.8
  38.3 1.6 %collective-permute-start.1 = (bf16[3,32,3072]{2,1,0:T(8,128)(2,1)S(1)}, bf16[3,32,3072]{2,1,0:T(8,128)(2,1)S(1)}, u32[]{:S(2)}, u32[]{:S(2)}) collective-permute-start(bf16[3,32,3072]{2,1,0:T(8,128)(2,1)S(1)} %get-tuple-element.34.refs_2_), channel_id=1, source_target_pairs={{0,2},{1,3},{2,0},{3,1},{4,6},{5,7},{6,4},{7,5},{8,10},{9,11},{10,... | collective-permute-start | bytes 1769480 | tf_op jit(solution)/shard_map/ppermute | solution.py:59
  39.9 8.3 %load_down.1 = (bf16[3072,2048]{1,0:T(8,128)(2,1)S(1)}, bf16[3072,2048]{1,0:T(8,128)(2,1)S(1)}) custom-call(bf16[3072,2048]{1,0:T(8,128)(2,1)} %refs_0_.1, bf16[3072,2048]{1,0:T(8,128)(2,1)} %refs_1_.1, bf16[3,32,3072]{2,1,0:T(8,128)(2,1)S(1)} %get-tuple-element.34.refs_2_), custom_call_target="tpu_custom_call" | custom-call | bytes 50331648 | tf_op jit(solution)/shard_map/load_down/pallas_call | solution.py:84
  48.2 5.6 %collective-permute-done.1.arrived_ref = bf16[3,32,3072]{2,1,0:T(8,128)(2,1)S(1)} collective-permute-done((bf16[3,32,3072]{2,1,0:T(8,128)(2,1)S(1)}, bf16[3,32,3072]{2,1,0:T(8,128)(2,1)S(1)}, u32[]{:S(2)}, u32[]{:S(2)}) %collective-permute-start.1) | collective-permute-done | bytes 589856 | tf_op jit(solution)/shard_map/ppermute | solution.py:59
  53.7 0.4 hidden_units.1
  54.1 0.1 collective-permute-start.2
  54.2 1.7 %collective-permute-done.2.other_ref = bf16[2,32,3072]{2,1,0:T(8,128)(2,1)S(1)} collective-permute-done((bf16[2,32,3072]{2,1,0:T(8,128)(2,1)S(1)}, bf16[2,32,3072]{2,1,0:T(8,128)(2,1)S(1)}, u32[]{:S(2)}, u32[]{:S(2)}) %collective-permute-start.2) | collective-permute-done | bytes 393248 | tf_op jit(solution)/shard_map/ppermute | solution.py:55
  55.9 2.1 %pieces_away.1 = (bf16[2,2,64,256]{3,2,1,0:T(8,128)(2,1)S(1)}, bf16[2,2,64,256]{3,2,1,0:T(8,128)(2,1)S(1)}) custom-call(bf16[2,32,3072]{2,1,0:T(8,128)(2,1)S(1)} %get-tuple-element.20.mine_ref, bf16[2,32,3072]{2,1,0:T(8,128)(2,1)S(1)} %collective-permute-done.2.other_ref, bf16[3072,2048]{1,0:T(8,128)(2,1)S(1)} %get-tuple-element.21.w_ref, ...), custom_call_target="tpu_custom_call" | custom-call | flops 1207959552 | bytes 12582912 | tf_op jit(solution)/shard_map/pieces_away/pallas_call | solution.py:379
  58.0 1.5 %collective-permute-start.3 = (bf16[2,2,64,256]{3,2,1,0:T(8,128)(2,1)S(1)}, bf16[2,2,64,256]{3,2,1,0:T(8,128)(2,1)S(1)}, u32[]{:S(2)}, u32[]{:S(2)}) collective-permute-start(bf16[2,2,64,256]{3,2,1,0:T(8,128)(2,1)S(1)} %get-tuple-element.23), channel_id=1, source_target_pairs={{0,4},{4,0},{8,12},{12,8},{16,20},{20,16},{24,28},{28,24},{1,5},{5... | collective-permute-start | bytes 393224 | tf_op jit(solution)/shard_map/ppermute | solution.py:355
  59.5 0.0 copy-start.1
  59.5 0.1 collective-permute-start.5
  59.6 2.1 %pieces_home.1 = (f32[2,2,64,256]{3,2,1,0:T(8,128)S(1)}, f32[2,2,64,256]{3,2,1,0:T(8,128)S(1)}) custom-call(bf16[2,32,3072]{2,1,0:T(8,128)(2,1)S(1)} %get-tuple-element.20.mine_ref, bf16[2,32,3072]{2,1,0:T(8,128)(2,1)S(1)} %collective-permute-done.2.other_ref, bf16[3072,2048]{1,0:T(8,128)(2,1)S(1)} %get-tuple-element.21.w_ref, ...), custom_call_target="tpu_custom_call" | custom-call | flops 1207959552 | bytes 12582912 | tf_op jit(solution)/shard_map/pieces_home/pallas_call | solution.py:379
  61.7 1.9 %collective-permute-done.3 = bf16[2,2,64,256]{3,2,1,0:T(8,128)(2,1)S(1)} collective-permute-done((bf16[2,2,64,256]{3,2,1,0:T(8,128)(2,1)S(1)}, bf16[2,2,64,256]{3,2,1,0:T(8,128)(2,1)S(1)}, u32[]{:S(2)}, u32[]{:S(2)}) %collective-permute-start.3) | collective-permute-done | bytes 131104 | tf_op jit(solution)/shard_map/ppermute | solution.py:355
  63.7 1.1 collective-permute-start.4
  64.8 0.0 collective-permute-done.5
  64.9 0.6 collective-permute-start.6
  65.5 2.5 %collective-permute-done.4 = bf16[2,64,256]{2,1,0:T(8,128)(2,1)S(1)} collective-permute-done((bf16[2,64,256]{2,1,0:T(8,128)(2,1)S(1)}, bf16[2,64,256]{2,1,0:T(8,128)(2,1)S(1)}, u32[]{:S(2)}, u32[]{:S(2)}) %collective-permute-start.4) | collective-permute-done | bytes 65568 | tf_op jit(solution)/shard_map/ppermute | solution.py:355
  68.0 1.2 %collective-permute-done.6 = bf16[2,64,256]{2,1,0:T(8,128)(2,1)S(1)} collective-permute-done((bf16[2,64,256]{2,1,0:T(8,128)(2,1)S(1)}, bf16[2,64,256]{2,1,0:T(8,128)(2,1)S(1)}, u32[]{:S(2)}, u32[]{:S(2)}) %collective-permute-start.6) | collective-permute-done | bytes 65568 | tf_op jit(solution)/shard_map/ppermute | solution.py:355
  69.3 0.7 collective-permute-start.7
  70.0 6.7 %collective-permute-done.7.arrived_ref = bf16[2,2,64,256]{3,2,1,0:T(8,128)(2,1)S(1)} collective-permute-done((bf16[2,2,64,256]{3,2,1,0:T(8,128)(2,1)S(1)}, bf16[2,2,64,256]{3,2,1,0:T(8,128)(2,1)S(1)}, u32[]{:S(2)}, u32[]{:S(2)}) %collective-permute-start.7) | collective-permute-done | bytes 131104 | tf_op jit(solution)/shard_map/ppermute | solution.py:355
  76.6 0.0 copy-done.1
  76.7 0.6 collective-permute-start.9
  77.3 0.5 collective-permute-start.8
  77.8 3.9 %collective-permute-done.9 = bf16[2,64,256]{2,1,0:T(8,128)(2,1)S(1)} collective-permute-done((bf16[2,64,256]{2,1,0:T(8,128)(2,1)S(1)}, bf16[2,64,256]{2,1,0:T(8,128)(2,1)S(1)}, u32[]{:S(2)}, u32[]{:S(2)}) %collective-permute-start.9) | collective-permute-done | bytes 65568 | tf_op jit(solution)/shard_map/ppermute | solution.py:355
  81.7 0.1 collective-permute-start.11
  81.8 0.0 collective-permute-done.8
  81.8 1.3 %collective-permute-start.10 = (bf16[2,2,64,256]{3,2,1,0:T(8,128)(2,1)S(1)}, bf16[2,2,64,256]{3,2,1,0:T(8,128)(2,1)S(1)}, u32[]{:S(2)}, u32[]{:S(2)}) collective-permute-start(bf16[2,2,64,256]{3,2,1,0:T(8,128)(2,1)S(1)} %pad_maximum_fusion.1.a_ref), channel_id=1, source_target_pairs={{0,4},{4,0},{8,12},{12,8},{16,20},{20,16},{24,28},{28,24},{1,5},{5... | collective-permute-start | bytes 393224 | tf_op jit(solution)/shard_map/ppermute | solution.py:355
  83.1 3.6 %back_first.1.part_ref = f32[3072,128]{1,0:T(8,128)S(1)} custom-call(bf16[2,2,64,256]{3,2,1,0:T(8,128)(2,1)S(1)} %pad_maximum_fusion.1.a_ref, bf16[2,2,64,256]{3,2,1,0:T(8,128)(2,1)S(1)} %pad_maximum_fusion.2.b_ref, bf16[3072,2048]{1,0:T(8,128)(2,1)S(1)} %get-tuple-element.21.w_ref, bf16[3072,2048]{1,0:T(8,128)(2,1)S(1)} %get-tuple-element.19.after_ref.v_ref), custom_call_target="tpu_custom_call" | custom-call | flops 603979776 | bytes 6291456 | tf_op jit(solution)/shard_map/back_first/pallas_call | solution.py:446
  86.7 0.0 collective-permute-done.11.b_far_ref
  86.8 0.1 collective-permute-done.10.a_far_ref
  86.8 4.0 %back_second.1 = (f32[2,32,3072]{2,1,0:T(8,128)S(1)}, bf16[2,32,3072]{2,1,0:T(8,128)(2,1)S(1)}, bf16[2,64,2048]{2,1,0:T(8,128)(2,1)S(1)}) custom-call(bf16[2,2,64,256]{3,2,1,0:T(8,128)(2,1)S(1)} %pad_maximum_fusion.1.a_ref, bf16[2,2,64,256]{3,2,1,0:T(8,128)(2,1)S(1)} %pad_maximum_fusion.2.b_ref, ...), custom_call_target="tpu_custom_call" | custom-call | flops 603979776 | bytes 6291456 | tf_op jit(solution)/shard_map/back_second/pallas_call | solution.py:491
  90.8 0.1 collective-permute-start.12
  90.9 1.7 %collective-permute-done.12 = bf16[2,32,3072]{2,1,0:T(8,128)(2,1)S(1)} collective-permute-done((bf16[2,32,3072]{2,1,0:T(8,128)(2,1)S(1)}, bf16[2,32,3072]{2,1,0:T(8,128)(2,1)S(1)}, u32[]{:S(2)}, u32[]{:S(2)}) %collective-permute-start.12) | collective-permute-done | bytes 393248 | tf_op jit(solution)/shard_map/ppermute | solution.py:55
  92.6 0.1 fusion.7
  92.7 1.5 %collective-permute-start.13 = (bf16[2,32,3072]{2,1,0:T(8,128)(2,1)S(1)}, bf16[2,32,3072]{2,1,0:T(8,128)(2,1)S(1)}, u32[]{:S(2)}, u32[]{:S(2)}) collective-permute-start(bf16[2,32,3072]{2,1,0:T(8,128)(2,1)S(1)} %get-tuple-element.32), channel_id=1, source_target_pairs={{0,2},{1,3},{2,0},{3,1},{4,6},{5,7},{6,4},{7,5},{8,10},{9,11},{10,... | collective-permute-start | bytes 1179656 | tf_op jit(solution)/shard_map/ppermute | solution.py:59
  94.2 0.0 slice-start
  94.2 0.0 slice-start.1
  94.2 7.2 %down_score.1.after_ref = bf16[3072,2048]{1,0:T(8,128)(2,1)} custom-call(bf16[2,32,3072]{2,1,0:T(8,128)(2,1)S(1)} %get-tuple-element.20.mine_ref, bf16[2,32,3072]{2,1,0:T(8,128)(2,1)S(1)} %collective-permute-done.2.other_ref, bf16[2,64,2048]{2,1,0:T(8,128)(2,1)S(1)} %get-tuple-element.31.res_ref, bf16[3072,2048]{1,0:T(8,128)(2,1)S(1)} %get-tuple-element.19.after_ref.v_ref), custom_call_target="tpu_custom_call" | custom-call | flops 1610612736 | bytes 25165824 | tf_op jit(solution)/shard_map/down_score/pallas_call | solution.py:267
  101.4 2.5 %collective-permute-done.13.arrived_ref = bf16[2,32,3072]{2,1,0:T(8,128)(2,1)S(1)} collective-permute-done((bf16[2,32,3072]{2,1,0:T(8,128)(2,1)S(1)}, bf16[2,32,3072]{2,1,0:T(8,128)(2,1)S(1)}, u32[]{:S(2)}, u32[]{:S(2)}) %collective-permute-start.13) | collective-permute-done | bytes 393248 | tf_op jit(solution)/shard_map/ppermute | solution.py:59
  103.9 0.0 copy-start
  103.9 4.6 %copy-done = bf16[3072,2048]{1,0:T(8,128)(2,1)S(1)} copy-done((bf16[3072,2048]{1,0:T(8,128)(2,1)S(1)}, bf16[3072,2048]{1,0:T(8,128)(2,1)}, u32[]{:S(2)}) %copy-start) | copy-done | bytes 12582936
  108.5 0.0 slice-start.2
  108.5 0.1 combined.1.mine_ref
  108.6 0.1 collective-permute-start.14
  108.7 1.4 %collective-permute-done.14.other_ref = bf16[32,3072]{1,0:T(8,128)(2,1)S(1)} collective-permute-done((bf16[32,3072]{1,0:T(8,128)(2,1)S(1)}, bf16[32,3072]{1,0:T(8,128)(2,1)S(1)}, u32[]{:S(2)}, u32[]{:S(2)}) %collective-permute-start.14) | collective-permute-done | bytes 196640 | tf_op jit(solution)/shard_map/ppermute | solution.py:55
  110.1 0.0 slice-done
  110.1 0.0 slice-done.1
  110.1 0.6 slice-done.2
  110.7 6.9 %gate_score.1 = bf16[2048,3072]{1,0:T(8,128)(2,1)} custom-call(bf16[64,2048]{1,0:T(8,128)(2,1)S(1)} %bitcast.29, bf16[32,3072]{1,0:T(8,128)(2,1)S(1)} %combined.1.mine_ref, bf16[32,3072]{1,0:T(8,128)(2,1)S(1)} %collective-permute-done.14.other_ref, bf16[2048,3072]{1,0:T(8,128)(2,1)S(1)} %bitcast.27), custom_call_target="tpu_custom_call" | custom-call | flops 805306368 | bytes 25165824 | tf_op jit(solution)/shard_map/gate_score/pallas_call | solution.py:334
  (12 shorter events, 0.2 us)
Async XLA Ops:
  0.6 0.9 copy-start.2
  1.5 0.8 copy-start.3
  36.1 2.1 %collective-permute-start = (bf16[3,32,3072]{2,1,0:T(8,128)(2,1)S(1)}, bf16[3,32,3072]{2,1,0:T(8,128)(2,1)S(1)}, u32[]{:S(2)}, u32[]{:S(2)}) collective-permute-start(bf16[3,32,3072]{2,1,0:T(8,128)(2,1)S(1)} %get-tuple-element.18), channel_id=1, source_target_pairs={{0,1},{1,0},{2,3},{3,2},{4,5},{5,4},{6,7},{7,6},{8,9},{9,8},{10,11... | collective-permute-start | bytes 1769480 | tf_op jit(solution)/shard_map/ppermute | solution.py:55
  38.3 15.4 %collective-permute-start.1 = (bf16[3,32,3072]{2,1,0:T(8,128)(2,1)S(1)}, bf16[3,32,3072]{2,1,0:T(8,128)(2,1)S(1)}, u32[]{:S(2)}, u32[]{:S(2)}) collective-permute-start(bf16[3,32,3072]{2,1,0:T(8,128)(2,1)S(1)} %get-tuple-element.34.refs_2_), channel_id=1, source_target_pairs={{0,2},{1,3},{2,0},{3,1},{4,6},{5,7},{6,4},{7,5},{8,10},{9,11},{10,... | collective-permute-start | bytes 1769480 | tf_op jit(solution)/shard_map/ppermute | solution.py:59
  54.1 1.8 %collective-permute-start.2 = (bf16[2,32,3072]{2,1,0:T(8,128)(2,1)S(1)}, bf16[2,32,3072]{2,1,0:T(8,128)(2,1)S(1)}, u32[]{:S(2)}, u32[]{:S(2)}) collective-permute-start(bf16[2,32,3072]{2,1,0:T(8,128)(2,1)S(1)} %get-tuple-element.20.mine_ref), channel_id=1, source_target_pairs={{0,1},{1,0},{2,3},{3,2},{4,5},{5,4},{6,7},{7,6},{8,9},{9,8},{10,11... | collective-permute-start | bytes 1179656 | tf_op jit(solution)/shard_map/ppermute | solution.py:55
  58.0 5.6 %collective-permute-start.3 = (bf16[2,2,64,256]{3,2,1,0:T(8,128)(2,1)S(1)}, bf16[2,2,64,256]{3,2,1,0:T(8,128)(2,1)S(1)}, u32[]{:S(2)}, u32[]{:S(2)}) collective-permute-start(bf16[2,2,64,256]{3,2,1,0:T(8,128)(2,1)S(1)} %get-tuple-element.23), channel_id=1, source_target_pairs={{0,4},{4,0},{8,12},{12,8},{16,20},{20,16},{24,28},{28,24},{1,5},{5... | collective-permute-start | bytes 393224 | tf_op jit(solution)/shard_map/ppermute | solution.py:355
  59.5 17.1 %copy-start.1 = (bf16[64,2048]{1,0:T(8,128)(2,1)S(1)}, bf16[64,2048]{1,0:T(8,128)(2,1)}, u32[]{:S(2)}) copy-start(bf16[64,2048]{1,0:T(8,128)(2,1)} %target_ref.1) | copy-start | bytes 786436
  59.5 5.3 %collective-permute-start.5 = (bf16[2,2,64,256]{3,2,1,0:T(8,128)(2,1)S(1)}, bf16[2,2,64,256]{3,2,1,0:T(8,128)(2,1)S(1)}, u32[]{:S(2)}, u32[]{:S(2)}) collective-permute-start(bf16[2,2,64,256]{3,2,1,0:T(8,128)(2,1)S(1)} %get-tuple-element.25), channel_id=1, source_target_pairs={{0,8},{4,12},{8,0},{12,4},{16,24},{20,28},{24,16},{28,20},{1,9},{5... | collective-permute-start | bytes 393224 | tf_op jit(solution)/shard_map/ppermute | solution.py:355
  63.7 4.3 %collective-permute-start.4 = (bf16[2,64,256]{2,1,0:T(8,128)(2,1)S(1)}, bf16[2,64,256]{2,1,0:T(8,128)(2,1)S(1)}, u32[]{:S(2)}, u32[]{:S(2)}) collective-permute-start(bf16[2,64,256]{2,1,0:T(8,128)(2,1)S(1)} %fusion.4), channel_id=1, source_target_pairs={{0,8},{4,12},{8,0},{12,4},{16,24},{20,28},{24,16},{28,20},{1,9},{5... | collective-permute-start | bytes 196616 | tf_op jit(solution)/shard_map/ppermute | solution.py:355
  64.9 4.3 %collective-permute-start.6 = (bf16[2,64,256]{2,1,0:T(8,128)(2,1)S(1)}, bf16[2,64,256]{2,1,0:T(8,128)(2,1)S(1)}, u32[]{:S(2)}, u32[]{:S(2)}) collective-permute-start(bf16[2,64,256]{2,1,0:T(8,128)(2,1)S(1)} %fusion.5), channel_id=1, source_target_pairs={{0,4},{4,0},{8,12},{12,8},{16,20},{20,16},{24,28},{28,24},{1,5},{5... | collective-permute-start | bytes 196616 | tf_op jit(solution)/shard_map/ppermute | solution.py:355
  69.3 7.4 %collective-permute-start.7 = (bf16[2,2,64,256]{3,2,1,0:T(8,128)(2,1)S(1)}, bf16[2,2,64,256]{3,2,1,0:T(8,128)(2,1)S(1)}, u32[]{:S(2)}, u32[]{:S(2)}) collective-permute-start(bf16[2,2,64,256]{3,2,1,0:T(8,128)(2,1)S(1)} %fusion.6), channel_id=1, source_target_pairs={{0,16},{4,20},{8,24},{12,28},{16,0},{20,4},{24,8},{28,12},{1,17},{... | collective-permute-start | bytes 393224 | tf_op jit(solution)/shard_map/ppermute | solution.py:355
  76.7 5.0 %collective-permute-start.9 = (bf16[2,64,256]{2,1,0:T(8,128)(2,1)S(1)}, bf16[2,64,256]{2,1,0:T(8,128)(2,1)S(1)}, u32[]{:S(2)}, u32[]{:S(2)}) collective-permute-start(bf16[2,64,256]{2,1,0:T(8,128)(2,1)S(1)} %get-tuple-element.27), channel_id=1, source_target_pairs={{0,4},{4,0},{8,12},{12,8},{16,20},{20,16},{24,28},{28,24},{1,5},{5... | collective-permute-start | bytes 196616 | tf_op jit(solution)/shard_map/ppermute | solution.py:355
  77.3 4.5 %collective-permute-start.8 = (bf16[2,64,256]{2,1,0:T(8,128)(2,1)S(1)}, bf16[2,64,256]{2,1,0:T(8,128)(2,1)S(1)}, u32[]{:S(2)}, u32[]{:S(2)}) collective-permute-start(bf16[2,64,256]{2,1,0:T(8,128)(2,1)S(1)} %get-tuple-element.26), channel_id=1, source_target_pairs={{0,8},{4,12},{8,0},{12,4},{16,24},{20,28},{24,16},{28,20},{1,9},{5... | collective-permute-start | bytes 196616 | tf_op jit(solution)/shard_map/ppermute | solution.py:355
  81.7 5.1 %collective-permute-start.11 = (bf16[2,2,64,256]{3,2,1,0:T(8,128)(2,1)S(1)}, bf16[2,2,64,256]{3,2,1,0:T(8,128)(2,1)S(1)}, u32[]{:S(2)}, u32[]{:S(2)}) collective-permute-start(bf16[2,2,64,256]{3,2,1,0:T(8,128)(2,1)S(1)} %pad_maximum_fusion.2.b_ref), channel_id=1, source_target_pairs={{0,8},{4,12},{8,0},{12,4},{16,24},{20,28},{24,16},{28,20},{1,9},{5... | collective-permute-start | bytes 393224 | tf_op jit(solution)/shard_map/ppermute | solution.py:355
  81.8 5.0 %collective-permute-start.10 = (bf16[2,2,64,256]{3,2,1,0:T(8,128)(2,1)S(1)}, bf16[2,2,64,256]{3,2,1,0:T(8,128)(2,1)S(1)}, u32[]{:S(2)}, u32[]{:S(2)}) collective-permute-start(bf16[2,2,64,256]{3,2,1,0:T(8,128)(2,1)S(1)} %pad_maximum_fusion.1.a_ref), channel_id=1, source_target_pairs={{0,4},{4,0},{8,12},{12,8},{16,20},{20,16},{24,28},{28,24},{1,5},{5... | collective-permute-start | bytes 393224 | tf_op jit(solution)/shard_map/ppermute | solution.py:355
  90.8 1.8 %collective-permute-start.12 = (bf16[2,32,3072]{2,1,0:T(8,128)(2,1)S(1)}, bf16[2,32,3072]{2,1,0:T(8,128)(2,1)S(1)}, u32[]{:S(2)}, u32[]{:S(2)}) collective-permute-start(bf16[2,32,3072]{2,1,0:T(8,128)(2,1)S(1)} %get-tuple-element.29), channel_id=1, source_target_pairs={{0,1},{1,0},{2,3},{3,2},{4,5},{5,4},{6,7},{7,6},{8,9},{9,8},{10,11... | collective-permute-start | bytes 1179656 | tf_op jit(solution)/shard_map/ppermute | solution.py:55
  92.7 11.2 %collective-permute-start.13 = (bf16[2,32,3072]{2,1,0:T(8,128)(2,1)S(1)}, bf16[2,32,3072]{2,1,0:T(8,128)(2,1)S(1)}, u32[]{:S(2)}, u32[]{:S(2)}) collective-permute-start(bf16[2,32,3072]{2,1,0:T(8,128)(2,1)S(1)} %get-tuple-element.32), channel_id=1, source_target_pairs={{0,2},{1,3},{2,0},{3,1},{4,6},{5,7},{6,4},{7,5},{8,10},{9,11},{10,... | collective-permute-start | bytes 1179656 | tf_op jit(solution)/shard_map/ppermute | solution.py:59
  94.2 15.9 %slice-start = ((s8[12582912]{0:T(1024)(128)(4,1)}), s8[4194304]{0:T(1024)(128)(4,1)S(1)}, s32[]{:S(2)}) async-start(s8[12582912]{0:T(1024)(128)(4,1)} %bitcast.26), calls=%async_computation.1 | async-start | bytes 8388608
  94.2 15.9 %slice-start.1 = ((s8[12582912]{0:T(1024)(128)(4,1)}), s8[4194304]{0:T(1024)(128)(4,1)S(1)}, s32[]{:S(2)}) async-start(s8[12582912]{0:T(1024)(128)(4,1)} %bitcast.26), calls=%async_computation.2 | async-start | bytes 8388608
  103.9 4.6 %copy-start = (bf16[3072,2048]{1,0:T(8,128)(2,1)S(1)}, bf16[3072,2048]{1,0:T(8,128)(2,1)}, u32[]{:S(2)}) copy-start(bf16[3072,2048]{1,0:T(8,128)(2,1)} %down_score.1.after_ref) | copy-start | bytes 37748740
  108.5 2.2 %slice-start.2 = ((s8[12582912]{0:T(1024)(128)(4,1)}), s8[4194304]{0:T(1024)(128)(4,1)S(1)}, s32[]{:S(2)}) async-start(s8[12582912]{0:T(1024)(128)(4,1)} %bitcast.26), calls=%async_computation.3 | async-start | bytes 8388608
  108.6 1.5 %collective-permute-start.14 = (bf16[32,3072]{1,0:T(8,128)(2,1)S(1)}, bf16[32,3072]{1,0:T(8,128)(2,1)S(1)}, u32[]{:S(2)}, u32[]{:S(2)}) collective-permute-start(bf16[32,3072]{1,0:T(8,128)(2,1)S(1)} %combined.1.mine_ref), channel_id=1, source_target_pairs={{0,1},{1,0},{2,3},{3,2},{4,5},{5,4},{6,7},{7,6},{8,9},{9,8},{10,11... | collective-permute-start | bytes 589832 | tf_op jit(solution)/shard_map/ppermute | solution.py:55

commit v3 on v2

--- a/solution.py
+++ b/solution.py
@@ -10,6 +10,7 @@
 bf16 = jnp.bfloat16
 f32 = jnp.float32
 MIB = 1024 * 1024
+WAIT_FLOPS = 6 * 10**9
 IN_VMEM = pl.BlockSpec(memory_space=pltpu.VMEM)
 IN_HBM = pl.BlockSpec(memory_space=pltpu.HBM)
 
@@ -96,10 +97,18 @@
 def norm_call(tokens, norm_gain, copies, col_width):
     own, features = tokens.shape
 
-    def body(tokens_ref, gain_ref, out_ref, scaled):
-        tokens_f = tokens_ref[...].astype(f32)
+    def body(tokens_ref, gain_ref, out_ref, tokens_in, gain_in, scaled, sems):
+        loads = [
+            pltpu.make_async_copy(tokens_ref, tokens_in, sems.at[0]),
+            pltpu.make_async_copy(gain_ref, gain_in, sems.at[1]),
+        ]
+        for load in loads:
+            load.start()
+        for load in loads:
+            load.wait()
+        tokens_f = tokens_in[...].astype(f32)
         squares = jnp.sum(tokens_f * tokens_f, axis=1, keepdims=True)
-        scaled[...] = tokens_f * lax.rsqrt(squares / features + epsilon) * gain_ref[...]
+        scaled[...] = tokens_f * lax.rsqrt(squares / features + epsilon) * gain_in[...]
         first = pl.multiple_of(lax.axis_index("mp") * col_width, col_width)
         mine = scaled[:, pl.ds(first, col_width)].astype(bf16)
         for i in range(copies):
@@ -107,11 +116,86 @@
 
     return pl.pallas_call(
         body,
+        in_specs=[IN_HBM] * 2,
+        out_specs=IN_VMEM,
         out_shape=jax.ShapeDtypeStruct((copies, own, col_width), bf16),
-        scratch_shapes=[pltpu.VMEM((own, features), f32)],
-        compiler_params=params(8),
+        scratch_shapes=[
+            pltpu.VMEM((own, features), bf16),
+            pltpu.VMEM((1, features), f32),
+            pltpu.VMEM((own, features), f32),
+            pltpu.SemaphoreType.DMA((2,)),
+        ],
+        compiler_params=params(4),
+        cost_estimate=cost(WAIT_FLOPS, 4 * own * features),
         name="norm_rows",
-    )(tokens, norm_gain.reshape(1, features))
+    )(kept_out(tokens), kept_out(norm_gain.reshape(1, features)))
+
+
+def join_call(blocks):
+    n = len(blocks)
+    lead = sum(b[0].shape[0] for b in blocks)
+    own = blocks[0][0].shape[1]
+    cols = [b.shape[2] for b in blocks[0]]
+    whole = len(cols) == 1
+
+    def body(*refs):
+        a_ref, b_ref = refs[-2:]
+        at = 0
+        for block, k in zip(blocks, range(0, n * len(cols), len(cols))):
+            size = block[0].shape[0]
+            if whole:
+                half = cols[0] // 2
+                a_ref[at : at + size] = refs[k][:, :, :half]
+                b_ref[at : at + size] = refs[k][:, :, half:]
+            else:
+                a_ref[at : at + size] = refs[k][...]
+                b_ref[at : at + size] = refs[k + 1][...]
+            at += size
+
+    half = cols[0] // 2 if whole else cols[0]
+    shape = jax.ShapeDtypeStruct((lead, own, half), bf16)
+    flat = [part for block in blocks for part in block]
+    return pl.pallas_call(
+        body,
+        in_specs=[IN_VMEM] * len(flat),
+        out_specs=[IN_VMEM] * 2,
+        out_shape=[shape, shape],
+        compiler_params=params(4),
+        cost_estimate=cost(WAIT_FLOPS, 8 * lead * own * half),
+        name="join",
+    )(*flat)
+
+
+def order_call(a_blocks, b_blocks):
+    _, own, half = a_blocks[0].shape
+
+    def body(a0, a1, b0, b1, out_ref):
+        index = lax.axis_index("dp")
+        for refs, order, cols in (
+            ((a0, a1), (0, 4, 2, 6, 1, 5, 3, 7), slice(0, half)),
+            ((b0, b1), (0, 4, 1, 5, 2, 6, 3, 7), slice(half, 2 * half)),
+        ):
+            for p, flip in enumerate(order):
+                out_ref[lax.bitwise_xor(index, flip), :, cols] = refs[p // 4][p % 4]
+
+    return pl.pallas_call(
+        body,
+        in_specs=[IN_VMEM] * 4,
+        out_specs=IN_VMEM,
+        out_shape=jax.ShapeDtypeStruct((8, own, 2 * half), bf16),
+        compiler_params=params(4),
+        cost_estimate=cost(0, 64 * own * half),
+        name="token_order",
+    )(*a_blocks, *b_blocks)
+
+
+def gather_tree(block):
+    arrived = swap_dp(block, 4)
+    a_two, b_two = join_call([[block], [arrived]])
+    a_came, b_came = swap_dp(a_two, 2), swap_dp(b_two, 1)
+    a_four, b_four = join_call([[a_two, b_two], [a_came, b_came]])
+    a_came, b_came = swap_dp(a_four, 1), swap_dp(b_four, 2)
+    return order_call((a_four, a_came), (b_four, b_came))
 
 
 def gate_call(normed, w_gate, w_up, v_gate, chunk, chunks):
@@ -144,6 +228,55 @@
         cost_estimate=cost(6 * count * depth * width, 6 * depth * width),
         name="gate_products",
     )(normed, *[kept_out(w) for w in (w_gate, w_up, v_gate)])
+
+
+def gate_held_call(normed, w_gate, w_up, v_gate, chunk, chunks, after):
+    count, depth = normed.shape
+    half = count // 2
+    width = w_gate.shape[1] // chunks
+    block = block_of(width, 512)
+    steps = width // block
+    first = chunk * width
+
+    def body(normed_ref, gate_ref, up_ref, tan_ref, after_ref, keep_ref, send_ref, buffer, sems):
+        copies = [
+            pltpu.make_async_copy(
+                tan_ref.at[:, pl.ds(first + j * block, block)], buffer.at[j], sems.at[j]
+            )
+            for j in range(steps)
+        ]
+        for copy in copies:
+            copy.start()
+        upper = lax.axis_index("mp") % 2 == 1
+        for i, weight in enumerate((gate_ref, up_ref, None)):
+            for j in range(steps):
+                span = slice(j * block, (j + 1) * block)
+                if weight is None:
+                    copies[j].wait()
+                    right = buffer[j]
+                else:
+                    right = weight[:, first + j * block : first + (j + 1) * block]
+                part = dot(normed_ref[...], right, 1, 0)
+                low, high = part[:half], part[half:]
+                keep_ref[i, :, span] = jnp.where(upper, high, low)
+                send_ref[i, :, span] = jnp.where(upper, low, high).astype(bf16)
+
+    return pl.pallas_call(
+        body,
+        in_specs=[IN_VMEM] * 3 + [IN_HBM, pl.BlockSpec(memory_space=pl.ANY)],
+        out_specs=[IN_VMEM] * 2,
+        out_shape=[
+            jax.ShapeDtypeStruct((3, half, width), f32),
+            jax.ShapeDtypeStruct((3, half, width), bf16),
+        ],
+        scratch_shapes=[
+            pltpu.VMEM((steps, depth, block), bf16),
+            pltpu.SemaphoreType.DMA((steps,)),
+        ],
+        compiler_params=params(4 + 2 * depth * width // MIB),
+        cost_estimate=cost(6 * count * depth * width, 6 * depth * width),
+        name="gate_products",
+    )(normed, held(w_gate), held(w_up), kept_out(v_gate), after)
 
 
 def hidden_call(chip_sum, arrived, after):
@@ -301,7 +434,7 @@
         compiler_params=params(8),
         cost_estimate=cost(0, 22 * half * width),
         name="combined",
-    )(chip_sum, arrived, factors, after)
+    )(chip_sum, arrived, factors, kept_out(after))
 
 
 def gate_score_call(normed, mine, other, v_gate):
@@ -548,9 +681,14 @@
     own = tokens.shape[0]
     count = own * dp
     col_width = w_gate.shape[0]
-    copies = norm_call(tokens, norm_gain, dp, col_width)
-    normed = lax.all_to_all(copies, "dp", 0, 0, tiled=True).reshape(count, col_width)
-    keep, send = gate_call(normed, w_gate, w_up, v_gate, 0, 1)
+    if dp == 8:
+        block = norm_call(tokens, norm_gain, 1, col_width)
+        normed = gather_tree(block).reshape(count, col_width)
+        keep, send = gate_held_call(normed, w_gate, w_up, v_gate, 0, 1, normed)
+    else:
+        copies = norm_call(tokens, norm_gain, dp, col_width)
+        normed = lax.all_to_all(copies, "dp", 0, 0, tiled=True).reshape(count, col_width)
+        keep, send = gate_call(normed, w_gate, w_up, v_gate, 0, 1)
     chip_sum = keep + swap_core(send).astype(f32)
     chip_send = chip_sum.astype(bf16)
     w_down, v_down = load_call([w_down, v_down], chip_send, "load_down")

time: 118 us -> 105 us (0.89)
  blocking collectives: 16 us -> 0 us
  starting transfers between devices: 9.89 us -> 21 us
  Pallas kernels: 52.5 us -> 44.3 us
  waiting for transfers between devices: 31.1 us -> 37.8 us
  local copies, waits for them, and re-layouts: 6.83 us -> 0.63 us
    all_to_all x1 -> x0, blocking collectives: 16 us -> none  [per_device(): lax.all_to_all(copies, 'dp', 0, 0, tiled=True).reshape(count, col_width)]
    ppermute x9 -> x14, starting transfers between devices: 6.53 us -> 17.6 us  [swap_dp(): return lax.ppermute(value, 'dp', [(i, i ^ bit) for i in range(8)])]
    pallas_call x2 -> x5, Pallas kernels: 17.7 us -> 9.54 us  [the longest x1 8.38 us: gate_held_call(): pl.pallas_call(body, in_specs=[IN_VMEM] * 3 + [IN_HBM, pl.BlockSpec(memor...]
    ppermute x9 -> x14, waiting for transfers between devices: 16.2 us -> 22.7 us  [swap_dp(): return lax.ppermute(value, 'dp', [(i, i ^ bit) for i in range(8)])]
    unnamed x14 -> x20, local copies, waits for them, and re-layouts: 6.81 us -> 0.61 us
  transfers between devices with their start and end apart: 15 -> 20, of which waited for: 12 -> 16; matrix products, arithmetic and copies ran while one was open for 0% -> 0% of each run, Pallas kernels for 18% -> 20%
where the time goes in v3:
time: 105 us
  Pallas kernels  44.3 us (42%)
  waiting for transfers between devices  37.8 us (36%)
  starting transfers between devices  21 us (20%)
  between operations  1.1 us (1%)
    ppermute x14, waiting for transfers between devices, swap_dp(): return lax.ppermute(value, 'dp', [(i, i ^ bit) for i in range(8)])  22.7 us
    ppermute x14, starting transfers between devices, swap_dp(): return lax.ppermute(value, 'dp', [(i, i ^ bit) for i in range(8)])  17.6 us
    pallas_call x1, Pallas kernels, gate_held_call(): pl.pallas_call(body, in_specs=[IN_VMEM] * 3 + [IN_HBM, pl.BlockSpec(memor...  8.38 us
    pallas_call x1, Pallas kernels, load_call(): pl.pallas_call(body, in_specs=[IN_HBM] * n + [pl.BlockSpec(memory_space=p...  8.3 us
    ppermute x2, waiting for transfers between devices, swap_chip(): return lax.ppermute(value, 'mp', [(i, i ^ 2) for i in range(4)])  8.25 us
    pallas_call x1, Pallas kernels, down_score_call(): pl.pallas_call(body, in_specs=[IN_VMEM] * 4, out_specs=IN_HBM, out_shape=...  6.98 us
    pallas_call x1, Pallas kernels, gate_score_call(): pl.pallas_call(body, in_specs=[IN_VMEM] * 4, out_specs=IN_HBM, out_shape=...  6.92 us
    ppermute x4, waiting for transfers between devices, swap_core(): return lax.ppermute(value, 'mp', [(i, i ^ 1) for i in range(4)])  6.84 us
  transfers between devices with their start and end apart: 20, of which 16 were waited for; matrix products, arithmetic and copies ran while one was open for 0% of the time, Pallas kernels for 20%

profile of v3, /device:TPU:0, one launch (start us, length us, event | category | flops | bytes accessed | tf_op | source)
XLA Modules:
  0.0 105.2 jit_solution(14815169696492690626)
XLA Ops:
  0.6 1.1 %norm_rows.1.refs_0_ = bf16[1,8,2048]{2,1,0:T(8,128)(2,1)S(1)} custom-call(bf16[8,8192]{1,0:T(8,128)(2,1)} %tokens_ref.1, f32[1,8192]{1,0:T(1,128)} %bitcast.39), custom_call_target="tpu_custom_call" | custom-call | flops 6000000000 | bytes 262144 | tf_op jit(solution)/shard_map/norm_rows/pallas_call | solution.py:117
  1.8 4.1 %collective-permute-start = (bf16[1,8,2048]{2,1,0:T(8,128)(2,1)S(1)}, bf16[1,8,2048]{2,1,0:T(8,128)(2,1)S(1)}, u32[]{:S(2)}, u32[]{:S(2)}) collective-permute-start(bf16[1,8,2048]{2,1,0:T(8,128)(2,1)S(1)} %norm_rows.1.refs_0_), channel_id=1, source_target_pairs={{0,16},{4,20},{8,24},{12,28},{16,0},{20,4},{24,8},{28,12},{1,17},{... | collective-permute-start | bytes 98312 | tf_op jit(solution)/shard_map/ppermute | solution.py:488
  5.9 2.2 %collective-permute-done.refs_1_ = bf16[1,8,2048]{2,1,0:T(8,128)(2,1)S(1)} collective-permute-done((bf16[1,8,2048]{2,1,0:T(8,128)(2,1)S(1)}, bf16[1,8,2048]{2,1,0:T(8,128)(2,1)S(1)}, u32[]{:S(2)}, u32[]{:S(2)}) %collective-permute-start) | collective-permute-done | bytes 32800 | tf_op jit(solution)/shard_map/ppermute | solution.py:488
  8.1 0.0 slice-start.3
  8.1 1.6 %collective-permute-start.1 = (bf16[2,8,1024]{2,1,0:T(8,128)(2,1)S(1)}, bf16[2,8,1024]{2,1,0:T(8,128)(2,1)S(1)}, u32[]{:S(2)}, u32[]{:S(2)}) collective-permute-start(bf16[2,8,1024]{2,1,0:T(8,128)(2,1)S(1)} %get-tuple-element.21.refs_0_), channel_id=1, source_target_pairs={{0,8},{4,12},{8,0},{12,4},{16,24},{20,28},{24,16},{28,20},{1,9},{5... | collective-permute-start | bytes 98312 | tf_op jit(solution)/shard_map/ppermute | solution.py:488
  9.8 1.5 %collective-permute-start.2 = (bf16[2,8,1024]{2,1,0:T(8,128)(2,1)S(1)}, bf16[2,8,1024]{2,1,0:T(8,128)(2,1)S(1)}, u32[]{:S(2)}, u32[]{:S(2)}) collective-permute-start(bf16[2,8,1024]{2,1,0:T(8,128)(2,1)S(1)} %get-tuple-element.22.refs_1_), channel_id=1, source_target_pairs={{0,4},{4,0},{8,12},{12,8},{16,20},{20,16},{24,28},{28,24},{1,5},{5... | collective-permute-start | bytes 98312 | tf_op jit(solution)/shard_map/ppermute | solution.py:488
  11.3 0.8 collective-permute-done.1.refs_2_
  12.1 1.6 %collective-permute-done.2.refs_3_ = bf16[2,8,1024]{2,1,0:T(8,128)(2,1)S(1)} collective-permute-done((bf16[2,8,1024]{2,1,0:T(8,128)(2,1)S(1)}, bf16[2,8,1024]{2,1,0:T(8,128)(2,1)S(1)}, u32[]{:S(2)}, u32[]{:S(2)}) %collective-permute-start.2) | collective-permute-done | bytes 32800 | tf_op jit(solution)/shard_map/ppermute | solution.py:488
  13.7 1.6 %collective-permute-start.3 = (bf16[4,8,1024]{2,1,0:T(8,128)(2,1)S(1)}, bf16[4,8,1024]{2,1,0:T(8,128)(2,1)S(1)}, u32[]{:S(2)}, u32[]{:S(2)}) collective-permute-start(bf16[4,8,1024]{2,1,0:T(8,128)(2,1)S(1)} %get-tuple-element.23.a0), channel_id=1, source_target_pairs={{0,4},{4,0},{8,12},{12,8},{16,20},{20,16},{24,28},{28,24},{1,5},{5... | collective-permute-start | bytes 196616 | tf_op jit(solution)/shard_map/ppermute | solution.py:488
  15.3 0.9 collective-permute-start.4
  16.2 1.8 %collective-permute-done.3.a1 = bf16[4,8,1024]{2,1,0:T(8,128)(2,1)S(1)} collective-permute-done((bf16[4,8,1024]{2,1,0:T(8,128)(2,1)S(1)}, bf16[4,8,1024]{2,1,0:T(8,128)(2,1)S(1)}, u32[]{:S(2)}, u32[]{:S(2)}) %collective-permute-start.3) | collective-permute-done | bytes 65568 | tf_op jit(solution)/shard_map/ppermute | solution.py:488
  18.0 1.6 %collective-permute-done.4.b1 = bf16[4,8,1024]{2,1,0:T(8,128)(2,1)S(1)} collective-permute-done((bf16[4,8,1024]{2,1,0:T(8,128)(2,1)S(1)}, bf16[4,8,1024]{2,1,0:T(8,128)(2,1)S(1)}, u32[]{:S(2)}, u32[]{:S(2)}) %collective-permute-start.4) | collective-permute-done | bytes 65568 | tf_op jit(solution)/shard_map/ppermute | solution.py:488
  19.6 0.0 slice-done.6
  19.6 0.0 slice-done.7
  19.6 0.0 slice-done.3
  19.6 0.0 slice-done.4
  19.7 0.0 slice-done.5
  19.7 0.0 slice-done.8
  19.7 8.4 %gate_products.1 = (f32[3,32,3072]{2,1,0:T(8,128)S(1)}, bf16[3,32,3072]{2,1,0:T(8,128)(2,1)S(1)}) custom-call(bf16[64,2048]{1,0:T(8,128)(2,1)S(1)} %bitcast.32, bf16[2048,3072]{1,0:T(8,128)(2,1)S(1)} %bitcast.29, bf16[2048,3072]{1,0:T(8,128)(2,1)S(1)} %bitcast.31, bf16[2048,3072]{1,0:T(8,128)(2,1)} %v_ref.1, bf16[64,2048]{1,0:T(8,128)(2,1)S(1)} %bitcast.33), custom_call_target="tpu_custom_call" | custom-call | flops 2415919104 | bytes 37748736 | tf_op jit(solution)/shard_map/gate_products/pallas_call | solution.py:264
  28.1 0.1 collective-permute-start.5
  28.2 2.0 %collective-permute-done.5 = bf16[3,32,3072]{2,1,0:T(8,128)(2,1)S(1)} collective-permute-done((bf16[3,32,3072]{2,1,0:T(8,128)(2,1)S(1)}, bf16[3,32,3072]{2,1,0:T(8,128)(2,1)S(1)}, u32[]{:S(2)}, u32[]{:S(2)}) %collective-permute-start.5) | collective-permute-done | bytes 589856 | tf_op jit(solution)/shard_map/ppermute | solution.py:56
  30.1 0.2 fusion.8
  30.3 1.6 %collective-permute-start.6 = (bf16[3,32,3072]{2,1,0:T(8,128)(2,1)S(1)}, bf16[3,32,3072]{2,1,0:T(8,128)(2,1)S(1)}, u32[]{:S(2)}, u32[]{:S(2)}) collective-permute-start(bf16[3,32,3072]{2,1,0:T(8,128)(2,1)S(1)} %get-tuple-element.42.refs_2_), channel_id=1, source_target_pairs={{0,2},{1,3},{2,0},{3,1},{4,6},{5,7},{6,4},{7,5},{8,10},{9,11},{10,... | collective-permute-start | bytes 1769480 | tf_op jit(solution)/shard_map/ppermute | solution.py:60
  31.9 8.3 %load_down.1 = (bf16[3072,2048]{1,0:T(8,128)(2,1)S(1)}, bf16[3072,2048]{1,0:T(8,128)(2,1)S(1)}) custom-call(bf16[3072,2048]{1,0:T(8,128)(2,1)} %refs_0_.1, bf16[3072,2048]{1,0:T(8,128)(2,1)} %refs_1_.1, bf16[3,32,3072]{2,1,0:T(8,128)(2,1)S(1)} %get-tuple-element.42.refs_2_), custom_call_target="tpu_custom_call" | custom-call | bytes 50331648 | tf_op jit(solution)/shard_map/load_down/pallas_call | solution.py:85
  40.2 5.6 %collective-permute-done.6.arrived_ref = bf16[3,32,3072]{2,1,0:T(8,128)(2,1)S(1)} collective-permute-done((bf16[3,32,3072]{2,1,0:T(8,128)(2,1)S(1)}, bf16[3,32,3072]{2,1,0:T(8,128)(2,1)S(1)}, u32[]{:S(2)}, u32[]{:S(2)}) %collective-permute-start.6) | collective-permute-done | bytes 589856 | tf_op jit(solution)/shard_map/ppermute | solution.py:60
  45.7 0.4 hidden_units.1
  46.1 0.1 collective-permute-start.7
  46.2 1.7 %collective-permute-done.7.other_ref = bf16[2,32,3072]{2,1,0:T(8,128)(2,1)S(1)} collective-permute-done((bf16[2,32,3072]{2,1,0:T(8,128)(2,1)S(1)}, bf16[2,32,3072]{2,1,0:T(8,128)(2,1)S(1)}, u32[]{:S(2)}, u32[]{:S(2)}) %collective-permute-start.7) | collective-permute-done | bytes 393248 | tf_op jit(solution)/shard_map/ppermute | solution.py:56
  47.9 2.1 %pieces_away.1 = (bf16[2,2,64,256]{3,2,1,0:T(8,128)(2,1)S(1)}, bf16[2,2,64,256]{3,2,1,0:T(8,128)(2,1)S(1)}) custom-call(bf16[2,32,3072]{2,1,0:T(8,128)(2,1)S(1)} %get-tuple-element.28.mine_ref, bf16[2,32,3072]{2,1,0:T(8,128)(2,1)S(1)} %collective-permute-done.7.other_ref, bf16[3072,2048]{1,0:T(8,128)(2,1)S(1)} %get-tuple-element.29.w_ref, ...), custom_call_target="tpu_custom_call" | custom-call | flops 1207959552 | bytes 12582912 | tf_op jit(solution)/shard_map/pieces_away/pallas_call | solution.py:512
  50.1 0.6 collective-permute-start.8
  50.6 0.7 collective-permute-start.10
  51.3 2.1 %pieces_home.1 = (f32[2,2,64,256]{3,2,1,0:T(8,128)S(1)}, f32[2,2,64,256]{3,2,1,0:T(8,128)S(1)}) custom-call(bf16[2,32,3072]{2,1,0:T(8,128)(2,1)S(1)} %get-tuple-element.28.mine_ref, bf16[2,32,3072]{2,1,0:T(8,128)(2,1)S(1)} %collective-permute-done.7.other_ref, bf16[3072,2048]{1,0:T(8,128)(2,1)S(1)} %get-tuple-element.29.w_ref, ...), custom_call_target="tpu_custom_call" | custom-call | flops 1207959552 | bytes 12582912 | tf_op jit(solution)/shard_map/pieces_home/pallas_call | solution.py:512
  53.5 2.2 %collective-permute-done.8 = bf16[2,2,64,256]{3,2,1,0:T(8,128)(2,1)S(1)} collective-permute-done((bf16[2,2,64,256]{3,2,1,0:T(8,128)(2,1)S(1)}, bf16[2,2,64,256]{3,2,1,0:T(8,128)(2,1)S(1)}, u32[]{:S(2)}, u32[]{:S(2)}) %collective-permute-start.8) | collective-permute-done | bytes 131104 | tf_op jit(solution)/shard_map/ppermute | solution.py:488
  55.7 1.0 collective-permute-start.9
  56.7 0.0 collective-permute-done.10
  56.8 0.8 collective-permute-start.11
  57.5 2.5 %collective-permute-done.9 = bf16[2,64,256]{2,1,0:T(8,128)(2,1)S(1)} collective-permute-done((bf16[2,64,256]{2,1,0:T(8,128)(2,1)S(1)}, bf16[2,64,256]{2,1,0:T(8,128)(2,1)S(1)}, u32[]{:S(2)}, u32[]{:S(2)}) %collective-permute-start.9) | collective-permute-done | bytes 65568 | tf_op jit(solution)/shard_map/ppermute | solution.py:488
  60.1 1.0 collective-permute-done.11
  61.1 2.2 %collective-permute-start.12 = (bf16[2,2,64,256]{3,2,1,0:T(8,128)(2,1)S(1)}, bf16[2,2,64,256]{3,2,1,0:T(8,128)(2,1)S(1)}, u32[]{:S(2)}, u32[]{:S(2)}) collective-permute-start(bf16[2,2,64,256]{3,2,1,0:T(8,128)(2,1)S(1)} %fusion.6), channel_id=1, source_target_pairs={{0,16},{4,20},{8,24},{12,28},{16,0},{20,4},{24,8},{28,12},{1,17},{... | collective-permute-start | bytes 393224 | tf_op jit(solution)/shard_map/ppermute | solution.py:488
  63.3 5.2 %collective-permute-done.12.arrived_ref = bf16[2,2,64,256]{3,2,1,0:T(8,128)(2,1)S(1)} collective-permute-done((bf16[2,2,64,256]{3,2,1,0:T(8,128)(2,1)S(1)}, bf16[2,2,64,256]{3,2,1,0:T(8,128)(2,1)S(1)}, u32[]{:S(2)}, u32[]{:S(2)}) %collective-permute-start.12) | collective-permute-done | bytes 131104 | tf_op jit(solution)/shard_map/ppermute | solution.py:488
  68.5 0.0 copy-done
  68.5 0.8 collective-permute-start.14
  69.3 0.4 collective-permute-start.13
  69.7 3.8 %collective-permute-done.14 = bf16[2,64,256]{2,1,0:T(8,128)(2,1)S(1)} collective-permute-done((bf16[2,64,256]{2,1,0:T(8,128)(2,1)S(1)}, bf16[2,64,256]{2,1,0:T(8,128)(2,1)S(1)}, u32[]{:S(2)}, u32[]{:S(2)}) %collective-permute-start.14) | collective-permute-done | bytes 65568 | tf_op jit(solution)/shard_map/ppermute | solution.py:488
  73.5 0.1 collective-permute-start.16
  73.6 0.0 collective-permute-done.13
  73.6 1.4 %collective-permute-start.15 = (bf16[2,2,64,256]{3,2,1,0:T(8,128)(2,1)S(1)}, bf16[2,2,64,256]{3,2,1,0:T(8,128)(2,1)S(1)}, u32[]{:S(2)}, u32[]{:S(2)}) collective-permute-start(bf16[2,2,64,256]{3,2,1,0:T(8,128)(2,1)S(1)} %pad_maximum_fusion.1.a_ref), channel_id=1, source_target_pairs={{0,4},{4,0},{8,12},{12,8},{16,20},{20,16},{24,28},{28,24},{1,5},{5... | collective-permute-start | bytes 393224 | tf_op jit(solution)/shard_map/ppermute | solution.py:488
  75.0 3.8 %back_first.1.part_ref = f32[3072,128]{1,0:T(8,128)S(1)} custom-call(bf16[2,2,64,256]{3,2,1,0:T(8,128)(2,1)S(1)} %pad_maximum_fusion.1.a_ref, bf16[2,2,64,256]{3,2,1,0:T(8,128)(2,1)S(1)} %pad_maximum_fusion.2.b_ref, bf16[3072,2048]{1,0:T(8,128)(2,1)S(1)} %get-tuple-element.29.w_ref, bf16[3072,2048]{1,0:T(8,128)(2,1)S(1)} %get-tuple-element.27.after_ref.v_ref), custom_call_target="tpu_custom_call" | custom-call | flops 603979776 | bytes 6291456 | tf_op jit(solution)/shard_map/back_first/pallas_call | solution.py:579
  78.8 0.0 collective-permute-done.16.b_far_ref
  78.8 0.0 collective-permute-done.15.a_far_ref
  78.8 4.0 %back_second.1 = (f32[2,32,3072]{2,1,0:T(8,128)S(1)}, bf16[2,32,3072]{2,1,0:T(8,128)(2,1)S(1)}, bf16[2,64,2048]{2,1,0:T(8,128)(2,1)S(1)}) custom-call(bf16[2,2,64,256]{3,2,1,0:T(8,128)(2,1)S(1)} %pad_maximum_fusion.1.a_ref, bf16[2,2,64,256]{3,2,1,0:T(8,128)(2,1)S(1)} %pad_maximum_fusion.2.b_ref, ...), custom_call_target="tpu_custom_call" | custom-call | flops 603979776 | bytes 6291456 | tf_op jit(solution)/shard_map/back_second/pallas_call | solution.py:624
  82.8 0.1 collective-permute-start.17
  82.9 1.7 %collective-permute-done.17 = bf16[2,32,3072]{2,1,0:T(8,128)(2,1)S(1)} collective-permute-done((bf16[2,32,3072]{2,1,0:T(8,128)(2,1)S(1)}, bf16[2,32,3072]{2,1,0:T(8,128)(2,1)S(1)}, u32[]{:S(2)}, u32[]{:S(2)}) %collective-permute-start.17) | collective-permute-done | bytes 393248 | tf_op jit(solution)/shard_map/ppermute | solution.py:56
  84.6 0.1 fusion.7
  84.7 1.6 %collective-permute-start.18 = (bf16[2,32,3072]{2,1,0:T(8,128)(2,1)S(1)}, bf16[2,32,3072]{2,1,0:T(8,128)(2,1)S(1)}, u32[]{:S(2)}, u32[]{:S(2)}) collective-permute-start(bf16[2,32,3072]{2,1,0:T(8,128)(2,1)S(1)} %get-tuple-element.40), channel_id=1, source_target_pairs={{0,2},{1,3},{2,0},{3,1},{4,6},{5,7},{6,4},{7,5},{8,10},{9,11},{10,... | collective-permute-start | bytes 1179656 | tf_op jit(solution)/shard_map/ppermute | solution.py:60
  86.2 7.0 %down_score.1.after_ref = bf16[3072,2048]{1,0:T(8,128)(2,1)} custom-call(bf16[2,32,3072]{2,1,0:T(8,128)(2,1)S(1)} %get-tuple-element.28.mine_ref, bf16[2,32,3072]{2,1,0:T(8,128)(2,1)S(1)} %collective-permute-done.7.other_ref, bf16[2,64,2048]{2,1,0:T(8,128)(2,1)S(1)} %get-tuple-element.39.res_ref, bf16[3072,2048]{1,0:T(8,128)(2,1)S(1)} %get-tuple-element.27.after_ref.v_ref), custom_call_target="tpu_custom_call" | custom-call | flops 1610612736 | bytes 25165824 | tf_op jit(solution)/shard_map/down_score/pallas_call | solution.py:400
  93.2 2.7 %collective-permute-done.18.arrived_ref = bf16[2,32,3072]{2,1,0:T(8,128)(2,1)S(1)} collective-permute-done((bf16[2,32,3072]{2,1,0:T(8,128)(2,1)S(1)}, bf16[2,32,3072]{2,1,0:T(8,128)(2,1)S(1)}, u32[]{:S(2)}, u32[]{:S(2)}) %collective-permute-start.18) | collective-permute-done | bytes 393248 | tf_op jit(solution)/shard_map/ppermute | solution.py:60
  95.9 0.1 combined.1.mine_ref
  96.0 0.1 collective-permute-start.19
  96.1 1.4 %collective-permute-done.19.other_ref = bf16[32,3072]{1,0:T(8,128)(2,1)S(1)} collective-permute-done((bf16[32,3072]{1,0:T(8,128)(2,1)S(1)}, bf16[32,3072]{1,0:T(8,128)(2,1)S(1)}, u32[]{:S(2)}, u32[]{:S(2)}) %collective-permute-start.19) | collective-permute-done | bytes 196640 | tf_op jit(solution)/shard_map/ppermute | solution.py:56
  97.5 0.0 slice-done
  97.5 0.0 slice-done.1
  97.5 0.6 slice-done.2
  98.1 6.9 %gate_score.1 = bf16[2048,3072]{1,0:T(8,128)(2,1)} custom-call(bf16[64,2048]{1,0:T(8,128)(2,1)S(1)} %bitcast.34, bf16[32,3072]{1,0:T(8,128)(2,1)S(1)} %combined.1.mine_ref, bf16[32,3072]{1,0:T(8,128)(2,1)S(1)} %collective-permute-done.19.other_ref, bf16[2048,3072]{1,0:T(8,128)(2,1)S(1)} %bitcast.27), custom_call_target="tpu_custom_call" | custom-call | flops 805306368 | bytes 25165824 | tf_op jit(solution)/shard_map/gate_score/pallas_call | solution.py:467
  (26 shorter events, 0.3 us)
Async XLA Ops:
  1.8 6.3 %collective-permute-start = (bf16[1,8,2048]{2,1,0:T(8,128)(2,1)S(1)}, bf16[1,8,2048]{2,1,0:T(8,128)(2,1)S(1)}, u32[]{:S(2)}, u32[]{:S(2)}) collective-permute-start(bf16[1,8,2048]{2,1,0:T(8,128)(2,1)S(1)} %norm_rows.1.refs_0_), channel_id=1, source_target_pairs={{0,16},{4,20},{8,24},{12,28},{16,0},{20,4},{24,8},{28,12},{1,17},{... | collective-permute-start | bytes 98312 | tf_op jit(solution)/shard_map/ppermute | solution.py:488
  8.1 11.5 %slice-start.6 = ((s8[12582912]{0:T(1024)(128)(4,1)}), s8[4194304]{0:T(1024)(128)(4,1)S(1)}, s32[]{:S(2)}) async-start(s8[12582912]{0:T(1024)(128)(4,1)} %bitcast.30), calls=%async_computation.6 | async-start | bytes 8388608
  8.1 11.5 %slice-start.7 = ((s8[12582912]{0:T(1024)(128)(4,1)}), s8[4194304]{0:T(1024)(128)(4,1)S(1)}, s32[]{:S(2)}) async-start(s8[12582912]{0:T(1024)(128)(4,1)} %bitcast.30), calls=%async_computation.7 | async-start | bytes 8388608
  8.1 11.5 %slice-start.3 = ((s8[12582912]{0:T(1024)(128)(4,1)}), s8[4194304]{0:T(1024)(128)(4,1)S(1)}, s32[]{:S(2)}) async-start(s8[12582912]{0:T(1024)(128)(4,1)} %bitcast.28), calls=%async_computation.3 | async-start | bytes 8388608
  8.1 4.0 %collective-permute-start.1 = (bf16[2,8,1024]{2,1,0:T(8,128)(2,1)S(1)}, bf16[2,8,1024]{2,1,0:T(8,128)(2,1)S(1)}, u32[]{:S(2)}, u32[]{:S(2)}) collective-permute-start(bf16[2,8,1024]{2,1,0:T(8,128)(2,1)S(1)} %get-tuple-element.21.refs_0_), channel_id=1, source_target_pairs={{0,8},{4,12},{8,0},{12,4},{16,24},{20,28},{24,16},{28,20},{1,9},{5... | collective-permute-start | bytes 98312 | tf_op jit(solution)/shard_map/ppermute | solution.py:488
  9.7 9.9 %slice-start.4 = ((s8[12582912]{0:T(1024)(128)(4,1)}), s8[4194304]{0:T(1024)(128)(4,1)S(1)}, s32[]{:S(2)}) async-start(s8[12582912]{0:T(1024)(128)(4,1)} %bitcast.28), calls=%async_computation.4 | async-start | bytes 8388608
  9.7 9.9 %slice-start.5 = ((s8[12582912]{0:T(1024)(128)(4,1)}), s8[4194304]{0:T(1024)(128)(4,1)S(1)}, s32[]{:S(2)}) async-start(s8[12582912]{0:T(1024)(128)(4,1)} %bitcast.28), calls=%async_computation.5 | async-start | bytes 8388608
  9.8 9.9 %slice-start.8 = ((s8[12582912]{0:T(1024)(128)(4,1)}), s8[4194304]{0:T(1024)(128)(4,1)S(1)}, s32[]{:S(2)}) async-start(s8[12582912]{0:T(1024)(128)(4,1)} %bitcast.30), calls=%async_computation.8 | async-start | bytes 8388608
  9.8 3.9 %collective-permute-start.2 = (bf16[2,8,1024]{2,1,0:T(8,128)(2,1)S(1)}, bf16[2,8,1024]{2,1,0:T(8,128)(2,1)S(1)}, u32[]{:S(2)}, u32[]{:S(2)}) collective-permute-start(bf16[2,8,1024]{2,1,0:T(8,128)(2,1)S(1)} %get-tuple-element.22.refs_1_), channel_id=1, source_target_pairs={{0,4},{4,0},{8,12},{12,8},{16,20},{20,16},{24,28},{28,24},{1,5},{5... | collective-permute-start | bytes 98312 | tf_op jit(solution)/shard_map/ppermute | solution.py:488
  13.7 4.3 %collective-permute-start.3 = (bf16[4,8,1024]{2,1,0:T(8,128)(2,1)S(1)}, bf16[4,8,1024]{2,1,0:T(8,128)(2,1)S(1)}, u32[]{:S(2)}, u32[]{:S(2)}) collective-permute-start(bf16[4,8,1024]{2,1,0:T(8,128)(2,1)S(1)} %get-tuple-element.23.a0), channel_id=1, source_target_pairs={{0,4},{4,0},{8,12},{12,8},{16,20},{20,16},{24,28},{28,24},{1,5},{5... | collective-permute-start | bytes 196616 | tf_op jit(solution)/shard_map/ppermute | solution.py:488
  15.3 4.3 %collective-permute-start.4 = (bf16[4,8,1024]{2,1,0:T(8,128)(2,1)S(1)}, bf16[4,8,1024]{2,1,0:T(8,128)(2,1)S(1)}, u32[]{:S(2)}, u32[]{:S(2)}) collective-permute-start(bf16[4,8,1024]{2,1,0:T(8,128)(2,1)S(1)} %get-tuple-element.24.b0), channel_id=1, source_target_pairs={{0,8},{4,12},{8,0},{12,4},{16,24},{20,28},{24,16},{28,20},{1,9},{5... | collective-permute-start | bytes 196616 | tf_op jit(solution)/shard_map/ppermute | solution.py:488
  28.1 2.1 %collective-permute-start.5 = (bf16[3,32,3072]{2,1,0:T(8,128)(2,1)S(1)}, bf16[3,32,3072]{2,1,0:T(8,128)(2,1)S(1)}, u32[]{:S(2)}, u32[]{:S(2)}) collective-permute-start(bf16[3,32,3072]{2,1,0:T(8,128)(2,1)S(1)} %get-tuple-element.26), channel_id=1, source_target_pairs={{0,1},{1,0},{2,3},{3,2},{4,5},{5,4},{6,7},{7,6},{8,9},{9,8},{10,11... | collective-permute-start | bytes 1769480 | tf_op jit(solution)/shard_map/ppermute | solution.py:56
  30.3 15.4 %collective-permute-start.6 = (bf16[3,32,3072]{2,1,0:T(8,128)(2,1)S(1)}, bf16[3,32,3072]{2,1,0:T(8,128)(2,1)S(1)}, u32[]{:S(2)}, u32[]{:S(2)}) collective-permute-start(bf16[3,32,3072]{2,1,0:T(8,128)(2,1)S(1)} %get-tuple-element.42.refs_2_), channel_id=1, source_target_pairs={{0,2},{1,3},{2,0},{3,1},{4,6},{5,7},{6,4},{7,5},{8,10},{9,11},{10,... | collective-permute-start | bytes 1769480 | tf_op jit(solution)/shard_map/ppermute | solution.py:60
  46.1 1.8 %collective-permute-start.7 = (bf16[2,32,3072]{2,1,0:T(8,128)(2,1)S(1)}, bf16[2,32,3072]{2,1,0:T(8,128)(2,1)S(1)}, u32[]{:S(2)}, u32[]{:S(2)}) collective-permute-start(bf16[2,32,3072]{2,1,0:T(8,128)(2,1)S(1)} %get-tuple-element.28.mine_ref), channel_id=1, source_target_pairs={{0,1},{1,0},{2,3},{3,2},{4,5},{5,4},{6,7},{7,6},{8,9},{9,8},{10,11... | collective-permute-start | bytes 1179656 | tf_op jit(solution)/shard_map/ppermute | solution.py:56
  50.1 5.6 %collective-permute-start.8 = (bf16[2,2,64,256]{3,2,1,0:T(8,128)(2,1)S(1)}, bf16[2,2,64,256]{3,2,1,0:T(8,128)(2,1)S(1)}, u32[]{:S(2)}, u32[]{:S(2)}) collective-permute-start(bf16[2,2,64,256]{3,2,1,0:T(8,128)(2,1)S(1)} %get-tuple-element.31), channel_id=1, source_target_pairs={{0,4},{4,0},{8,12},{12,8},{16,20},{20,16},{24,28},{28,24},{1,5},{5... | collective-permute-start | bytes 393224 | tf_op jit(solution)/shard_map/ppermute | solution.py:488
  50.6 17.9 %copy-start = (bf16[64,2048]{1,0:T(8,128)(2,1)S(1)}, bf16[64,2048]{1,0:T(8,128)(2,1)}, u32[]{:S(2)}) copy-start(bf16[64,2048]{1,0:T(8,128)(2,1)} %target_ref.1) | copy-start | bytes 786436
  50.6 6.1 %collective-permute-start.10 = (bf16[2,2,64,256]{3,2,1,0:T(8,128)(2,1)S(1)}, bf16[2,2,64,256]{3,2,1,0:T(8,128)(2,1)S(1)}, u32[]{:S(2)}, u32[]{:S(2)}) collective-permute-start(bf16[2,2,64,256]{3,2,1,0:T(8,128)(2,1)S(1)} %get-tuple-element.33), channel_id=1, source_target_pairs={{0,8},{4,12},{8,0},{12,4},{16,24},{20,28},{24,16},{28,20},{1,9},{5... | collective-permute-start | bytes 393224 | tf_op jit(solution)/shard_map/ppermute | solution.py:488
  55.7 4.3 %collective-permute-start.9 = (bf16[2,64,256]{2,1,0:T(8,128)(2,1)S(1)}, bf16[2,64,256]{2,1,0:T(8,128)(2,1)S(1)}, u32[]{:S(2)}, u32[]{:S(2)}) collective-permute-start(bf16[2,64,256]{2,1,0:T(8,128)(2,1)S(1)} %fusion.4), channel_id=1, source_target_pairs={{0,8},{4,12},{8,0},{12,4},{16,24},{20,28},{24,16},{28,20},{1,9},{5... | collective-permute-start | bytes 196616 | tf_op jit(solution)/shard_map/ppermute | solution.py:488
  56.8 4.3 %collective-permute-start.11 = (bf16[2,64,256]{2,1,0:T(8,128)(2,1)S(1)}, bf16[2,64,256]{2,1,0:T(8,128)(2,1)S(1)}, u32[]{:S(2)}, u32[]{:S(2)}) collective-permute-start(bf16[2,64,256]{2,1,0:T(8,128)(2,1)S(1)} %fusion.5), channel_id=1, source_target_pairs={{0,4},{4,0},{8,12},{12,8},{16,20},{20,16},{24,28},{28,24},{1,5},{5... | collective-permute-start | bytes 196616 | tf_op jit(solution)/shard_map/ppermute | solution.py:488
  61.1 7.3 %collective-permute-start.12 = (bf16[2,2,64,256]{3,2,1,0:T(8,128)(2,1)S(1)}, bf16[2,2,64,256]{3,2,1,0:T(8,128)(2,1)S(1)}, u32[]{:S(2)}, u32[]{:S(2)}) collective-permute-start(bf16[2,2,64,256]{3,2,1,0:T(8,128)(2,1)S(1)} %fusion.6), channel_id=1, source_target_pairs={{0,16},{4,20},{8,24},{12,28},{16,0},{20,4},{24,8},{28,12},{1,17},{... | collective-permute-start | bytes 393224 | tf_op jit(solution)/shard_map/ppermute | solution.py:488
  68.5 4.9 %collective-permute-start.14 = (bf16[2,64,256]{2,1,0:T(8,128)(2,1)S(1)}, bf16[2,64,256]{2,1,0:T(8,128)(2,1)S(1)}, u32[]{:S(2)}, u32[]{:S(2)}) collective-permute-start(bf16[2,64,256]{2,1,0:T(8,128)(2,1)S(1)} %get-tuple-element.35), channel_id=1, source_target_pairs={{0,4},{4,0},{8,12},{12,8},{16,20},{20,16},{24,28},{28,24},{1,5},{5... | collective-permute-start | bytes 196616 | tf_op jit(solution)/shard_map/ppermute | solution.py:488
  69.3 4.3 %collective-permute-start.13 = (bf16[2,64,256]{2,1,0:T(8,128)(2,1)S(1)}, bf16[2,64,256]{2,1,0:T(8,128)(2,1)S(1)}, u32[]{:S(2)}, u32[]{:S(2)}) collective-permute-start(bf16[2,64,256]{2,1,0:T(8,128)(2,1)S(1)} %get-tuple-element.34), channel_id=1, source_target_pairs={{0,8},{4,12},{8,0},{12,4},{16,24},{20,28},{24,16},{28,20},{1,9},{5... | collective-permute-start | bytes 196616 | tf_op jit(solution)/shard_map/ppermute | solution.py:488
  73.5 5.3 %collective-permute-start.16 = (bf16[2,2,64,256]{3,2,1,0:T(8,128)(2,1)S(1)}, bf16[2,2,64,256]{3,2,1,0:T(8,128)(2,1)S(1)}, u32[]{:S(2)}, u32[]{:S(2)}) collective-permute-start(bf16[2,2,64,256]{3,2,1,0:T(8,128)(2,1)S(1)} %pad_maximum_fusion.2.b_ref), channel_id=1, source_target_pairs={{0,8},{4,12},{8,0},{12,4},{16,24},{20,28},{24,16},{28,20},{1,9},{5... | collective-permute-start | bytes 393224 | tf_op jit(solution)/shard_map/ppermute | solution.py:488
  73.6 5.2 %collective-permute-start.15 = (bf16[2,2,64,256]{3,2,1,0:T(8,128)(2,1)S(1)}, bf16[2,2,64,256]{3,2,1,0:T(8,128)(2,1)S(1)}, u32[]{:S(2)}, u32[]{:S(2)}) collective-permute-start(bf16[2,2,64,256]{3,2,1,0:T(8,128)(2,1)S(1)} %pad_maximum_fusion.1.a_ref), channel_id=1, source_target_pairs={{0,4},{4,0},{8,12},{12,8},{16,20},{20,16},{24,28},{28,24},{1,5},{5... | collective-permute-start | bytes 393224 | tf_op jit(solution)/shard_map/ppermute | solution.py:488
  82.8 1.8 %collective-permute-start.17 = (bf16[2,32,3072]{2,1,0:T(8,128)(2,1)S(1)}, bf16[2,32,3072]{2,1,0:T(8,128)(2,1)S(1)}, u32[]{:S(2)}, u32[]{:S(2)}) collective-permute-start(bf16[2,32,3072]{2,1,0:T(8,128)(2,1)S(1)} %get-tuple-element.37), channel_id=1, source_target_pairs={{0,1},{1,0},{2,3},{3,2},{4,5},{5,4},{6,7},{7,6},{8,9},{9,8},{10,11... | collective-permute-start | bytes 1179656 | tf_op jit(solution)/shard_map/ppermute | solution.py:56
  84.7 11.2 %collective-permute-start.18 = (bf16[2,32,3072]{2,1,0:T(8,128)(2,1)S(1)}, bf16[2,32,3072]{2,1,0:T(8,128)(2,1)S(1)}, u32[]{:S(2)}, u32[]{:S(2)}) collective-permute-start(bf16[2,32,3072]{2,1,0:T(8,128)(2,1)S(1)} %get-tuple-element.40), channel_id=1, source_target_pairs={{0,2},{1,3},{2,0},{3,1},{4,6},{5,7},{6,4},{7,5},{8,10},{9,11},{10,... | collective-permute-start | bytes 1179656 | tf_op jit(solution)/shard_map/ppermute | solution.py:60
  86.2 11.3 %slice-start = ((s8[12582912]{0:T(1024)(128)(4,1)}), s8[4194304]{0:T(1024)(128)(4,1)S(1)}, s32[]{:S(2)}) async-start(s8[12582912]{0:T(1024)(128)(4,1)} %bitcast.26), calls=%async_computation | async-start | bytes 8388608
  86.2 11.3 %slice-start.1 = ((s8[12582912]{0:T(1024)(128)(4,1)}), s8[4194304]{0:T(1024)(128)(4,1)S(1)}, s32[]{:S(2)}) async-start(s8[12582912]{0:T(1024)(128)(4,1)} %bitcast.26), calls=%async_computation.1 | async-start | bytes 8388608
  95.9 2.2 %slice-start.2 = ((s8[12582912]{0:T(1024)(128)(4,1)}), s8[4194304]{0:T(1024)(128)(4,1)S(1)}, s32[]{:S(2)}) async-start(s8[12582912]{0:T(1024)(128)(4,1)} %bitcast.26), calls=%async_computation.2 | async-start | bytes 8388608
  96.0 1.5 %collective-permute-start.19 = (bf16[32,3072]{1,0:T(8,128)(2,1)S(1)}, bf16[32,3072]{1,0:T(8,128)(2,1)S(1)}, u32[]{:S(2)}, u32[]{:S(2)}) collective-permute-start(bf16[32,3072]{1,0:T(8,128)(2,1)S(1)} %combined.1.mine_ref), channel_id=1, source_target_pairs={{0,1},{1,0},{2,3},{3,2},{4,5},{5,4},{6,7},{7,6},{8,9},{9,8},{10,11... | collective-permute-start | bytes 589832 | tf_op jit(solution)/shard_map/ppermute | solution.py:56

commit v4 on v3

--- a/solution.py
+++ b/solution.py
@@ -1,4 +1,5 @@
 import functools
+import math
 import jax
 import jax.numpy as jnp
 from jax import lax
@@ -11,6 +12,9 @@
 f32 = jnp.float32
 MIB = 1024 * 1024
 WAIT_FLOPS = 6 * 10**9
+CHUNKS = 3
+BACK_CHUNKS = 2
+BUFFERS = 4
 IN_VMEM = pl.BlockSpec(memory_space=pltpu.VMEM)
 IN_HBM = pl.BlockSpec(memory_space=pltpu.HBM)
 
@@ -36,12 +40,28 @@
     )
 
 
+def order(operands, in_specs, after):
+    if after is not None:
+        operands.append(after)
+        in_specs.append(pl.BlockSpec(memory_space=pl.ANY))
+
+
 def held(value):
     return pltpu.with_memory_space_constraint(value, pltpu.VMEM)
 
 
 def kept_out(value):
     return pltpu.with_memory_space_constraint(value, pltpu.HBM)
+
+
+def join_hidden(refs, left):
+    at = 0
+    for mine_ref, other_ref in zip(refs[::2], refs[1::2]):
+        _, half, width = mine_ref.shape
+        for i in range(2):
+            left[2 * i * half : (2 * i + 1) * half, at : at + width] = mine_ref[i]
+            left[(2 * i + 1) * half : (2 * i + 2) * half, at : at + width] = other_ref[i]
+        at += width
 
 
 def silu_parts(gate_pre):
@@ -238,7 +258,8 @@
     steps = width // block
     first = chunk * width
 
-    def body(normed_ref, gate_ref, up_ref, tan_ref, after_ref, keep_ref, send_ref, buffer, sems):
+    def body(normed_ref, gate_ref, up_ref, tan_ref, *rest):
+        keep_ref, send_ref, buffer, sems = rest[-4:]
         copies = [
             pltpu.make_async_copy(
                 tan_ref.at[:, pl.ds(first + j * block, block)], buffer.at[j], sems.at[j]
@@ -261,9 +282,12 @@
                 keep_ref[i, :, span] = jnp.where(upper, high, low)
                 send_ref[i, :, span] = jnp.where(upper, low, high).astype(bf16)
 
-    return pl.pallas_call(
-        body,
-        in_specs=[IN_VMEM] * 3 + [IN_HBM, pl.BlockSpec(memory_space=pl.ANY)],
+    operands = [normed, held(w_gate), held(w_up), kept_out(v_gate)]
+    in_specs = [IN_VMEM] * 3 + [IN_HBM]
+    order(operands, in_specs, after)
+    return pl.pallas_call(
+        body,
+        in_specs=in_specs,
         out_specs=[IN_VMEM] * 2,
         out_shape=[
             jax.ShapeDtypeStruct((3, half, width), f32),
@@ -276,7 +300,7 @@
         compiler_params=params(4 + 2 * depth * width // MIB),
         cost_estimate=cost(6 * count * depth * width, 6 * depth * width),
         name="gate_products",
-    )(normed, held(w_gate), held(w_up), kept_out(v_gate), after)
+    )(*operands)
 
 
 def hidden_call(chip_sum, arrived, after):
@@ -284,7 +308,8 @@
     width = shape[1]
     block = block_of(width, 512)
 
-    def body(sum_ref, arrived_ref, after_ref, mine_ref, factor_ref):
+    def body(sum_ref, arrived_ref, *rest):
+        mine_ref, factor_ref = rest[-2:]
         for j in range(width // block):
             span = slice(j * block, (j + 1) * block)
             gate_pre, up_value, tangent = [
@@ -296,9 +321,11 @@
             factor_ref[0, :, span] = up_value * slope_gate
             factor_ref[1, :, span] = up_value * curvature * tangent
 
-    return pl.pallas_call(
-        body,
-        in_specs=[IN_VMEM, IN_VMEM, pl.BlockSpec(memory_space=pl.ANY)],
+    operands, in_specs = [chip_sum, arrived], [IN_VMEM] * 2
+    order(operands, in_specs, after)
+    return pl.pallas_call(
+        body,
+        in_specs=in_specs,
         out_specs=[IN_VMEM] * 2,
         out_shape=[
             jax.ShapeDtypeStruct((2,) + shape, bf16),
@@ -307,19 +334,18 @@
         compiler_params=params(8),
         cost_estimate=cost(0, 30 * shape[0] * width),
         name="hidden_units",
-    )(chip_sum, arrived, after)
-
-
-def down_call(mine, other, w_down, v_down):
-    half, rows = mine.shape[1:]
-    count = 2 * half
-    features = w_down.shape[1]
+    )(*operands)
+
+
+def down_call(hiddens, w_down, v_down):
+    count = 2 * hiddens[0].shape[1]
+    rows, features = w_down.shape
     block = block_of(features, 512)
-
-    def body(mine_ref, other_ref, w_ref, v_ref, out_ref, left):
-        for i in range(2):
-            left[i * count : i * count + half] = mine_ref[i]
-            left[i * count + half : (i + 1) * count] = other_ref[i]
+    n = len(hiddens)
+
+    def body(*refs):
+        w_ref, v_ref, out_ref, left = refs[n:]
+        join_hidden(refs[:n], left)
         for j in range(features // block):
             span = slice(j * block, (j + 1) * block)
             both = dot(left[...], w_ref[:, span], 1, 0)
@@ -328,14 +354,14 @@
 
     return pl.pallas_call(
         body,
-        in_specs=[IN_VMEM] * 4,
+        in_specs=[IN_VMEM] * (n + 2),
         out_specs=IN_VMEM,
         out_shape=jax.ShapeDtypeStruct((2, count, features), bf16),
         scratch_shapes=[pltpu.VMEM((2 * count, rows), bf16)],
         compiler_params=params(12),
         cost_estimate=cost(6 * count * rows * features, 4 * rows * features),
         name="down_products",
-    )(mine, other, held(w_down), held(v_down))
+    )(*hiddens, held(w_down), held(v_down))
 
 
 def back_call(residuals, w_down, v_down):
@@ -369,114 +395,128 @@
     )(residuals, held(w_down), held(v_down))
 
 
-def down_score_call(mine, other, residuals, v_down):
-    half, rows = mine.shape[1:]
-    count = 2 * half
-    features = v_down.shape[1]
+def down_score_call(hiddens, residuals, v_down):
+    rows, features = v_down.shape
+    count = residuals.shape[1]
     block = block_of(rows, 512)
     steps = rows // block
-
-    def body(mine_ref, other_ref, res_ref, v_ref, out_ref, buffer, sems):
+    n = len(hiddens)
+
+    def body(*refs):
+        res_ref, v_ref, out_ref, left, right, buffer, sems = refs[n:]
+        join_hidden(refs[:n], left)
+        right[:count] = res_ref[1]
+        right[count:] = res_ref[0]
         copies = []
         for j in range(steps):
             span = slice(j * block, (j + 1) * block)
-            if j >= 2:
-                copies[j - 2].wait()
-            left = jnp.concatenate(
-                [mine_ref[1, :, span], other_ref[1, :, span], mine_ref[0, :, span], other_ref[0, :, span]],
-                axis=0,
-            )
-            hess = dot(left, res_ref[...].reshape(2 * count, features), 0, 0)
-            buffer[j % 2] = (v_ref[span, :].astype(f32) * hess).astype(bf16)
+            if j >= BUFFERS:
+                copies[j - BUFFERS].wait()
+            hess = dot(left[:, span], right[...], 0, 0)
+            buffer[j % BUFFERS] = (v_ref[span, :].astype(f32) * hess).astype(bf16)
             copies.append(
                 pltpu.make_async_copy(
-                    buffer.at[j % 2], out_ref.at[pl.ds(j * block, block)], sems.at[j % 2]
+                    buffer.at[j % BUFFERS], out_ref.at[pl.ds(j * block, block)], sems.at[j % BUFFERS]
                 )
             )
             copies[j].start()
-        for copy in copies[-2:]:
+        for copy in copies[-BUFFERS:]:
             copy.wait()
 
     return pl.pallas_call(
         body,
-        in_specs=[IN_VMEM] * 4,
+        in_specs=[IN_VMEM] * (n + 2),
         out_specs=IN_HBM,
         out_shape=jax.ShapeDtypeStruct((rows, features), bf16),
         scratch_shapes=[
-            pltpu.VMEM((2, block, features), bf16),
-            pltpu.SemaphoreType.DMA((2,)),
+            pltpu.VMEM((2 * count, rows), bf16),
+            pltpu.VMEM((2 * count, features), bf16),
+            pltpu.VMEM((BUFFERS, block, features), bf16),
+            pltpu.SemaphoreType.DMA((BUFFERS,)),
         ],
-        compiler_params=params(16),
+        compiler_params=params(20),
         cost_estimate=cost(4 * count * rows * features, 4 * rows * features),
         name="down_score",
-    )(mine, other, residuals, held(v_down))
-
-
-def combine_call(chip_sum, arrived, factors, after):
+    )(*hiddens, residuals, held(v_down))
+
+
+def combine_call(chip_sum, arrived, factors, chunk, after):
     half, width = chip_sum.shape[1:]
-    block = block_of(width, 512)
-
-    def body(sum_ref, arrived_ref, factor_ref, after_ref, out_ref):
+    part = factors[0].shape[2]
+    block = block_of(math.gcd(width, part), 512)
+    n = len(factors)
+
+    def body(sum_ref, arrived_ref, *rest):
+        factor_refs, out_ref = rest[:n], rest[-1]
         for j in range(width // block):
             span = slice(j * block, (j + 1) * block)
             back_grad, back_tangent = [
                 sum_ref[i, :, span] + arrived_ref[i, :, span].astype(f32) for i in range(2)
             ]
+            at = chunk * width + j * block
+            factor_ref, start = factor_refs[at // part], at % part
+            taken = slice(start, start + block)
             out_ref[:, span] = (
-                back_tangent * factor_ref[0, :, span] + back_grad * factor_ref[1, :, span]
+                back_tangent * factor_ref[0, :, taken] + back_grad * factor_ref[1, :, taken]
             ).astype(bf16)
 
     return pl.pallas_call(
         body,
-        in_specs=[IN_VMEM] * 3 + [pl.BlockSpec(memory_space=pl.ANY)],
+        in_specs=[IN_VMEM] * (n + 2) + [pl.BlockSpec(memory_space=pl.ANY)],
         out_specs=IN_VMEM,
         out_shape=jax.ShapeDtypeStruct((half, width), bf16),
         compiler_params=params(8),
         cost_estimate=cost(0, 22 * half * width),
         name="combined",
-    )(chip_sum, arrived, factors, kept_out(after))
-
-
-def gate_score_call(normed, mine, other, v_gate):
+    )(chip_sum, arrived, *factors, kept_out(after))
+
+
+def gate_score_call(normed, combined, v_gate):
     count, depth = normed.shape
     half = count // 2
     width = v_gate.shape[1]
-    block = block_of(width, 512)
+    part = combined[0].shape[1]
+    block = block_of(part, 512)
     steps = width // block
-
-    def body(normed_ref, mine_ref, other_ref, v_ref, out_ref, buffer, sems):
+    n = len(combined)
+
+    def body(normed_ref, *rest):
+        v_ref, out_ref, buffer, sems = rest[n:]
         upper = lax.axis_index("mp") % 2 == 1
         copies = []
         for j in range(steps):
             span = slice(j * block, (j + 1) * block)
-            if j >= 2:
-                copies[j - 2].wait()
-            low = jnp.where(upper, other_ref[:, span], mine_ref[:, span])
-            high = jnp.where(upper, mine_ref[:, span], other_ref[:, span])
+            at = j * block // part
+            taken = slice(j * block % part, j * block % part + block)
+            mine, other = rest[2 * at][:, taken], rest[2 * at + 1][:, taken]
+            if j >= BUFFERS:
+                copies[j - BUFFERS].wait()
+            low = jnp.where(upper, other, mine)
+            high = jnp.where(upper, mine, other)
             hess = dot(normed_ref[...], jnp.concatenate([low, high], axis=0), 0, 0)
-            buffer[j % 2] = (v_ref[:, span].astype(f32) * hess).astype(bf16)
+            buffer[j % BUFFERS] = (v_ref[:, span].astype(f32) * hess).astype(bf16)
             copies.append(
                 pltpu.make_async_copy(
-                    buffer.at[j % 2], out_ref.at[:, pl.ds(j * block, block)], sems.at[j % 2]
+                    buffer.at[j % BUFFERS], out_ref.at[:, pl.ds(j * block, block)], sems.at[j % BUFFERS]
                 )
             )
             copies[j].start()
-        for copy in copies[-2:]:
+        for copy in copies[-BUFFERS:]:
             copy.wait()
 
     return pl.pallas_call(
         body,
-        in_specs=[IN_VMEM] * 4,
+        in_specs=[IN_VMEM] * (n + 2),
         out_specs=IN_HBM,
         out_shape=jax.ShapeDtypeStruct((depth, width), bf16),
         scratch_shapes=[
-            pltpu.VMEM((2, depth, block), bf16),
-            pltpu.SemaphoreType.DMA((2,)),
+            pltpu.VMEM((BUFFERS, depth, block), bf16),
+            pltpu.SemaphoreType.DMA((BUFFERS,)),
         ],
-        compiler_params=params(16),
+        compiler_params=params(20),
         cost_estimate=cost(2 * count * depth * width, 4 * depth * width),
         name="gate_score",
-    )(normed, mine, other, v_gate)
+    )(normed, *combined, held(v_gate))
 
 
 def bits():
@@ -488,17 +528,16 @@
     return lax.ppermute(value, "dp", [(i, i ^ bit) for i in range(8)])
 
 
-def piece_call(mine, other, w_down, v_down, away, dtype):
-    half, rows = mine.shape[1:]
-    count = 2 * half
-    features = w_down.shape[1]
+def piece_call(hiddens, w_down, v_down, away, dtype):
+    count = 2 * hiddens[0].shape[1]
+    rows, features = w_down.shape
+    n = len(hiddens)
     piece = features // 8
 
-    def body(mine_ref, other_ref, w_ref, v_ref, a_ref, b_ref, left):
+    def body(*refs):
+        w_ref, v_ref, a_ref, b_ref, left = refs[n:]
         y, z = bits()
-        for i in range(2):
-            left[i * count : i * count + half] = mine_ref[i]
-            left[i * count + half : (i + 1) * count] = other_ref[i]
+        join_hidden(refs[:n], left)
         for out_ref, base, outer, inner in ((a_ref, 0, y, z), (b_ref, 4, z, y)):
             group = 1 - outer if away else outer
             for k, low in enumerate((1 - inner, inner)):
@@ -511,14 +550,14 @@
     shape = jax.ShapeDtypeStruct((2, 2, count, piece), dtype)
     return pl.pallas_call(
         body,
-        in_specs=[IN_VMEM] * 4,
+        in_specs=[IN_VMEM] * (n + 2),
         out_specs=[IN_VMEM] * 2,
         out_shape=[shape, shape],
         scratch_shapes=[pltpu.VMEM((2 * count, rows), bf16)],
         compiler_params=params(8),
         cost_estimate=cost(3 * count * rows * features, 2 * rows * features),
         name="pieces_away" if away else "pieces_home",
-    )(mine, other, held(w_down), held(v_down))
+    )(*hiddens, held(w_down), held(v_down))
 
 
 def residual_call(sums, arrived, target):
@@ -588,48 +627,55 @@
     )(a_pieces, b_pieces, held(w_down), held(v_down))
 
 
-def back_second_call(a_pieces, b_pieces, a_far, b_far, first_part, w_down, v_down):
+def back_second_call(a_pieces, b_pieces, a_far, b_far, first_part, w_down, v_down, chunk, chunks):
     count, piece = a_pieces.shape[2:]
     half = count // 2
-    rows, features = w_down.shape
+    features = w_down.shape[1]
+    rows = w_down.shape[0] // chunks
     block = block_of(rows, 512)
-
-    def body(a_ref, b_ref, a_far_ref, b_far_ref, part_ref, w_ref, v_ref, keep_ref, send_ref, res_ref, right):
+    from_row = chunk * rows
+
+    def body(a_ref, b_ref, a_far_ref, b_far_ref, part_ref, w_ref, v_ref, keep_ref, send_ref, *rest):
+        right = rest[-1]
         y, z = bits()
         for i, (ref, far_ref, outer, inner) in enumerate(((a_ref, a_far_ref, y, z), (b_ref, b_far_ref, z, y))):
             for k, low in enumerate((inner, 1 - inner)):
                 first = pl.multiple_of((2 * i + low) * piece, piece)
                 right[pl.ds(first, piece), :] = far_ref[k].reshape(2 * count, piece).T
-                near = pl.multiple_of((4 * i + 2 * outer + low) * piece, piece)
-                far = pl.multiple_of((4 * i + 2 * (1 - outer) + low) * piece, piece)
-                for t in range(2):
-                    res_ref[t, :, pl.ds(near, piece)] = ref[k, t]
-                    res_ref[t, :, pl.ds(far, piece)] = far_ref[k, t]
+                if chunk == 0:
+                    near = pl.multiple_of((4 * i + 2 * outer + low) * piece, piece)
+                    far = pl.multiple_of((4 * i + 2 * (1 - outer) + low) * piece, piece)
+                    for t in range(2):
+                        rest[0][t, :, pl.ds(near, piece)] = ref[k, t]
+                        rest[0][t, :, pl.ds(far, piece)] = far_ref[k, t]
         starts = [
             pl.multiple_of(2 * piece * (1 - y), 2 * piece),
             pl.multiple_of(2 * piece * (3 - z), 2 * piece),
         ]
         for j in range(rows // block):
             span = slice(j * block, (j + 1) * block)
-            total = part_ref[span]
+            taken = slice(from_row + j * block, from_row + (j + 1) * block)
+            total = part_ref[taken]
             tangent = jnp.zeros((block, count), f32)
             for i, first in enumerate(starts):
                 part = right[2 * i * piece : 2 * (i + 1) * piece]
-                total += dot(w_ref[span, pl.ds(first, 2 * piece)], part, 1, 0)
-                tangent += dot(v_ref[span, pl.ds(first, 2 * piece)], part[:, :count], 1, 0)
+                total += dot(w_ref[taken, pl.ds(first, 2 * piece)], part, 1, 0)
+                tangent += dot(v_ref[taken, pl.ds(first, 2 * piece)], part[:, :count], 1, 0)
             for i, value in enumerate((total[:, :count].T, (total[:, count:] + tangent).T)):
                 keep_ref[i, :, span] = value[:half]
                 send_ref[i, :, span] = value[half:].astype(bf16)
 
+    out_shape = [
+        jax.ShapeDtypeStruct((2, half, rows), f32),
+        jax.ShapeDtypeStruct((2, half, rows), bf16),
+    ]
+    if chunk == 0:
+        out_shape.append(jax.ShapeDtypeStruct((2, count, features), bf16))
     return pl.pallas_call(
         body,
         in_specs=[IN_VMEM] * 7,
-        out_specs=[IN_VMEM] * 3,
-        out_shape=[
-            jax.ShapeDtypeStruct((2, half, rows), f32),
-            jax.ShapeDtypeStruct((2, half, rows), bf16),
-            jax.ShapeDtypeStruct((2, count, features), bf16),
-        ],
+        out_specs=[IN_VMEM] * len(out_shape),
+        out_shape=out_shape,
         scratch_shapes=[pltpu.VMEM((4 * piece, 2 * count), bf16)],
         compiler_params=params(8),
         cost_estimate=cost(12 * count * rows * piece, 8 * rows * piece),
@@ -637,10 +683,10 @@
     )(a_pieces, b_pieces, a_far, b_far, first_part, held(w_down), held(v_down))
 
 
-def middle_tree(mine, other, target, w_down, v_down):
-    a_send, b_send = piece_call(mine, other, w_down, v_down, True, bf16)
+def middle_tree(hiddens, target, w_down, v_down, chunks):
+    a_send, b_send = piece_call(hiddens, w_down, v_down, True, bf16)
     a_recv, b_recv = swap_dp(a_send, 1), swap_dp(b_send, 2)
-    a_home, b_home = piece_call(mine, other, w_down, v_down, False, f32)
+    a_home, b_home = piece_call(hiddens, w_down, v_down, False, f32)
     a_sum = a_home + a_recv.astype(f32)
     b_sum = b_home + b_recv.astype(f32)
     a_recv, b_recv = swap_dp(a_sum[0].astype(bf16), 2), swap_dp(b_sum[0].astype(bf16), 1)
@@ -651,15 +697,19 @@
     b_pieces = jnp.stack([b_res, swap_dp(b_res, 1)])
     a_far, b_far = swap_dp(a_pieces, 1), swap_dp(b_pieces, 2)
     first_part = back_first_call(a_pieces, b_pieces, w_down, v_down)
-    return back_second_call(a_pieces, b_pieces, a_far, b_far, first_part, w_down, v_down)
-
-
-def middle_direct(dp, mine, other, target, w_down, v_down):
-    half = mine.shape[1]
+    parts = [
+        back_second_call(a_pieces, b_pieces, a_far, b_far, first_part, w_down, v_down, chunk, chunks)
+        for chunk in range(chunks)
+    ]
+    return [chip_sum_of(part[:2]) for part in parts], parts[0][2]
+
+
+def middle_direct(dp, hiddens, target, w_down, v_down):
+    half = hiddens[0].shape[1]
     count = 2 * half
     own = count // dp
     features = w_down.shape[1]
-    out_parts = down_call(mine, other, w_down, v_down)
+    out_parts = down_call(hiddens, w_down, v_down)
     pieces = out_parts.reshape(2, dp, own, features).swapaxes(0, 1)
     arrived = lax.all_to_all(pieces, "dp", 0, 0, tiled=True).astype(f32)
     totals = jnp.sum(arrived, axis=0)
@@ -673,36 +723,53 @@
         jnp.broadcast_to(rows[None], (dp,) + rows.shape), "dp", 0, 0, tiled=True
     )
     residuals = spread.swapaxes(0, 1).reshape(2, count, features)
-    keep, send = back_call(residuals, w_down, v_down)
-    return keep, send, residuals
+    return [chip_sum_of(back_call(residuals, w_down, v_down))], residuals
+
+
+def chip_sum_of(product):
+    keep, send = product
+    chip_sum = keep + swap_core(send).astype(f32)
+    return chip_sum, chip_sum.astype(bf16)
 
 
 def per_device(dp, tokens, norm_gain, target, w_gate, w_up, v_gate, w_down, v_down):
     own = tokens.shape[0]
     count = own * dp
     col_width = w_gate.shape[0]
+    chunks, back_chunks = (CHUNKS, BACK_CHUNKS) if dp == 8 else (1, 1)
     if dp == 8:
         block = norm_call(tokens, norm_gain, 1, col_width)
         normed = gather_tree(block).reshape(count, col_width)
-        keep, send = gate_held_call(normed, w_gate, w_up, v_gate, 0, 1, normed)
+        sums = []
+        for chunk in range(chunks):
+            after = sums[chunk - 2][1] if chunk > 1 else None
+            products = gate_held_call(normed, w_gate, w_up, v_gate, chunk, chunks, after)
+            sums.append(chip_sum_of(products))
     else:
         copies = norm_call(tokens, norm_gain, dp, col_width)
         normed = lax.all_to_all(copies, "dp", 0, 0, tiled=True).reshape(count, col_width)
-        keep, send = gate_call(normed, w_gate, w_up, v_gate, 0, 1)
-    chip_sum = keep + swap_core(send).astype(f32)
-    chip_send = chip_sum.astype(bf16)
-    w_down, v_down = load_call([w_down, v_down], chip_send, "load_down")
-    mine, factors = hidden_call(chip_sum, swap_chip(chip_send), held(v_down))
-    other = swap_core(mine)
+        sums = [chip_sum_of(gate_call(normed, w_gate, w_up, v_gate, 0, 1))]
+    arrived = [swap_chip(send) for _, send in sums]
+    waits = [None] * chunks
     if dp == 8:
-        keep, send, residuals = middle_tree(mine, other, target, w_down, v_down)
+        w_down, v_down = load_call([w_down, v_down], sums[-1][1], "load_down")
+        waits = [w_down] * chunks
+    hiddens, factors = [], []
+    for chunk, ((chip_sum, _), came, wait) in enumerate(zip(sums, arrived, waits)):
+        mine, factor = hidden_call(chip_sum, came, None if wait is None else held(wait))
+        hiddens += [mine, swap_core(mine)]
+        factors.append(factor)
+    if dp == 8:
+        sums, residuals = middle_tree(hiddens, target, w_down, v_down, back_chunks)
     else:
-        keep, send, residuals = middle_direct(dp, mine, other, target, w_down, v_down)
-    chip_sum = keep + swap_core(send).astype(f32)
-    arrived = swap_chip(chip_sum.astype(bf16))
-    down_score = down_score_call(mine, other, residuals, v_down)
-    combined = combine_call(chip_sum, arrived, factors, down_score)
-    gate_score = gate_score_call(normed, combined, swap_core(combined), v_gate)
+        sums, residuals = middle_direct(dp, hiddens, target, w_down, v_down)
+    arrived = [swap_chip(send) for _, send in sums]
+    down_score = down_score_call(hiddens, residuals, v_down)
+    combined = []
+    for chunk, ((chip_sum, _), came) in enumerate(zip(sums, arrived)):
+        mine = combine_call(chip_sum, came, factors, chunk, down_score)
+        combined += [mine, swap_core(mine)]
+    gate_score = gate_score_call(normed, combined, v_gate)
     return (gate_score, down_score)
 
 

time: 105 us -> 100 us (0.952)
  waiting for transfers between devices: 37.8 us -> 29.3 us
  starting transfers between devices: 21 us -> 25.2 us
  Pallas kernels: 44.3 us -> 43.1 us
    ppermute x2 -> x5, waiting for transfers between devices: 8.25 us -> 3.41 us  [swap_chip(): return lax.ppermute(value, 'mp', [(i, i ^ 2) for i in range(4)])]
    ppermute x4 -> x10, waiting for transfers between devices: 6.84 us -> 3.38 us  [swap_core(): return lax.ppermute(value, 'mp', [(i, i ^ 1) for i in range(4)])]
    ppermute x2 -> x5, starting transfers between devices: 3.11 us -> 5.22 us  [swap_chip(): return lax.ppermute(value, 'mp', [(i, i ^ 2) for i in range(4)])]
    ppermute x4 -> x10, starting transfers between devices: 0.28 us -> 2.16 us  [swap_core(): return lax.ppermute(value, 'mp', [(i, i ^ 1) for i in range(4)])]
    pallas_call x8 -> x14, Pallas kernels: 31 us -> 29.8 us  [the longest x3 9.7 us: gate_held_call(): pl.pallas_call(body, in_specs=in_specs, out_specs=[IN_VMEM] * 2, out_shap...]
  transfers between devices with their start and end apart: 20 -> 29, of which waited for: 16 -> 18; matrix products, arithmetic and copies ran while one was open for 0% -> 0% of each run, Pallas kernels for 20% -> 29%
where the time goes in v4:
time: 100 us
  Pallas kernels  43.1 us (43%)
  waiting for transfers between devices  29.3 us (29%)
  starting transfers between devices  25.2 us (25%)
  between operations  1.22 us (1%)
    ppermute x14, waiting for transfers between devices, swap_dp(): return lax.ppermute(value, 'dp', [(i, i ^ bit) for i in range(8)])  22.5 us
    ppermute x14, starting transfers between devices, swap_dp(): return lax.ppermute(value, 'dp', [(i, i ^ bit) for i in range(8)])  17.8 us
    pallas_call x3, Pallas kernels, gate_held_call(): pl.pallas_call(body, in_specs=in_specs, out_specs=[IN_VMEM] * 2, out_shap...  9.7 us
    pallas_call x1, Pallas kernels, load_call(): pl.pallas_call(body, in_specs=[IN_HBM] * n + [pl.BlockSpec(memory_space=p...  8.3 us
    pallas_call x1, Pallas kernels, down_score_call(): pl.pallas_call(body, in_specs=[IN_VMEM] * (n + 2), out_specs=IN_HBM, out_...  5.36 us
    pallas_call x1, Pallas kernels, gate_score_call(): pl.pallas_call(body, in_specs=[IN_VMEM] * (n + 2), out_specs=IN_HBM, out_...  5.36 us
    ppermute x5, starting transfers between devices, swap_chip(): return lax.ppermute(value, 'mp', [(i, i ^ 2) for i in range(4)])  5.22 us
    pallas_call x2, Pallas kernels, back_second_call(): pl.pallas_call(body, in_specs=[IN_VMEM] * 7, out_specs=[IN_VMEM] * len(ou...  4.62 us
  transfers between devices with their start and end apart: 29, of which 18 were waited for; matrix products, arithmetic and copies ran while one was open for 0% of the time, Pallas kernels for 29%

profile of v4, /device:TPU:0, one launch (start us, length us, event | category | flops | bytes accessed | tf_op | source)
XLA Modules:
  0.0 100.0 jit_solution(9625017889898458954)
XLA Ops:
  0.6 1.1 %norm_rows.1.refs_0_ = bf16[1,8,2048]{2,1,0:T(8,128)(2,1)S(1)} custom-call(bf16[8,8192]{1,0:T(8,128)(2,1)} %tokens_ref.1, f32[1,8192]{1,0:T(1,128)} %bitcast.40), custom_call_target="tpu_custom_call" | custom-call | flops 6000000000 | bytes 262144 | tf_op jit(solution)/shard_map/norm_rows/pallas_call | solution.py:137
  1.8 4.1 %collective-permute-start = (bf16[1,8,2048]{2,1,0:T(8,128)(2,1)S(1)}, bf16[1,8,2048]{2,1,0:T(8,128)(2,1)S(1)}, u32[]{:S(2)}, u32[]{:S(2)}) collective-permute-start(bf16[1,8,2048]{2,1,0:T(8,128)(2,1)S(1)} %norm_rows.1.refs_0_), channel_id=1, source_target_pairs={{0,16},{4,20},{8,24},{12,28},{16,0},{20,4},{24,8},{28,12},{1,17},{... | collective-permute-start | bytes 98312 | tf_op jit(solution)/shard_map/ppermute | solution.py:528
  5.9 2.2 %collective-permute-done.refs_1_ = bf16[1,8,2048]{2,1,0:T(8,128)(2,1)S(1)} collective-permute-done((bf16[1,8,2048]{2,1,0:T(8,128)(2,1)S(1)}, bf16[1,8,2048]{2,1,0:T(8,128)(2,1)S(1)}, u32[]{:S(2)}, u32[]{:S(2)}) %collective-permute-start) | collective-permute-done | bytes 32800 | tf_op jit(solution)/shard_map/ppermute | solution.py:528
  8.1 1.6 %collective-permute-start.1 = (bf16[2,8,1024]{2,1,0:T(8,128)(2,1)S(1)}, bf16[2,8,1024]{2,1,0:T(8,128)(2,1)S(1)}, u32[]{:S(2)}, u32[]{:S(2)}) collective-permute-start(bf16[2,8,1024]{2,1,0:T(8,128)(2,1)S(1)} %get-tuple-element.31.refs_0_), channel_id=1, source_target_pairs={{0,8},{4,12},{8,0},{12,4},{16,24},{20,28},{24,16},{28,20},{1,9},{5... | collective-permute-start | bytes 98312 | tf_op jit(solution)/shard_map/ppermute | solution.py:528
  9.8 1.5 %collective-permute-start.2 = (bf16[2,8,1024]{2,1,0:T(8,128)(2,1)S(1)}, bf16[2,8,1024]{2,1,0:T(8,128)(2,1)S(1)}, u32[]{:S(2)}, u32[]{:S(2)}) collective-permute-start(bf16[2,8,1024]{2,1,0:T(8,128)(2,1)S(1)} %get-tuple-element.32.refs_1_), channel_id=1, source_target_pairs={{0,4},{4,0},{8,12},{12,8},{16,20},{20,16},{24,28},{28,24},{1,5},{5... | collective-permute-start | bytes 98312 | tf_op jit(solution)/shard_map/ppermute | solution.py:528
  11.3 0.8 collective-permute-done.1.refs_2_
  12.1 1.6 %collective-permute-done.2.refs_3_ = bf16[2,8,1024]{2,1,0:T(8,128)(2,1)S(1)} collective-permute-done((bf16[2,8,1024]{2,1,0:T(8,128)(2,1)S(1)}, bf16[2,8,1024]{2,1,0:T(8,128)(2,1)S(1)}, u32[]{:S(2)}, u32[]{:S(2)}) %collective-permute-start.2) | collective-permute-done | bytes 32800 | tf_op jit(solution)/shard_map/ppermute | solution.py:528
  13.7 1.6 %collective-permute-start.3 = (bf16[4,8,1024]{2,1,0:T(8,128)(2,1)S(1)}, bf16[4,8,1024]{2,1,0:T(8,128)(2,1)S(1)}, u32[]{:S(2)}, u32[]{:S(2)}) collective-permute-start(bf16[4,8,1024]{2,1,0:T(8,128)(2,1)S(1)} %get-tuple-element.33.a0), channel_id=1, source_target_pairs={{0,4},{4,0},{8,12},{12,8},{16,20},{20,16},{24,28},{28,24},{1,5},{5... | collective-permute-start | bytes 196616 | tf_op jit(solution)/shard_map/ppermute | solution.py:528
  15.3 0.9 collective-permute-start.4
  16.2 1.8 %collective-permute-done.3.a1 = bf16[4,8,1024]{2,1,0:T(8,128)(2,1)S(1)} collective-permute-done((bf16[4,8,1024]{2,1,0:T(8,128)(2,1)S(1)}, bf16[4,8,1024]{2,1,0:T(8,128)(2,1)S(1)}, u32[]{:S(2)}, u32[]{:S(2)}) %collective-permute-start.3) | collective-permute-done | bytes 65568 | tf_op jit(solution)/shard_map/ppermute | solution.py:528
  18.0 1.6 %collective-permute-done.4.b1 = bf16[4,8,1024]{2,1,0:T(8,128)(2,1)S(1)} collective-permute-done((bf16[4,8,1024]{2,1,0:T(8,128)(2,1)S(1)}, bf16[4,8,1024]{2,1,0:T(8,128)(2,1)S(1)}, u32[]{:S(2)}, u32[]{:S(2)}) %collective-permute-start.4) | collective-permute-done | bytes 65568 | tf_op jit(solution)/shard_map/ppermute | solution.py:528
  19.7 3.2 %gate_products.3 = (f32[3,32,1024]{2,1,0:T(8,128)S(1)}, bf16[3,32,1024]{2,1,0:T(8,128)(2,1)S(1)}) custom-call(bf16[64,2048]{1,0:T(8,128)(2,1)S(1)} %bitcast.32, bf16[2048,3072]{1,0:T(8,128)(2,1)S(1)} %bitcast.29, bf16[2048,3072]{1,0:T(8,128)(2,1)S(1)} %bitcast.31, bf16[2048,3072]{1,0:T(8,128)(2,1)} %rest_4_.1), custom_call_target="tpu_custom_call" | custom-call | flops 805306368 | bytes 12582912 | tf_op jit(solution)/shard_map/gate_products/pallas_call | solution.py:288
  22.9 0.1 collective-permute-start.5
  23.0 3.2 %gate_products.5 = (f32[3,32,1024]{2,1,0:T(8,128)S(1)}, bf16[3,32,1024]{2,1,0:T(8,128)(2,1)S(1)}) custom-call(bf16[64,2048]{1,0:T(8,128)(2,1)S(1)} %bitcast.33, bf16[2048,3072]{1,0:T(8,128)(2,1)S(1)} %bitcast.29, bf16[2048,3072]{1,0:T(8,128)(2,1)S(1)} %bitcast.31, bf16[2048,3072]{1,0:T(8,128)(2,1)} %rest_4_.1), custom_call_target="tpu_custom_call" | custom-call | flops 805306368 | bytes 12582912 | tf_op jit(solution)/shard_map/gate_products/pallas_call | solution.py:288
  26.3 0.6 collective-permute-start.9
  26.9 1.6 %collective-permute-start.6 = (bf16[3,32,1024]{2,1,0:T(8,128)(2,1)S(1)}, bf16[3,32,1024]{2,1,0:T(8,128)(2,1)S(1)}, u32[]{:S(2)}, u32[]{:S(2)}) collective-permute-start(bf16[3,32,1024]{2,1,0:T(8,128)(2,1)S(1)} %get-tuple-element.68.rest_0_), channel_id=1, source_target_pairs={{0,2},{1,3},{2,0},{3,1},{4,6},{5,7},{6,4},{7,5},{8,10},{9,11},{10,... | collective-permute-start | bytes 589832 | tf_op jit(solution)/shard_map/ppermute | solution.py:80
  28.4 3.2 %gate_products.4 = (f32[3,32,1024]{2,1,0:T(8,128)S(1)}, bf16[3,32,1024]{2,1,0:T(8,128)(2,1)S(1)}) custom-call(bf16[64,2048]{1,0:T(8,128)(2,1)S(1)} %bitcast.34, bf16[2048,3072]{1,0:T(8,128)(2,1)S(1)} %bitcast.29, bf16[2048,3072]{1,0:T(8,128)(2,1)S(1)} %bitcast.31, bf16[2048,3072]{1,0:T(8,128)(2,1)} %rest_4_.1, bf16[3,32,1024]{2,1,0:T(8,128)(2,1)S(1)} %get-tuple-element.68.rest_0_), custom_call_target="tpu_custom_call" | custom-call | flops 805306368 | bytes 12582912 | tf_op jit(solution)/shard_map/gate_products/pallas_call | solution.py:288
  31.7 0.1 collective-permute-start.7
  31.8 0.1 fusion.9
  31.8 0.6 collective-permute-start.10
  32.4 0.8 collective-permute-done.7
  33.2 0.8 collective-permute-start.12
  34.0 8.3 %load_down.1 = (bf16[3072,2048]{1,0:T(8,128)(2,1)S(1)}, bf16[3072,2048]{1,0:T(8,128)(2,1)S(1)}) custom-call(bf16[3072,2048]{1,0:T(8,128)(2,1)} %refs_0_.1, bf16[3072,2048]{1,0:T(8,128)(2,1)} %refs_1_.1, bf16[3,32,1024]{2,1,0:T(8,128)(2,1)S(1)} %get-tuple-element.66.refs_2_), custom_call_target="tpu_custom_call" | custom-call | bytes 50331648 | tf_op jit(solution)/shard_map/load_down/pallas_call | solution.py:105
  42.4 0.1 hidden_units.4
  42.5 0.1 collective-permute-start.11
  42.6 0.1 hidden_units.3
  42.7 0.6 collective-permute-start.8
  43.3 0.1 collective-permute-done.12.arrived_ref
  43.4 0.1 hidden_units.5
  43.5 0.1 collective-permute-start.13
  43.6 0.3 collective-permute-done.11.refs_3_
  43.9 0.3 collective-permute-done.8.refs_1_
  44.3 0.7 collective-permute-done.13.refs_5_
  45.0 2.1 %pieces_away.1 = (bf16[2,2,64,256]{3,2,1,0:T(8,128)(2,1)S(1)}, bf16[2,2,64,256]{3,2,1,0:T(8,128)(2,1)S(1)}) custom-call(bf16[2,32,1024]{2,1,0:T(8,128)(2,1)S(1)} %get-tuple-element.40.refs_0_, bf16[2,32,1024]{2,1,0:T(8,128)(2,1)S(1)} %collective-permute-done.8.refs_1_, bf16[2,32,1024]{2,1,0:T(8,128)(2,1)S(1)} %get-tuple-element.43.refs_2_, ...), custom_call_target="tpu_custom_call" | custom-call | flops 1207959552 | bytes 12582912 | tf_op jit(solution)/shard_map/pieces_away/pallas_call | solution.py:551
  47.1 0.6 collective-permute-start.14
  47.7 0.9 collective-permute-start.16
  48.6 2.1 %pieces_home.1 = (f32[2,2,64,256]{3,2,1,0:T(8,128)S(1)}, f32[2,2,64,256]{3,2,1,0:T(8,128)S(1)}) custom-call(bf16[2,32,1024]{2,1,0:T(8,128)(2,1)S(1)} %get-tuple-element.40.refs_0_, bf16[2,32,1024]{2,1,0:T(8,128)(2,1)S(1)} %collective-permute-done.8.refs_1_, bf16[2,32,1024]{2,1,0:T(8,128)(2,1)S(1)} %get-tuple-element.43.refs_2_, ...), custom_call_target="tpu_custom_call" | custom-call | flops 1207959552 | bytes 12582912 | tf_op jit(solution)/shard_map/pieces_home/pallas_call | solution.py:551
  50.7 2.0 %collective-permute-done.14 = bf16[2,2,64,256]{3,2,1,0:T(8,128)(2,1)S(1)} collective-permute-done((bf16[2,2,64,256]{3,2,1,0:T(8,128)(2,1)S(1)}, bf16[2,2,64,256]{3,2,1,0:T(8,128)(2,1)S(1)}, u32[]{:S(2)}, u32[]{:S(2)}) %collective-permute-start.14) | collective-permute-done | bytes 131104 | tf_op jit(solution)/shard_map/ppermute | solution.py:528
  52.8 1.0 %collective-permute-start.15 = (bf16[2,64,256]{2,1,0:T(8,128)(2,1)S(1)}, bf16[2,64,256]{2,1,0:T(8,128)(2,1)S(1)}, u32[]{:S(2)}, u32[]{:S(2)}) collective-permute-start(bf16[2,64,256]{2,1,0:T(8,128)(2,1)S(1)} %fusion.4), channel_id=1, source_target_pairs={{0,8},{4,12},{8,0},{12,4},{16,24},{20,28},{24,16},{28,20},{1,9},{5... | collective-permute-start | bytes 196616 | tf_op jit(solution)/shard_map/ppermute | solution.py:528
  53.8 0.8 collective-permute-start.17
  54.6 2.5 %collective-permute-done.15 = bf16[2,64,256]{2,1,0:T(8,128)(2,1)S(1)} collective-permute-done((bf16[2,64,256]{2,1,0:T(8,128)(2,1)S(1)}, bf16[2,64,256]{2,1,0:T(8,128)(2,1)S(1)}, u32[]{:S(2)}, u32[]{:S(2)}) %collective-permute-start.15) | collective-permute-done | bytes 65568 | tf_op jit(solution)/shard_map/ppermute | solution.py:528
  57.1 1.0 %collective-permute-done.17 = bf16[2,64,256]{2,1,0:T(8,128)(2,1)S(1)} collective-permute-done((bf16[2,64,256]{2,1,0:T(8,128)(2,1)S(1)}, bf16[2,64,256]{2,1,0:T(8,128)(2,1)S(1)}, u32[]{:S(2)}, u32[]{:S(2)}) %collective-permute-start.17) | collective-permute-done | bytes 65568 | tf_op jit(solution)/shard_map/ppermute | solution.py:528
  58.2 2.2 %collective-permute-start.18 = (bf16[2,2,64,256]{3,2,1,0:T(8,128)(2,1)S(1)}, bf16[2,2,64,256]{3,2,1,0:T(8,128)(2,1)S(1)}, u32[]{:S(2)}, u32[]{:S(2)}) collective-permute-start(bf16[2,2,64,256]{3,2,1,0:T(8,128)(2,1)S(1)} %fusion.6), channel_id=1, source_target_pairs={{0,16},{4,20},{8,24},{12,28},{16,0},{20,4},{24,8},{28,12},{1,17},{... | collective-permute-start | bytes 393224 | tf_op jit(solution)/shard_map/ppermute | solution.py:528
  60.4 5.2 %collective-permute-done.18.arrived_ref = bf16[2,2,64,256]{3,2,1,0:T(8,128)(2,1)S(1)} collective-permute-done((bf16[2,2,64,256]{3,2,1,0:T(8,128)(2,1)S(1)}, bf16[2,2,64,256]{3,2,1,0:T(8,128)(2,1)S(1)}, u32[]{:S(2)}, u32[]{:S(2)}) %collective-permute-start.18) | collective-permute-done | bytes 131104 | tf_op jit(solution)/shard_map/ppermute | solution.py:528
  65.6 0.8 collective-permute-start.20
  66.3 0.4 collective-permute-start.19
  66.7 3.8 %collective-permute-done.20 = bf16[2,64,256]{2,1,0:T(8,128)(2,1)S(1)} collective-permute-done((bf16[2,64,256]{2,1,0:T(8,128)(2,1)S(1)}, bf16[2,64,256]{2,1,0:T(8,128)(2,1)S(1)}, u32[]{:S(2)}, u32[]{:S(2)}) %collective-permute-start.20) | collective-permute-done | bytes 65568 | tf_op jit(solution)/shard_map/ppermute | solution.py:528
  70.5 0.1 collective-permute-start.22
  70.7 1.4 %collective-permute-start.21 = (bf16[2,2,64,256]{3,2,1,0:T(8,128)(2,1)S(1)}, bf16[2,2,64,256]{3,2,1,0:T(8,128)(2,1)S(1)}, u32[]{:S(2)}, u32[]{:S(2)}) collective-permute-start(bf16[2,2,64,256]{3,2,1,0:T(8,128)(2,1)S(1)} %pad_maximum_fusion.1.a_ref), channel_id=1, source_target_pairs={{0,4},{4,0},{8,12},{12,8},{16,20},{20,16},{24,28},{28,24},{1,5},{5... | collective-permute-start | bytes 393224 | tf_op jit(solution)/shard_map/ppermute | solution.py:528
  72.0 3.8 %back_first.1.part_ref = f32[3072,128]{1,0:T(8,128)S(1)} custom-call(bf16[2,2,64,256]{3,2,1,0:T(8,128)(2,1)S(1)} %pad_maximum_fusion.1.a_ref, bf16[2,2,64,256]{3,2,1,0:T(8,128)(2,1)S(1)} %pad_maximum_fusion.2.b_ref, bf16[3072,2048]{1,0:T(8,128)(2,1)S(1)} %get-tuple-element.39.rest_0_.refs_6_.w_ref, bf16[3072,2048]{1,0:T(8,128)(2,1)S(1)} %get-tuple-element.45.refs_7_.v_ref), custom_call_target="tpu_custom_call" | custom-call | flops 603979776 | bytes 6291456 | tf_op jit(solution)/shard_map/back_first/pallas_call | solution.py:618
  75.8 2.3 %back_second.3 = (f32[2,32,1536]{2,1,0:T(8,128)S(1)}, bf16[2,32,1536]{2,1,0:T(8,128)(2,1)S(1)}) custom-call(bf16[2,2,64,256]{3,2,1,0:T(8,128)(2,1)S(1)} %pad_maximum_fusion.1.a_ref, bf16[2,2,64,256]{3,2,1,0:T(8,128)(2,1)S(1)} %pad_maximum_fusion.2.b_ref, bf16[2,2,64,256]{3,2,1,0:T(8,128)(2,1)S(1)} %collective-permute-done.21.a_far_ref, ...), custom_call_target="tpu_custom_call" | custom-call | flops 301989888 | bytes 3145728 | tf_op jit(solution)/shard_map/back_second/pallas_call | solution.py:674
  78.1 0.1 collective-permute-start.26
  78.2 2.3 %back_second.2 = (f32[2,32,1536]{2,1,0:T(8,128)S(1)}, bf16[2,32,1536]{2,1,0:T(8,128)(2,1)S(1)}, bf16[2,64,2048]{2,1,0:T(8,128)(2,1)S(1)}) custom-call(bf16[2,2,64,256]{3,2,1,0:T(8,128)(2,1)S(1)} %pad_maximum_fusion.1.a_ref, bf16[2,2,64,256]{3,2,1,0:T(8,128)(2,1)S(1)} %pad_maximum_fusion.2.b_ref, ...), custom_call_target="tpu_custom_call" | custom-call | flops 301989888 | bytes 3145728 | tf_op jit(solution)/shard_map/back_second/pallas_call | solution.py:674
  80.5 0.6 collective-permute-start.23
  81.1 1.2 %collective-permute-start.27 = (bf16[2,32,1536]{2,1,0:T(8,128)(2,1)S(1)}, bf16[2,32,1536]{2,1,0:T(8,128)(2,1)S(1)}, u32[]{:S(2)}, u32[]{:S(2)}) collective-permute-start(bf16[2,32,1536]{2,1,0:T(8,128)(2,1)S(1)} %get-tuple-element.60), channel_id=1, source_target_pairs={{0,2},{1,3},{2,0},{3,1},{4,6},{5,7},{6,4},{7,5},{8,10},{9,11},{10,... | collective-permute-start | bytes 589832 | tf_op jit(solution)/shard_map/ppermute | solution.py:80
  82.4 1.0 %collective-permute-start.24 = (bf16[2,32,1536]{2,1,0:T(8,128)(2,1)S(1)}, bf16[2,32,1536]{2,1,0:T(8,128)(2,1)S(1)}, u32[]{:S(2)}, u32[]{:S(2)}) collective-permute-start(bf16[2,32,1536]{2,1,0:T(8,128)(2,1)S(1)} %get-tuple-element.62), channel_id=1, source_target_pairs={{0,2},{1,3},{2,0},{3,1},{4,6},{5,7},{6,4},{7,5},{8,10},{9,11},{10,... | collective-permute-start | bytes 589832 | tf_op jit(solution)/shard_map/ppermute | solution.py:80
  83.5 5.4 %down_score.1.rest_3_ = bf16[3072,2048]{1,0:T(8,128)(2,1)} custom-call(bf16[2,32,1024]{2,1,0:T(8,128)(2,1)S(1)} %get-tuple-element.40.refs_0_, bf16[2,32,1024]{2,1,0:T(8,128)(2,1)S(1)} %collective-permute-done.8.refs_1_, bf16[2,32,1024]{2,1,0:T(8,128)(2,1)S(1)} %get-tuple-element.43.refs_2_, bf16[2,32,1024]{2,1,0:T(8,128)(2,1)S(1)} %collective-permute-done.11.refs_3_, ...), custom_call_target="tpu_custom_call" | custom-call | flops 1610612736 | bytes 25165824 | tf_op jit(solution)/shard_map/down_score/pallas_call | solution.py:426
  88.8 0.1 collective-permute-done.27.arrived_ref
  89.0 0.1 collective-permute-start.28
  89.1 3.1 %collective-permute-done.24.arrived_ref = bf16[2,32,1536]{2,1,0:T(8,128)(2,1)S(1)} collective-permute-done((bf16[2,32,1536]{2,1,0:T(8,128)(2,1)S(1)}, bf16[2,32,1536]{2,1,0:T(8,128)(2,1)S(1)}, u32[]{:S(2)}, u32[]{:S(2)}) %collective-permute-start.24) | collective-permute-done | bytes 196640 | tf_op jit(solution)/shard_map/ppermute | solution.py:80
  92.3 0.1 collective-permute-start.25
  92.4 1.3 %collective-permute-done.25.rest_1_ = bf16[32,1536]{1,0:T(8,128)(2,1)S(1)} collective-permute-done((bf16[32,1536]{1,0:T(8,128)(2,1)S(1)}, bf16[32,1536]{1,0:T(8,128)(2,1)S(1)}, u32[]{:S(2)}, u32[]{:S(2)}) %collective-permute-start.25) | collective-permute-done | bytes 98336 | tf_op jit(solution)/shard_map/ppermute | solution.py:76
  93.7 0.8 slice-done.2
  94.5 5.4 %gate_score.1 = bf16[2048,3072]{1,0:T(8,128)(2,1)} custom-call(bf16[64,2048]{1,0:T(8,128)(2,1)S(1)} %bitcast.35, bf16[32,1536]{1,0:T(8,128)(2,1)S(1)} %combined.2.rest_0_, bf16[32,1536]{1,0:T(8,128)(2,1)S(1)} %collective-permute-done.25.rest_1_, bf16[32,1536]{1,0:T(8,128)(2,1)S(1)} %combined.3.rest_2_, bf16[32,1536]{1,0:T(8,128)(2,1)S(1)} %collective-permute-done.28.rest_3_, ...), custom_call_target="tpu_custom_call" | custom-call | flops 805306368 | bytes 25165824 | tf_op jit(solution)/shard_map/gate_score/pallas_call | solution.py:507
  (53 shorter events, 0.6 us)
Async XLA Ops:
  1.8 6.3 %collective-permute-start = (bf16[1,8,2048]{2,1,0:T(8,128)(2,1)S(1)}, bf16[1,8,2048]{2,1,0:T(8,128)(2,1)S(1)}, u32[]{:S(2)}, u32[]{:S(2)}) collective-permute-start(bf16[1,8,2048]{2,1,0:T(8,128)(2,1)S(1)} %norm_rows.1.refs_0_), channel_id=1, source_target_pairs={{0,16},{4,20},{8,24},{12,28},{16,0},{20,4},{24,8},{28,12},{1,17},{... | collective-permute-start | bytes 98312 | tf_op jit(solution)/shard_map/ppermute | solution.py:528
  8.1 11.5 %slice-start.6 = ((s8[12582912]{0:T(1024)(128)(4,1)}), s8[4194304]{0:T(1024)(128)(4,1)S(1)}, s32[]{:S(2)}) async-start(s8[12582912]{0:T(1024)(128)(4,1)} %bitcast.30), calls=%async_computation.6 | async-start | bytes 8388608
  8.1 11.5 %slice-start.7 = ((s8[12582912]{0:T(1024)(128)(4,1)}), s8[4194304]{0:T(1024)(128)(4,1)S(1)}, s32[]{:S(2)}) async-start(s8[12582912]{0:T(1024)(128)(4,1)} %bitcast.30), calls=%async_computation.7 | async-start | bytes 8388608
  8.1 11.5 %slice-start.3 = ((s8[12582912]{0:T(1024)(128)(4,1)}), s8[4194304]{0:T(1024)(128)(4,1)S(1)}, s32[]{:S(2)}) async-start(s8[12582912]{0:T(1024)(128)(4,1)} %bitcast.28), calls=%async_computation.3 | async-start | bytes 8388608
  8.1 4.0 %collective-permute-start.1 = (bf16[2,8,1024]{2,1,0:T(8,128)(2,1)S(1)}, bf16[2,8,1024]{2,1,0:T(8,128)(2,1)S(1)}, u32[]{:S(2)}, u32[]{:S(2)}) collective-permute-start(bf16[2,8,1024]{2,1,0:T(8,128)(2,1)S(1)} %get-tuple-element.31.refs_0_), channel_id=1, source_target_pairs={{0,8},{4,12},{8,0},{12,4},{16,24},{20,28},{24,16},{28,20},{1,9},{5... | collective-permute-start | bytes 98312 | tf_op jit(solution)/shard_map/ppermute | solution.py:528
  9.7 9.9 %slice-start.4 = ((s8[12582912]{0:T(1024)(128)(4,1)}), s8[4194304]{0:T(1024)(128)(4,1)S(1)}, s32[]{:S(2)}) async-start(s8[12582912]{0:T(1024)(128)(4,1)} %bitcast.28), calls=%async_computation.4 | async-start | bytes 8388608
  9.7 9.9 %slice-start.5 = ((s8[12582912]{0:T(1024)(128)(4,1)}), s8[4194304]{0:T(1024)(128)(4,1)S(1)}, s32[]{:S(2)}) async-start(s8[12582912]{0:T(1024)(128)(4,1)} %bitcast.28), calls=%async_computation.5 | async-start | bytes 8388608
  9.8 9.9 %slice-start.8 = ((s8[12582912]{0:T(1024)(128)(4,1)}), s8[4194304]{0:T(1024)(128)(4,1)S(1)}, s32[]{:S(2)}) async-start(s8[12582912]{0:T(1024)(128)(4,1)} %bitcast.30), calls=%async_computation.8 | async-start | bytes 8388608
  9.8 3.9 %collective-permute-start.2 = (bf16[2,8,1024]{2,1,0:T(8,128)(2,1)S(1)}, bf16[2,8,1024]{2,1,0:T(8,128)(2,1)S(1)}, u32[]{:S(2)}, u32[]{:S(2)}) collective-permute-start(bf16[2,8,1024]{2,1,0:T(8,128)(2,1)S(1)} %get-tuple-element.32.refs_1_), channel_id=1, source_target_pairs={{0,4},{4,0},{8,12},{12,8},{16,20},{20,16},{24,28},{28,24},{1,5},{5... | collective-permute-start | bytes 98312 | tf_op jit(solution)/shard_map/ppermute | solution.py:528
  13.7 4.3 %collective-permute-start.3 = (bf16[4,8,1024]{2,1,0:T(8,128)(2,1)S(1)}, bf16[4,8,1024]{2,1,0:T(8,128)(2,1)S(1)}, u32[]{:S(2)}, u32[]{:S(2)}) collective-permute-start(bf16[4,8,1024]{2,1,0:T(8,128)(2,1)S(1)} %get-tuple-element.33.a0), channel_id=1, source_target_pairs={{0,4},{4,0},{8,12},{12,8},{16,20},{20,16},{24,28},{28,24},{1,5},{5... | collective-permute-start | bytes 196616 | tf_op jit(solution)/shard_map/ppermute | solution.py:528
  15.3 4.3 %collective-permute-start.4 = (bf16[4,8,1024]{2,1,0:T(8,128)(2,1)S(1)}, bf16[4,8,1024]{2,1,0:T(8,128)(2,1)S(1)}, u32[]{:S(2)}, u32[]{:S(2)}) collective-permute-start(bf16[4,8,1024]{2,1,0:T(8,128)(2,1)S(1)} %get-tuple-element.34.b0), channel_id=1, source_target_pairs={{0,8},{4,12},{8,0},{12,4},{16,24},{20,28},{24,16},{28,20},{1,9},{5... | collective-permute-start | bytes 196616 | tf_op jit(solution)/shard_map/ppermute | solution.py:528
  22.9 3.9 %collective-permute-start.5 = (bf16[3,32,1024]{2,1,0:T(8,128)(2,1)S(1)}, bf16[3,32,1024]{2,1,0:T(8,128)(2,1)S(1)}, u32[]{:S(2)}, u32[]{:S(2)}) collective-permute-start(bf16[3,32,1024]{2,1,0:T(8,128)(2,1)S(1)} %get-tuple-element.36), channel_id=1, source_target_pairs={{0,1},{1,0},{2,3},{3,2},{4,5},{5,4},{6,7},{7,6},{8,9},{9,8},{10,11... | collective-permute-start | bytes 589832 | tf_op jit(solution)/shard_map/ppermute | solution.py:76
  26.3 5.5 %collective-permute-start.9 = (bf16[3,32,1024]{2,1,0:T(8,128)(2,1)S(1)}, bf16[3,32,1024]{2,1,0:T(8,128)(2,1)S(1)}, u32[]{:S(2)}, u32[]{:S(2)}) collective-permute-start(bf16[3,32,1024]{2,1,0:T(8,128)(2,1)S(1)} %get-tuple-element.42), channel_id=1, source_target_pairs={{0,1},{1,0},{2,3},{3,2},{4,5},{5,4},{6,7},{7,6},{8,9},{9,8},{10,11... | collective-permute-start | bytes 589832 | tf_op jit(solution)/shard_map/ppermute | solution.py:76
  26.9 15.7 %collective-permute-start.6 = (bf16[3,32,1024]{2,1,0:T(8,128)(2,1)S(1)}, bf16[3,32,1024]{2,1,0:T(8,128)(2,1)S(1)}, u32[]{:S(2)}, u32[]{:S(2)}) collective-permute-start(bf16[3,32,1024]{2,1,0:T(8,128)(2,1)S(1)} %get-tuple-element.68.rest_0_), channel_id=1, source_target_pairs={{0,2},{1,3},{2,0},{3,1},{4,6},{5,7},{6,4},{7,5},{8,10},{9,11},{10,... | collective-permute-start | bytes 589832 | tf_op jit(solution)/shard_map/ppermute | solution.py:80
  31.7 1.5 %collective-permute-start.7 = (bf16[3,32,1024]{2,1,0:T(8,128)(2,1)S(1)}, bf16[3,32,1024]{2,1,0:T(8,128)(2,1)S(1)}, u32[]{:S(2)}, u32[]{:S(2)}) collective-permute-start(bf16[3,32,1024]{2,1,0:T(8,128)(2,1)S(1)} %get-tuple-element.38), channel_id=1, source_target_pairs={{0,1},{1,0},{2,3},{3,2},{4,5},{5,4},{6,7},{7,6},{8,9},{9,8},{10,11... | collective-permute-start | bytes 589832 | tf_op jit(solution)/shard_map/ppermute | solution.py:76
  31.8 10.5 %collective-permute-start.10 = (bf16[3,32,1024]{2,1,0:T(8,128)(2,1)S(1)}, bf16[3,32,1024]{2,1,0:T(8,128)(2,1)S(1)}, u32[]{:S(2)}, u32[]{:S(2)}) collective-permute-start(bf16[3,32,1024]{2,1,0:T(8,128)(2,1)S(1)} %get-tuple-element.64), channel_id=1, source_target_pairs={{0,2},{1,3},{2,0},{3,1},{4,6},{5,7},{6,4},{7,5},{8,10},{9,11},{10,... | collective-permute-start | bytes 589832 | tf_op jit(solution)/shard_map/ppermute | solution.py:80
  33.2 10.2 %collective-permute-start.12 = (bf16[3,32,1024]{2,1,0:T(8,128)(2,1)S(1)}, bf16[3,32,1024]{2,1,0:T(8,128)(2,1)S(1)}, u32[]{:S(2)}, u32[]{:S(2)}) collective-permute-start(bf16[3,32,1024]{2,1,0:T(8,128)(2,1)S(1)} %get-tuple-element.66.refs_2_), channel_id=1, source_target_pairs={{0,2},{1,3},{2,0},{3,1},{4,6},{5,7},{6,4},{7,5},{8,10},{9,11},{10,... | collective-permute-start | bytes 589832 | tf_op jit(solution)/shard_map/ppermute | solution.py:80
  42.5 1.4 %collective-permute-start.11 = (bf16[2,32,1024]{2,1,0:T(8,128)(2,1)S(1)}, bf16[2,32,1024]{2,1,0:T(8,128)(2,1)S(1)}, u32[]{:S(2)}, u32[]{:S(2)}) collective-permute-start(bf16[2,32,1024]{2,1,0:T(8,128)(2,1)S(1)} %get-tuple-element.43.refs_2_), channel_id=1, source_target_pairs={{0,1},{1,0},{2,3},{3,2},{4,5},{5,4},{6,7},{7,6},{8,9},{9,8},{10,11... | collective-permute-start | bytes 393224 | tf_op jit(solution)/shard_map/ppermute | solution.py:76
  42.7 1.5 %collective-permute-start.8 = (bf16[2,32,1024]{2,1,0:T(8,128)(2,1)S(1)}, bf16[2,32,1024]{2,1,0:T(8,128)(2,1)S(1)}, u32[]{:S(2)}, u32[]{:S(2)}) collective-permute-start(bf16[2,32,1024]{2,1,0:T(8,128)(2,1)S(1)} %get-tuple-element.40.refs_0_), channel_id=1, source_target_pairs={{0,1},{1,0},{2,3},{3,2},{4,5},{5,4},{6,7},{7,6},{8,9},{9,8},{10,11... | collective-permute-start | bytes 393224 | tf_op jit(solution)/shard_map/ppermute | solution.py:76
  43.5 1.4 %collective-permute-start.13 = (bf16[2,32,1024]{2,1,0:T(8,128)(2,1)S(1)}, bf16[2,32,1024]{2,1,0:T(8,128)(2,1)S(1)}, u32[]{:S(2)}, u32[]{:S(2)}) collective-permute-start(bf16[2,32,1024]{2,1,0:T(8,128)(2,1)S(1)} %get-tuple-element.44.refs_4_), channel_id=1, source_target_pairs={{0,1},{1,0},{2,3},{3,2},{4,5},{5,4},{6,7},{7,6},{8,9},{9,8},{10,11... | collective-permute-start | bytes 393224 | tf_op jit(solution)/shard_map/ppermute | solution.py:76
  47.1 5.6 %collective-permute-start.14 = (bf16[2,2,64,256]{3,2,1,0:T(8,128)(2,1)S(1)}, bf16[2,2,64,256]{3,2,1,0:T(8,128)(2,1)S(1)}, u32[]{:S(2)}, u32[]{:S(2)}) collective-permute-start(bf16[2,2,64,256]{3,2,1,0:T(8,128)(2,1)S(1)} %get-tuple-element.47), channel_id=1, source_target_pairs={{0,4},{4,0},{8,12},{12,8},{16,20},{20,16},{24,28},{28,24},{1,5},{5... | collective-permute-start | bytes 393224 | tf_op jit(solution)/shard_map/ppermute | solution.py:528
  47.7 17.8 %copy-start = (bf16[64,2048]{1,0:T(8,128)(2,1)S(1)}, bf16[64,2048]{1,0:T(8,128)(2,1)}, u32[]{:S(2)}) copy-start(bf16[64,2048]{1,0:T(8,128)(2,1)} %target_ref.1) | copy-start | bytes 786436
  47.7 6.1 %collective-permute-start.16 = (bf16[2,2,64,256]{3,2,1,0:T(8,128)(2,1)S(1)}, bf16[2,2,64,256]{3,2,1,0:T(8,128)(2,1)S(1)}, u32[]{:S(2)}, u32[]{:S(2)}) collective-permute-start(bf16[2,2,64,256]{3,2,1,0:T(8,128)(2,1)S(1)} %get-tuple-element.49), channel_id=1, source_target_pairs={{0,8},{4,12},{8,0},{12,4},{16,24},{20,28},{24,16},{28,20},{1,9},{5... | collective-permute-start | bytes 393224 | tf_op jit(solution)/shard_map/ppermute | solution.py:528
  52.8 4.3 %collective-permute-start.15 = (bf16[2,64,256]{2,1,0:T(8,128)(2,1)S(1)}, bf16[2,64,256]{2,1,0:T(8,128)(2,1)S(1)}, u32[]{:S(2)}, u32[]{:S(2)}) collective-permute-start(bf16[2,64,256]{2,1,0:T(8,128)(2,1)S(1)} %fusion.4), channel_id=1, source_target_pairs={{0,8},{4,12},{8,0},{12,4},{16,24},{20,28},{24,16},{28,20},{1,9},{5... | collective-permute-start | bytes 196616 | tf_op jit(solution)/shard_map/ppermute | solution.py:528
  53.8 4.3 %collective-permute-start.17 = (bf16[2,64,256]{2,1,0:T(8,128)(2,1)S(1)}, bf16[2,64,256]{2,1,0:T(8,128)(2,1)S(1)}, u32[]{:S(2)}, u32[]{:S(2)}) collective-permute-start(bf16[2,64,256]{2,1,0:T(8,128)(2,1)S(1)} %fusion.5), channel_id=1, source_target_pairs={{0,4},{4,0},{8,12},{12,8},{16,20},{20,16},{24,28},{28,24},{1,5},{5... | collective-permute-start | bytes 196616 | tf_op jit(solution)/shard_map/ppermute | solution.py:528
  58.2 7.3 %collective-permute-start.18 = (bf16[2,2,64,256]{3,2,1,0:T(8,128)(2,1)S(1)}, bf16[2,2,64,256]{3,2,1,0:T(8,128)(2,1)S(1)}, u32[]{:S(2)}, u32[]{:S(2)}) collective-permute-start(bf16[2,2,64,256]{3,2,1,0:T(8,128)(2,1)S(1)} %fusion.6), channel_id=1, source_target_pairs={{0,16},{4,20},{8,24},{12,28},{16,0},{20,4},{24,8},{28,12},{1,17},{... | collective-permute-start | bytes 393224 | tf_op jit(solution)/shard_map/ppermute | solution.py:528
  65.6 5.0 %collective-permute-start.20 = (bf16[2,64,256]{2,1,0:T(8,128)(2,1)S(1)}, bf16[2,64,256]{2,1,0:T(8,128)(2,1)S(1)}, u32[]{:S(2)}, u32[]{:S(2)}) collective-permute-start(bf16[2,64,256]{2,1,0:T(8,128)(2,1)S(1)} %get-tuple-element.51), channel_id=1, source_target_pairs={{0,4},{4,0},{8,12},{12,8},{16,20},{20,16},{24,28},{28,24},{1,5},{5... | collective-permute-start | bytes 196616 | tf_op jit(solution)/shard_map/ppermute | solution.py:528
  66.3 4.3 %collective-permute-start.19 = (bf16[2,64,256]{2,1,0:T(8,128)(2,1)S(1)}, bf16[2,64,256]{2,1,0:T(8,128)(2,1)S(1)}, u32[]{:S(2)}, u32[]{:S(2)}) collective-permute-start(bf16[2,64,256]{2,1,0:T(8,128)(2,1)S(1)} %get-tuple-element.50), channel_id=1, source_target_pairs={{0,8},{4,12},{8,0},{12,4},{16,24},{20,28},{24,16},{28,20},{1,9},{5... | collective-permute-start | bytes 196616 | tf_op jit(solution)/shard_map/ppermute | solution.py:528
  70.5 5.3 %collective-permute-start.22 = (bf16[2,2,64,256]{3,2,1,0:T(8,128)(2,1)S(1)}, bf16[2,2,64,256]{3,2,1,0:T(8,128)(2,1)S(1)}, u32[]{:S(2)}, u32[]{:S(2)}) collective-permute-start(bf16[2,2,64,256]{3,2,1,0:T(8,128)(2,1)S(1)} %pad_maximum_fusion.2.b_ref), channel_id=1, source_target_pairs={{0,8},{4,12},{8,0},{12,4},{16,24},{20,28},{24,16},{28,20},{1,9},{5... | collective-permute-start | bytes 393224 | tf_op jit(solution)/shard_map/ppermute | solution.py:528
  70.7 5.1 %collective-permute-start.21 = (bf16[2,2,64,256]{3,2,1,0:T(8,128)(2,1)S(1)}, bf16[2,2,64,256]{3,2,1,0:T(8,128)(2,1)S(1)}, u32[]{:S(2)}, u32[]{:S(2)}) collective-permute-start(bf16[2,2,64,256]{3,2,1,0:T(8,128)(2,1)S(1)} %pad_maximum_fusion.1.a_ref), channel_id=1, source_target_pairs={{0,4},{4,0},{8,12},{12,8},{16,20},{20,16},{24,28},{28,24},{1,5},{5... | collective-permute-start | bytes 393224 | tf_op jit(solution)/shard_map/ppermute | solution.py:528
  78.1 3.0 %collective-permute-start.26 = (bf16[2,32,1536]{2,1,0:T(8,128)(2,1)S(1)}, bf16[2,32,1536]{2,1,0:T(8,128)(2,1)S(1)}, u32[]{:S(2)}, u32[]{:S(2)}) collective-permute-start(bf16[2,32,1536]{2,1,0:T(8,128)(2,1)S(1)} %get-tuple-element.59), channel_id=1, source_target_pairs={{0,1},{1,0},{2,3},{3,2},{4,5},{5,4},{6,7},{7,6},{8,9},{9,8},{10,11... | collective-permute-start | bytes 589832 | tf_op jit(solution)/shard_map/ppermute | solution.py:76
  80.5 1.8 %collective-permute-start.23 = (bf16[2,32,1536]{2,1,0:T(8,128)(2,1)S(1)}, bf16[2,32,1536]{2,1,0:T(8,128)(2,1)S(1)}, u32[]{:S(2)}, u32[]{:S(2)}) collective-permute-start(bf16[2,32,1536]{2,1,0:T(8,128)(2,1)S(1)} %get-tuple-element.53), channel_id=1, source_target_pairs={{0,1},{1,0},{2,3},{3,2},{4,5},{5,4},{6,7},{7,6},{8,9},{9,8},{10,11... | collective-permute-start | bytes 589832 | tf_op jit(solution)/shard_map/ppermute | solution.py:76
  81.1 7.8 %collective-permute-start.27 = (bf16[2,32,1536]{2,1,0:T(8,128)(2,1)S(1)}, bf16[2,32,1536]{2,1,0:T(8,128)(2,1)S(1)}, u32[]{:S(2)}, u32[]{:S(2)}) collective-permute-start(bf16[2,32,1536]{2,1,0:T(8,128)(2,1)S(1)} %get-tuple-element.60), channel_id=1, source_target_pairs={{0,2},{1,3},{2,0},{3,1},{4,6},{5,7},{6,4},{7,5},{8,10},{9,11},{10,... | collective-permute-start | bytes 589832 | tf_op jit(solution)/shard_map/ppermute | solution.py:80
  82.4 9.8 %collective-permute-start.24 = (bf16[2,32,1536]{2,1,0:T(8,128)(2,1)S(1)}, bf16[2,32,1536]{2,1,0:T(8,128)(2,1)S(1)}, u32[]{:S(2)}, u32[]{:S(2)}) collective-permute-start(bf16[2,32,1536]{2,1,0:T(8,128)(2,1)S(1)} %get-tuple-element.62), channel_id=1, source_target_pairs={{0,2},{1,3},{2,0},{3,1},{4,6},{5,7},{6,4},{7,5},{8,10},{9,11},{10,... | collective-permute-start | bytes 589832 | tf_op jit(solution)/shard_map/ppermute | solution.py:80
  89.0 4.7 %slice-start = ((s8[12582912]{0:T(1024)(128)(4,1)}), s8[4194304]{0:T(1024)(128)(4,1)S(1)}, s32[]{:S(2)}) async-start(s8[12582912]{0:T(1024)(128)(4,1)} %bitcast.26), calls=%async_computation | async-start | bytes 8388608
  89.0 4.7 %slice-start.1 = ((s8[12582912]{0:T(1024)(128)(4,1)}), s8[4194304]{0:T(1024)(128)(4,1)S(1)}, s32[]{:S(2)}) async-start(s8[12582912]{0:T(1024)(128)(4,1)} %bitcast.26), calls=%async_computation.1 | async-start | bytes 8388608
  89.0 3.4 %collective-permute-start.28 = (bf16[32,1536]{1,0:T(8,128)(2,1)S(1)}, bf16[32,1536]{1,0:T(8,128)(2,1)S(1)}, u32[]{:S(2)}, u32[]{:S(2)}) collective-permute-start(bf16[32,1536]{1,0:T(8,128)(2,1)S(1)} %combined.3.rest_2_), channel_id=1, source_target_pairs={{0,1},{1,0},{2,3},{3,2},{4,5},{5,4},{6,7},{7,6},{8,9},{9,8},{10,11... | collective-permute-start | bytes 294920 | tf_op jit(solution)/shard_map/ppermute | solution.py:76
  92.2 2.2 %slice-start.2 = ((s8[12582912]{0:T(1024)(128)(4,1)}), s8[4194304]{0:T(1024)(128)(4,1)S(1)}, s32[]{:S(2)}) async-start(s8[12582912]{0:T(1024)(128)(4,1)} %bitcast.26), calls=%async_computation.2 | async-start | bytes 8388608
  92.3 1.4 %collective-permute-start.25 = (bf16[32,1536]{1,0:T(8,128)(2,1)S(1)}, bf16[32,1536]{1,0:T(8,128)(2,1)S(1)}, u32[]{:S(2)}, u32[]{:S(2)}) collective-permute-start(bf16[32,1536]{1,0:T(8,128)(2,1)S(1)} %combined.2.rest_0_), channel_id=1, source_target_pairs={{0,1},{1,0},{2,3},{3,2},{4,5},{5,4},{6,7},{7,6},{8,9},{9,8},{10,11... | collective-permute-start | bytes 294920 | tf_op jit(solution)/shard_map/ppermute | solution.py:76

commit v5 on v4

--- a/solution.py
+++ b/solution.py
@@ -11,7 +11,7 @@
 bf16 = jnp.bfloat16
 f32 = jnp.float32
 MIB = 1024 * 1024
-WAIT_FLOPS = 6 * 10**9
+WAIT_FLOPS = 15 * 10**9
 CHUNKS = 3
 BACK_CHUNKS = 2
 BUFFERS = 4
@@ -80,8 +80,9 @@
     return lax.ppermute(value, "mp", [(i, i ^ 2) for i in range(4)])
 
 
-def load_call(weights, after, name):
+def load_call(weights, after, name, shares=1):
     n = len(weights)
+    shapes = [(w.shape[0], w.shape[1] // shares) for w in weights]
     parts = 4
 
     def body(*refs):
@@ -93,7 +94,7 @@
                 span = pl.ds(j * rows, rows)
                 copies.append(
                     pltpu.make_async_copy(
-                        sources[i].at[span], targets[i].at[span], sems.at[i, j]
+                        sources[i].at[span, pl.ds(0, shapes[i][1])], targets[i].at[span], sems.at[i, j]
                     )
                 )
         for copy in copies:
@@ -101,12 +102,12 @@
         for copy in copies:
             copy.wait()
 
-    size = sum(w.size * 2 for w in weights)
+    size = sum(w.size * 2 for w in weights) // shares
     return pl.pallas_call(
         body,
         in_specs=[IN_HBM] * n + [pl.BlockSpec(memory_space=pl.ANY)],
         out_specs=[IN_VMEM] * n,
-        out_shape=[pltpu.VMEM(w.shape, w.dtype) for w in weights],
+        out_shape=[pltpu.VMEM(shape, w.dtype) for shape, w in zip(shapes, weights)],
         scratch_shapes=[pltpu.SemaphoreType.DMA((n, parts))],
         compiler_params=params(1),
         cost_estimate=cost(0, 2 * size),
@@ -186,10 +187,10 @@
     )(*flat)
 
 
-def order_call(a_blocks, b_blocks):
+def order_call(a_blocks, b_blocks, after):
     _, own, half = a_blocks[0].shape
 
-    def body(a0, a1, b0, b1, out_ref):
+    def body(a0, a1, b0, b1, after_ref, out_ref):
         index = lax.axis_index("dp")
         for refs, order, cols in (
             ((a0, a1), (0, 4, 2, 6, 1, 5, 3, 7), slice(0, half)),
@@ -200,22 +201,23 @@
 
     return pl.pallas_call(
         body,
-        in_specs=[IN_VMEM] * 4,
+        in_specs=[IN_VMEM] * 4 + [pl.BlockSpec(memory_space=pl.ANY)],
         out_specs=IN_VMEM,
         out_shape=jax.ShapeDtypeStruct((8, own, 2 * half), bf16),
         compiler_params=params(4),
         cost_estimate=cost(0, 64 * own * half),
         name="token_order",
-    )(*a_blocks, *b_blocks)
-
-
-def gather_tree(block):
+    )(*a_blocks, *b_blocks, after)
+
+
+def gather_tree(block, v_gate, chunks):
     arrived = swap_dp(block, 4)
     a_two, b_two = join_call([[block], [arrived]])
     a_came, b_came = swap_dp(a_two, 2), swap_dp(b_two, 1)
     a_four, b_four = join_call([[a_two, b_two], [a_came, b_came]])
     a_came, b_came = swap_dp(a_four, 1), swap_dp(b_four, 2)
-    return order_call((a_four, a_came), (b_four, b_came))
+    (first,) = load_call([v_gate], a_four, "load_first", chunks)
+    return order_call((a_four, a_came), (b_four, b_came), held(first)), first
 
 
 def gate_call(normed, w_gate, w_up, v_gate, chunk, chunks):
@@ -250,7 +252,7 @@
     )(normed, *[kept_out(w) for w in (w_gate, w_up, v_gate)])
 
 
-def gate_held_call(normed, w_gate, w_up, v_gate, chunk, chunks, after):
+def gate_held_call(normed, w_gate, w_up, v_gate, first_probe, chunk, chunks, after):
     count, depth = normed.shape
     half = count // 2
     width = w_gate.shape[1] // chunks
@@ -264,7 +266,7 @@
             pltpu.make_async_copy(
                 tan_ref.at[:, pl.ds(first + j * block, block)], buffer.at[j], sems.at[j]
             )
-            for j in range(steps)
+            for j in range(0 if chunk == 0 else steps)
         ]
         for copy in copies:
             copy.start()
@@ -272,7 +274,9 @@
         for i, weight in enumerate((gate_ref, up_ref, None)):
             for j in range(steps):
                 span = slice(j * block, (j + 1) * block)
-                if weight is None:
+                if weight is None and chunk == 0:
+                    right = tan_ref[:, span]
+                elif weight is None:
                     copies[j].wait()
                     right = buffer[j]
                 else:
@@ -282,8 +286,9 @@
                 keep_ref[i, :, span] = jnp.where(upper, high, low)
                 send_ref[i, :, span] = jnp.where(upper, low, high).astype(bf16)
 
-    operands = [normed, held(w_gate), held(w_up), kept_out(v_gate)]
-    in_specs = [IN_VMEM] * 3 + [IN_HBM]
+    probe = held(first_probe) if chunk == 0 else kept_out(v_gate)
+    operands = [normed, held(w_gate), held(w_up), probe]
+    in_specs = [IN_VMEM] * 3 + [IN_VMEM if chunk == 0 else IN_HBM]
     order(operands, in_specs, after)
     return pl.pallas_call(
         body,
@@ -739,11 +744,14 @@
     chunks, back_chunks = (CHUNKS, BACK_CHUNKS) if dp == 8 else (1, 1)
     if dp == 8:
         block = norm_call(tokens, norm_gain, 1, col_width)
-        normed = gather_tree(block).reshape(count, col_width)
+        normed, first = gather_tree(block, v_gate, chunks)
+        normed = normed.reshape(count, col_width)
         sums = []
         for chunk in range(chunks):
             after = sums[chunk - 2][1] if chunk > 1 else None
-            products = gate_held_call(normed, w_gate, w_up, v_gate, chunk, chunks, after)
+            products = gate_held_call(
+                normed, w_gate, w_up, v_gate, first, chunk, chunks, after
+            )
             sums.append(chip_sum_of(products))
     else:
         copies = norm_call(tokens, norm_gain, dp, col_width)
@@ -753,7 +761,7 @@
     waits = [None] * chunks
     if dp == 8:
         w_down, v_down = load_call([w_down, v_down], sums[-1][1], "load_down")
-        waits = [w_down] * chunks
+        waits = [None] + [w_down] * (chunks - 1)
     hiddens, factors = [], []
     for chunk, ((chip_sum, _), came, wait) in enumerate(zip(sums, arrived, waits)):
         mine, factor = hidden_call(chip_sum, came, None if wait is None else held(wait))

time: 100 us -> 99.4 us (level)
  waiting for transfers between devices: 29.3 us -> 23.6 us
  starting transfers between devices: 25.2 us -> 28 us
  Pallas kernels: 43.1 us -> 45.1 us
    ppermute x14, waiting for transfers between devices: 22.5 us -> 16.8 us  [swap_dp(): return lax.ppermute(value, 'dp', [(i, i ^ bit) for i in range(8)])]
    pallas_call x1 -> x2, Pallas kernels: 8.3 us -> 11.3 us  [load_call(): pl.pallas_call(body, in_specs=[IN_HBM] * n + [pl.BlockSpec(memory_space=p...]
    ppermute x14, starting transfers between devices: 17.8 us -> 20.6 us  [swap_dp(): return lax.ppermute(value, 'dp', [(i, i ^ bit) for i in range(8)])]
  transfers between devices with their start and end apart: 29 -> 29, of which waited for: 18 -> 18; matrix products, arithmetic and copies ran while one was open for 0% -> 0% of each run, Pallas kernels for 29% -> 32%
where the time goes in v5:
time: 99.4 us; the launch traced here: 99.3 us
  Pallas kernels  45.1 us (45%)
  starting transfers between devices  28 us (28%)
  waiting for transfers between devices  23.6 us (24%)
  between operations  1.21 us (1%)
  local copies, waits for them, and re-layouts  1 us (1%)
    ppermute x14, starting transfers between devices, swap_dp(): return lax.ppermute(value, 'dp', [(i, i ^ bit) for i in range(8)])  20.6 us
    ppermute x14, waiting for transfers between devices, swap_dp(): return lax.ppermute(value, 'dp', [(i, i ^ bit) for i in range(8)])  16.8 us
    pallas_call x2, Pallas kernels, load_call(): pl.pallas_call(body, in_specs=[IN_HBM] * n + [pl.BlockSpec(memory_space=p...  11.3 us
    pallas_call x3, Pallas kernels, gate_held_call(): pl.pallas_call(body, in_specs=in_specs, out_specs=[IN_VMEM] * 2, out_shap...  8.79 us
    pallas_call x1, Pallas kernels, down_score_call(): pl.pallas_call(body, in_specs=[IN_VMEM] * (n + 2), out_specs=IN_HBM, out_...  5.36 us
    pallas_call x1, Pallas kernels, gate_score_call(): pl.pallas_call(body, in_specs=[IN_VMEM] * (n + 2), out_specs=IN_HBM, out_...  5.36 us
    ppermute x5, starting transfers between devices, swap_chip(): return lax.ppermute(value, 'mp', [(i, i ^ 2) for i in range(4)])  5.22 us
    pallas_call x2, Pallas kernels, back_second_call(): pl.pallas_call(body, in_specs=[IN_VMEM] * 7, out_specs=[IN_VMEM] * len(ou...  4.62 us
  transfers between devices with their start and end apart: 29, of which 18 were waited for; matrix products, arithmetic and copies ran while one was open for 0% of the time, Pallas kernels for 32%

profile of v5, /device:TPU:0, one launch (start us, length us, event | category | flops | bytes accessed | tf_op | source)
XLA Modules:
  0.0 99.3 jit_solution(7102316897813156234)
XLA Ops:
  0.6 1.1 %norm_rows.1.refs_0_ = bf16[1,8,2048]{2,1,0:T(8,128)(2,1)S(1)} custom-call(bf16[8,8192]{1,0:T(8,128)(2,1)} %tokens_ref.1, f32[1,8192]{1,0:T(1,128)} %bitcast.40), custom_call_target="tpu_custom_call" | custom-call | flops 15000000512 | bytes 262144 | tf_op jit(solution)/shard_map/norm_rows/pallas_call | solution.py:138
  1.8 4.1 %collective-permute-start = (bf16[1,8,2048]{2,1,0:T(8,128)(2,1)S(1)}, bf16[1,8,2048]{2,1,0:T(8,128)(2,1)S(1)}, u32[]{:S(2)}, u32[]{:S(2)}) collective-permute-start(bf16[1,8,2048]{2,1,0:T(8,128)(2,1)S(1)} %norm_rows.1.refs_0_), channel_id=1, source_target_pairs={{0,16},{4,20},{8,24},{12,28},{16,0},{20,4},{24,8},{28,12},{1,17},{... | collective-permute-start | bytes 98312 | tf_op jit(solution)/shard_map/ppermute | solution.py:533
  5.9 2.2 %collective-permute-done.refs_1_ = bf16[1,8,2048]{2,1,0:T(8,128)(2,1)S(1)} collective-permute-done((bf16[1,8,2048]{2,1,0:T(8,128)(2,1)S(1)}, bf16[1,8,2048]{2,1,0:T(8,128)(2,1)S(1)}, u32[]{:S(2)}, u32[]{:S(2)}) %collective-permute-start) | collective-permute-done | bytes 32800 | tf_op jit(solution)/shard_map/ppermute | solution.py:533
  8.1 1.6 %collective-permute-start.1 = (bf16[2,8,1024]{2,1,0:T(8,128)(2,1)S(1)}, bf16[2,8,1024]{2,1,0:T(8,128)(2,1)S(1)}, u32[]{:S(2)}, u32[]{:S(2)}) collective-permute-start(bf16[2,8,1024]{2,1,0:T(8,128)(2,1)S(1)} %get-tuple-element.31.refs_0_), channel_id=1, source_target_pairs={{0,8},{4,12},{8,0},{12,4},{16,24},{20,28},{24,16},{28,20},{1,9},{5... | collective-permute-start | bytes 98312 | tf_op jit(solution)/shard_map/ppermute | solution.py:533
  9.7 1.6 %collective-permute-start.2 = (bf16[2,8,1024]{2,1,0:T(8,128)(2,1)S(1)}, bf16[2,8,1024]{2,1,0:T(8,128)(2,1)S(1)}, u32[]{:S(2)}, u32[]{:S(2)}) collective-permute-start(bf16[2,8,1024]{2,1,0:T(8,128)(2,1)S(1)} %get-tuple-element.32.refs_1_), channel_id=1, source_target_pairs={{0,4},{4,0},{8,12},{12,8},{16,20},{20,16},{24,28},{28,24},{1,5},{5... | collective-permute-start | bytes 98312 | tf_op jit(solution)/shard_map/ppermute | solution.py:533
  11.3 0.7 collective-permute-done.1.refs_2_
  12.0 1.7 %collective-permute-done.2.refs_3_ = bf16[2,8,1024]{2,1,0:T(8,128)(2,1)S(1)} collective-permute-done((bf16[2,8,1024]{2,1,0:T(8,128)(2,1)S(1)}, bf16[2,8,1024]{2,1,0:T(8,128)(2,1)S(1)}, u32[]{:S(2)}, u32[]{:S(2)}) %collective-permute-start.2) | collective-permute-done | bytes 32800 | tf_op jit(solution)/shard_map/ppermute | solution.py:533
  13.7 0.5 collective-permute-start.4
  14.2 1.7 %collective-permute-start.3 = (bf16[4,8,1024]{2,1,0:T(8,128)(2,1)S(1)}, bf16[4,8,1024]{2,1,0:T(8,128)(2,1)S(1)}, u32[]{:S(2)}, u32[]{:S(2)}) collective-permute-start(bf16[4,8,1024]{2,1,0:T(8,128)(2,1)S(1)} %get-tuple-element.33.refs_1_.a0), channel_id=1, source_target_pairs={{0,4},{4,0},{8,12},{12,8},{16,20},{20,16},{24,28},{28,24},{1,5},{5... | collective-permute-start | bytes 196616 | tf_op jit(solution)/shard_map/ppermute | solution.py:533
  15.9 3.0 %load_first.1.after_ref.tan_ref = bf16[2048,1024]{1,0:T(8,128)(2,1)S(1)} custom-call(bf16[2048,3072]{1,0:T(8,128)(2,1)} %rest_4_.1, bf16[4,8,1024]{2,1,0:T(8,128)(2,1)S(1)} %get-tuple-element.33.refs_1_.a0), custom_call_target="tpu_custom_call" | custom-call | bytes 8388608 | tf_op jit(solution)/shard_map/load_first/pallas_call | solution.py:106
  19.0 0.1 slice-done.8
  19.2 2.3 %gate_products.3 = (f32[3,32,1024]{2,1,0:T(8,128)S(1)}, bf16[3,32,1024]{2,1,0:T(8,128)(2,1)S(1)}) custom-call(bf16[64,2048]{1,0:T(8,128)(2,1)S(1)} %bitcast.32, bf16[2048,3072]{1,0:T(8,128)(2,1)S(1)} %bitcast.29, bf16[2048,3072]{1,0:T(8,128)(2,1)S(1)} %bitcast.31, bf16[2048,1024]{1,0:T(8,128)(2,1)S(1)} %load_first.1.after_ref.tan_ref), custom_call_target="tpu_custom_call" | custom-call | flops 805306368 | bytes 12582912 | tf_op jit(solution)/shard_map/gate_products/pallas_call | solution.py:293
  21.5 0.1 collective-permute-start.5
  21.6 3.2 %gate_products.4 = (f32[3,32,1024]{2,1,0:T(8,128)S(1)}, bf16[3,32,1024]{2,1,0:T(8,128)(2,1)S(1)}) custom-call(bf16[64,2048]{1,0:T(8,128)(2,1)S(1)} %bitcast.33, bf16[2048,3072]{1,0:T(8,128)(2,1)S(1)} %bitcast.29, bf16[2048,3072]{1,0:T(8,128)(2,1)S(1)} %bitcast.31, bf16[2048,3072]{1,0:T(8,128)(2,1)} %rest_4_.1), custom_call_target="tpu_custom_call" | custom-call | flops 805306368 | bytes 12582912 | tf_op jit(solution)/shard_map/gate_products/pallas_call | solution.py:293
  24.8 0.6 collective-permute-start.8
  25.5 1.6 %collective-permute-start.6 = (bf16[3,32,1024]{2,1,0:T(8,128)(2,1)S(1)}, bf16[3,32,1024]{2,1,0:T(8,128)(2,1)S(1)}, u32[]{:S(2)}, u32[]{:S(2)}) collective-permute-start(bf16[3,32,1024]{2,1,0:T(8,128)(2,1)S(1)} %get-tuple-element.68.rest_0_), channel_id=1, source_target_pairs={{0,2},{1,3},{2,0},{3,1},{4,6},{5,7},{6,4},{7,5},{8,10},{9,11},{10,... | collective-permute-start | bytes 589832 | tf_op jit(solution)/shard_map/ppermute | solution.py:80
  27.0 3.2 %gate_products.5 = (f32[3,32,1024]{2,1,0:T(8,128)S(1)}, bf16[3,32,1024]{2,1,0:T(8,128)(2,1)S(1)}) custom-call(bf16[64,2048]{1,0:T(8,128)(2,1)S(1)} %bitcast.34, bf16[2048,3072]{1,0:T(8,128)(2,1)S(1)} %bitcast.29, bf16[2048,3072]{1,0:T(8,128)(2,1)S(1)} %bitcast.31, bf16[2048,3072]{1,0:T(8,128)(2,1)} %rest_4_.1, bf16[3,32,1024]{2,1,0:T(8,128)(2,1)S(1)} %get-tuple-element.68.rest_0_), custom_call_target="tpu_custom_call" | custom-call | flops 805306368 | bytes 12582912 | tf_op jit(solution)/shard_map/gate_products/pallas_call | solution.py:293
  30.3 0.1 collective-permute-start.10
  30.4 0.6 collective-permute-start.9
  31.0 0.8 collective-permute-done.10
  31.8 0.8 collective-permute-start.12
  32.6 0.1 hidden_units.3
  32.8 8.3 %load_down.1 = (bf16[3072,2048]{1,0:T(8,128)(2,1)S(1)}, bf16[3072,2048]{1,0:T(8,128)(2,1)S(1)}) custom-call(bf16[3072,2048]{1,0:T(8,128)(2,1)} %refs_0_.3, bf16[3072,2048]{1,0:T(8,128)(2,1)} %refs_1_.1, bf16[3,32,1024]{2,1,0:T(8,128)(2,1)S(1)} %get-tuple-element.64.refs_2_), custom_call_target="tpu_custom_call" | custom-call | bytes 50331648 | tf_op jit(solution)/shard_map/load_down/pallas_call | solution.py:106
  41.2 0.1 hidden_units.4
  41.3 0.6 collective-permute-start.11
  41.9 0.1 collective-permute-done.12.arrived_ref
  42.0 0.1 hidden_units.5
  42.1 0.1 collective-permute-start.13
  42.2 0.6 collective-permute-done.11.refs_3_
  42.8 0.7 collective-permute-done.13.refs_5_
  43.5 2.1 %pieces_away.1 = (bf16[2,2,64,256]{3,2,1,0:T(8,128)(2,1)S(1)}, bf16[2,2,64,256]{3,2,1,0:T(8,128)(2,1)S(1)}) custom-call(bf16[2,32,1024]{2,1,0:T(8,128)(2,1)S(1)} %get-tuple-element.37.refs_0_, bf16[2,32,1024]{2,1,0:T(8,128)(2,1)S(1)} %collective-permute-done.7.refs_1_, bf16[2,32,1024]{2,1,0:T(8,128)(2,1)S(1)} %get-tuple-element.43.refs_2_, ...), custom_call_target="tpu_custom_call" | custom-call | flops 1207959552 | bytes 12582912 | tf_op jit(solution)/shard_map/pieces_away/pallas_call | solution.py:556
  45.7 1.6 %collective-permute-start.14 = (bf16[2,2,64,256]{3,2,1,0:T(8,128)(2,1)S(1)}, bf16[2,2,64,256]{3,2,1,0:T(8,128)(2,1)S(1)}, u32[]{:S(2)}, u32[]{:S(2)}) collective-permute-start(bf16[2,2,64,256]{3,2,1,0:T(8,128)(2,1)S(1)} %get-tuple-element.47), channel_id=1, source_target_pairs={{0,4},{4,0},{8,12},{12,8},{16,20},{20,16},{24,28},{28,24},{1,5},{5... | collective-permute-start | bytes 393224 | tf_op jit(solution)/shard_map/ppermute | solution.py:533
  47.3 1.0 collective-permute-start.16
  48.2 2.1 %pieces_home.1 = (f32[2,2,64,256]{3,2,1,0:T(8,128)S(1)}, f32[2,2,64,256]{3,2,1,0:T(8,128)S(1)}) custom-call(bf16[2,32,1024]{2,1,0:T(8,128)(2,1)S(1)} %get-tuple-element.37.refs_0_, bf16[2,32,1024]{2,1,0:T(8,128)(2,1)S(1)} %collective-permute-done.7.refs_1_, bf16[2,32,1024]{2,1,0:T(8,128)(2,1)S(1)} %get-tuple-element.43.refs_2_, ...), custom_call_target="tpu_custom_call" | custom-call | flops 1207959552 | bytes 12582912 | tf_op jit(solution)/shard_map/pieces_home/pallas_call | solution.py:556
  50.4 0.9 collective-permute-done.14
  51.3 1.0 %collective-permute-start.15 = (bf16[2,64,256]{2,1,0:T(8,128)(2,1)S(1)}, bf16[2,64,256]{2,1,0:T(8,128)(2,1)S(1)}, u32[]{:S(2)}, u32[]{:S(2)}) collective-permute-start(bf16[2,64,256]{2,1,0:T(8,128)(2,1)S(1)} %fusion.4), channel_id=1, source_target_pairs={{0,8},{4,12},{8,0},{12,4},{16,24},{20,28},{24,16},{28,20},{1,9},{5... | collective-permute-start | bytes 196616 | tf_op jit(solution)/shard_map/ppermute | solution.py:533
  52.4 0.2 collective-permute-done.16
  52.6 1.4 %collective-permute-start.17 = (bf16[2,64,256]{2,1,0:T(8,128)(2,1)S(1)}, bf16[2,64,256]{2,1,0:T(8,128)(2,1)S(1)}, u32[]{:S(2)}, u32[]{:S(2)}) collective-permute-start(bf16[2,64,256]{2,1,0:T(8,128)(2,1)S(1)} %fusion.5), channel_id=1, source_target_pairs={{0,4},{4,0},{8,12},{12,8},{16,20},{20,16},{24,28},{28,24},{1,5},{5... | collective-permute-start | bytes 196616 | tf_op jit(solution)/shard_map/ppermute | solution.py:533
  54.0 1.7 %collective-permute-done.15 = bf16[2,64,256]{2,1,0:T(8,128)(2,1)S(1)} collective-permute-done((bf16[2,64,256]{2,1,0:T(8,128)(2,1)S(1)}, bf16[2,64,256]{2,1,0:T(8,128)(2,1)S(1)}, u32[]{:S(2)}, u32[]{:S(2)}) %collective-permute-start.15) | collective-permute-done | bytes 65568 | tf_op jit(solution)/shard_map/ppermute | solution.py:533
  55.7 1.2 %collective-permute-done.17 = bf16[2,64,256]{2,1,0:T(8,128)(2,1)S(1)} collective-permute-done((bf16[2,64,256]{2,1,0:T(8,128)(2,1)S(1)}, bf16[2,64,256]{2,1,0:T(8,128)(2,1)S(1)}, u32[]{:S(2)}, u32[]{:S(2)}) %collective-permute-start.17) | collective-permute-done | bytes 65568 | tf_op jit(solution)/shard_map/ppermute | solution.py:533
  57.0 2.9 %collective-permute-start.18 = (bf16[2,2,64,256]{3,2,1,0:T(8,128)(2,1)S(1)}, bf16[2,2,64,256]{3,2,1,0:T(8,128)(2,1)S(1)}, u32[]{:S(2)}, u32[]{:S(2)}) collective-permute-start(bf16[2,2,64,256]{3,2,1,0:T(8,128)(2,1)S(1)} %fusion.6), channel_id=1, source_target_pairs={{0,16},{4,20},{8,24},{12,28},{16,0},{20,4},{24,8},{28,12},{1,17},{... | collective-permute-start | bytes 393224 | tf_op jit(solution)/shard_map/ppermute | solution.py:533
  59.9 4.4 %collective-permute-done.18.arrived_ref = bf16[2,2,64,256]{3,2,1,0:T(8,128)(2,1)S(1)} collective-permute-done((bf16[2,2,64,256]{3,2,1,0:T(8,128)(2,1)S(1)}, bf16[2,2,64,256]{3,2,1,0:T(8,128)(2,1)S(1)}, u32[]{:S(2)}, u32[]{:S(2)}) %collective-permute-start.18) | collective-permute-done | bytes 131104 | tf_op jit(solution)/shard_map/ppermute | solution.py:533
  64.3 1.4 %collective-permute-start.20 = (bf16[2,64,256]{2,1,0:T(8,128)(2,1)S(1)}, bf16[2,64,256]{2,1,0:T(8,128)(2,1)S(1)}, u32[]{:S(2)}, u32[]{:S(2)}) collective-permute-start(bf16[2,64,256]{2,1,0:T(8,128)(2,1)S(1)} %get-tuple-element.51), channel_id=1, source_target_pairs={{0,4},{4,0},{8,12},{12,8},{16,20},{20,16},{24,28},{28,24},{1,5},{5... | collective-permute-start | bytes 196616 | tf_op jit(solution)/shard_map/ppermute | solution.py:533
  65.8 0.5 collective-permute-start.19
  66.3 2.8 %collective-permute-done.20 = bf16[2,64,256]{2,1,0:T(8,128)(2,1)S(1)} collective-permute-done((bf16[2,64,256]{2,1,0:T(8,128)(2,1)S(1)}, bf16[2,64,256]{2,1,0:T(8,128)(2,1)S(1)}, u32[]{:S(2)}, u32[]{:S(2)}) %collective-permute-start.20) | collective-permute-done | bytes 65568 | tf_op jit(solution)/shard_map/ppermute | solution.py:533
  69.1 0.2 collective-permute-start.22
  69.4 0.6 collective-permute-done.19
  70.1 1.0 collective-permute-start.21
  71.0 3.8 %back_first.1.part_ref = f32[3072,128]{1,0:T(8,128)S(1)} custom-call(bf16[2,2,64,256]{3,2,1,0:T(8,128)(2,1)S(1)} %pad_maximum_fusion.1.a_ref, bf16[2,2,64,256]{3,2,1,0:T(8,128)(2,1)S(1)} %pad_maximum_fusion.2.b_ref, bf16[3072,2048]{1,0:T(8,128)(2,1)S(1)} %get-tuple-element.42.rest_0_.refs_6_.w_ref, bf16[3072,2048]{1,0:T(8,128)(2,1)S(1)} %get-tuple-element.45.refs_7_.v_ref), custom_call_target="tpu_custom_call" | custom-call | flops 603979776 | bytes 6291456 | tf_op jit(solution)/shard_map/back_first/pallas_call | solution.py:623
  74.8 0.3 collective-permute-done.21.a_far_ref
  75.1 2.3 %back_second.3 = (f32[2,32,1536]{2,1,0:T(8,128)S(1)}, bf16[2,32,1536]{2,1,0:T(8,128)(2,1)S(1)}) custom-call(bf16[2,2,64,256]{3,2,1,0:T(8,128)(2,1)S(1)} %pad_maximum_fusion.1.a_ref, bf16[2,2,64,256]{3,2,1,0:T(8,128)(2,1)S(1)} %pad_maximum_fusion.2.b_ref, bf16[2,2,64,256]{3,2,1,0:T(8,128)(2,1)S(1)} %collective-permute-done.21.a_far_ref, ...), custom_call_target="tpu_custom_call" | custom-call | flops 301989888 | bytes 3145728 | tf_op jit(solution)/shard_map/back_second/pallas_call | solution.py:679
  77.4 0.1 collective-permute-start.26
  77.5 2.3 %back_second.2 = (f32[2,32,1536]{2,1,0:T(8,128)S(1)}, bf16[2,32,1536]{2,1,0:T(8,128)(2,1)S(1)}, bf16[2,64,2048]{2,1,0:T(8,128)(2,1)S(1)}) custom-call(bf16[2,2,64,256]{3,2,1,0:T(8,128)(2,1)S(1)} %pad_maximum_fusion.1.a_ref, bf16[2,2,64,256]{3,2,1,0:T(8,128)(2,1)S(1)} %pad_maximum_fusion.2.b_ref, ...), custom_call_target="tpu_custom_call" | custom-call | flops 301989888 | bytes 3145728 | tf_op jit(solution)/shard_map/back_second/pallas_call | solution.py:679
  79.8 0.6 collective-permute-start.23
  80.4 1.2 %collective-permute-start.27 = (bf16[2,32,1536]{2,1,0:T(8,128)(2,1)S(1)}, bf16[2,32,1536]{2,1,0:T(8,128)(2,1)S(1)}, u32[]{:S(2)}, u32[]{:S(2)}) collective-permute-start(bf16[2,32,1536]{2,1,0:T(8,128)(2,1)S(1)} %get-tuple-element.60), channel_id=1, source_target_pairs={{0,2},{1,3},{2,0},{3,1},{4,6},{5,7},{6,4},{7,5},{8,10},{9,11},{10,... | collective-permute-start | bytes 589832 | tf_op jit(solution)/shard_map/ppermute | solution.py:80
  81.7 1.0 %collective-permute-start.24 = (bf16[2,32,1536]{2,1,0:T(8,128)(2,1)S(1)}, bf16[2,32,1536]{2,1,0:T(8,128)(2,1)S(1)}, u32[]{:S(2)}, u32[]{:S(2)}) collective-permute-start(bf16[2,32,1536]{2,1,0:T(8,128)(2,1)S(1)} %get-tuple-element.62), channel_id=1, source_target_pairs={{0,2},{1,3},{2,0},{3,1},{4,6},{5,7},{6,4},{7,5},{8,10},{9,11},{10,... | collective-permute-start | bytes 589832 | tf_op jit(solution)/shard_map/ppermute | solution.py:80
  82.7 5.4 %down_score.1.rest_3_ = bf16[3072,2048]{1,0:T(8,128)(2,1)} custom-call(bf16[2,32,1024]{2,1,0:T(8,128)(2,1)S(1)} %get-tuple-element.37.refs_0_, bf16[2,32,1024]{2,1,0:T(8,128)(2,1)S(1)} %collective-permute-done.7.refs_1_, bf16[2,32,1024]{2,1,0:T(8,128)(2,1)S(1)} %get-tuple-element.43.refs_2_, bf16[2,32,1024]{2,1,0:T(8,128)(2,1)S(1)} %collective-permute-done.11.refs_3_, ...), custom_call_target="tpu_custom_call" | custom-call | flops 1610612736 | bytes 25165824 | tf_op jit(solution)/shard_map/down_score/pallas_call | solution.py:431
  88.1 0.1 collective-permute-done.27.arrived_ref
  88.3 0.1 collective-permute-start.28
  88.4 3.1 %collective-permute-done.24.arrived_ref = bf16[2,32,1536]{2,1,0:T(8,128)(2,1)S(1)} collective-permute-done((bf16[2,32,1536]{2,1,0:T(8,128)(2,1)S(1)}, bf16[2,32,1536]{2,1,0:T(8,128)(2,1)S(1)}, u32[]{:S(2)}, u32[]{:S(2)}) %collective-permute-start.24) | collective-permute-done | bytes 196640 | tf_op jit(solution)/shard_map/ppermute | solution.py:80
  91.6 0.1 collective-permute-start.25
  91.7 1.3 %collective-permute-done.25.rest_1_ = bf16[32,1536]{1,0:T(8,128)(2,1)S(1)} collective-permute-done((bf16[32,1536]{1,0:T(8,128)(2,1)S(1)}, bf16[32,1536]{1,0:T(8,128)(2,1)S(1)}, u32[]{:S(2)}, u32[]{:S(2)}) %collective-permute-start.25) | collective-permute-done | bytes 98336 | tf_op jit(solution)/shard_map/ppermute | solution.py:76
  92.9 0.8 slice-done.2
  93.8 5.4 %gate_score.1 = bf16[2048,3072]{1,0:T(8,128)(2,1)} custom-call(bf16[64,2048]{1,0:T(8,128)(2,1)S(1)} %bitcast.35, bf16[32,1536]{1,0:T(8,128)(2,1)S(1)} %combined.2.rest_0_, bf16[32,1536]{1,0:T(8,128)(2,1)S(1)} %collective-permute-done.25.rest_1_, bf16[32,1536]{1,0:T(8,128)(2,1)S(1)} %combined.3.rest_2_, bf16[32,1536]{1,0:T(8,128)(2,1)S(1)} %collective-permute-done.28.rest_3_, ...), custom_call_target="tpu_custom_call" | custom-call | flops 805306368 | bytes 25165824 | tf_op jit(solution)/shard_map/gate_score/pallas_call | solution.py:512
  (54 shorter events, 0.7 us)
Async XLA Ops:
  1.8 6.3 %collective-permute-start = (bf16[1,8,2048]{2,1,0:T(8,128)(2,1)S(1)}, bf16[1,8,2048]{2,1,0:T(8,128)(2,1)S(1)}, u32[]{:S(2)}, u32[]{:S(2)}) collective-permute-start(bf16[1,8,2048]{2,1,0:T(8,128)(2,1)S(1)} %norm_rows.1.refs_0_), channel_id=1, source_target_pairs={{0,16},{4,20},{8,24},{12,28},{16,0},{20,4},{24,8},{28,12},{1,17},{... | collective-permute-start | bytes 98312 | tf_op jit(solution)/shard_map/ppermute | solution.py:533
  8.1 3.9 %collective-permute-start.1 = (bf16[2,8,1024]{2,1,0:T(8,128)(2,1)S(1)}, bf16[2,8,1024]{2,1,0:T(8,128)(2,1)S(1)}, u32[]{:S(2)}, u32[]{:S(2)}) collective-permute-start(bf16[2,8,1024]{2,1,0:T(8,128)(2,1)S(1)} %get-tuple-element.31.refs_0_), channel_id=1, source_target_pairs={{0,8},{4,12},{8,0},{12,4},{16,24},{20,28},{24,16},{28,20},{1,9},{5... | collective-permute-start | bytes 98312 | tf_op jit(solution)/shard_map/ppermute | solution.py:533
  9.7 9.3 %slice-start.3 = ((s8[12582912]{0:T(1024)(128)(4,1)}), s8[4194304]{0:T(1024)(128)(4,1)S(1)}, s32[]{:S(2)}) async-start(s8[12582912]{0:T(1024)(128)(4,1)} %bitcast.28), calls=%async_computation.3 | async-start | bytes 8388608
  9.7 9.3 %slice-start.6 = ((s8[12582912]{0:T(1024)(128)(4,1)}), s8[4194304]{0:T(1024)(128)(4,1)S(1)}, s32[]{:S(2)}) async-start(s8[12582912]{0:T(1024)(128)(4,1)} %bitcast.30), calls=%async_computation.6 | async-start | bytes 8388608
  9.7 9.3 %slice-start.4 = ((s8[12582912]{0:T(1024)(128)(4,1)}), s8[4194304]{0:T(1024)(128)(4,1)S(1)}, s32[]{:S(2)}) async-start(s8[12582912]{0:T(1024)(128)(4,1)} %bitcast.28), calls=%async_computation.4 | async-start | bytes 8388608
  9.7 9.4 %slice-start.5 = ((s8[12582912]{0:T(1024)(128)(4,1)}), s8[4194304]{0:T(1024)(128)(4,1)S(1)}, s32[]{:S(2)}) async-start(s8[12582912]{0:T(1024)(128)(4,1)} %bitcast.28), calls=%async_computation.5 | async-start | bytes 8388608
  9.7 9.4 %slice-start.7 = ((s8[12582912]{0:T(1024)(128)(4,1)}), s8[4194304]{0:T(1024)(128)(4,1)S(1)}, s32[]{:S(2)}) async-start(s8[12582912]{0:T(1024)(128)(4,1)} %bitcast.30), calls=%async_computation.7 | async-start | bytes 8388608
  9.7 9.5 %slice-start.8 = ((s8[12582912]{0:T(1024)(128)(4,1)}), s8[4194304]{0:T(1024)(128)(4,1)S(1)}, s32[]{:S(2)}) async-start(s8[12582912]{0:T(1024)(128)(4,1)} %bitcast.30), calls=%async_computation.8 | async-start | bytes 8388608
  9.7 4.0 %collective-permute-start.2 = (bf16[2,8,1024]{2,1,0:T(8,128)(2,1)S(1)}, bf16[2,8,1024]{2,1,0:T(8,128)(2,1)S(1)}, u32[]{:S(2)}, u32[]{:S(2)}) collective-permute-start(bf16[2,8,1024]{2,1,0:T(8,128)(2,1)S(1)} %get-tuple-element.32.refs_1_), channel_id=1, source_target_pairs={{0,4},{4,0},{8,12},{12,8},{16,20},{20,16},{24,28},{28,24},{1,5},{5... | collective-permute-start | bytes 98312 | tf_op jit(solution)/shard_map/ppermute | solution.py:533
  13.7 5.2 %collective-permute-start.4 = (bf16[4,8,1024]{2,1,0:T(8,128)(2,1)S(1)}, bf16[4,8,1024]{2,1,0:T(8,128)(2,1)S(1)}, u32[]{:S(2)}, u32[]{:S(2)}) collective-permute-start(bf16[4,8,1024]{2,1,0:T(8,128)(2,1)S(1)} %get-tuple-element.34.b0), channel_id=1, source_target_pairs={{0,8},{4,12},{8,0},{12,4},{16,24},{20,28},{24,16},{28,20},{1,9},{5... | collective-permute-start | bytes 196616 | tf_op jit(solution)/shard_map/ppermute | solution.py:533
  14.2 4.7 %collective-permute-start.3 = (bf16[4,8,1024]{2,1,0:T(8,128)(2,1)S(1)}, bf16[4,8,1024]{2,1,0:T(8,128)(2,1)S(1)}, u32[]{:S(2)}, u32[]{:S(2)}) collective-permute-start(bf16[4,8,1024]{2,1,0:T(8,128)(2,1)S(1)} %get-tuple-element.33.refs_1_.a0), channel_id=1, source_target_pairs={{0,4},{4,0},{8,12},{12,8},{16,20},{20,16},{24,28},{28,24},{1,5},{5... | collective-permute-start | bytes 196616 | tf_op jit(solution)/shard_map/ppermute | solution.py:533
  21.5 3.9 %collective-permute-start.5 = (bf16[3,32,1024]{2,1,0:T(8,128)(2,1)S(1)}, bf16[3,32,1024]{2,1,0:T(8,128)(2,1)S(1)}, u32[]{:S(2)}, u32[]{:S(2)}) collective-permute-start(bf16[3,32,1024]{2,1,0:T(8,128)(2,1)S(1)} %get-tuple-element.36), channel_id=1, source_target_pairs={{0,1},{1,0},{2,3},{3,2},{4,5},{5,4},{6,7},{7,6},{8,9},{9,8},{10,11... | collective-permute-start | bytes 589832 | tf_op jit(solution)/shard_map/ppermute | solution.py:76
  24.8 5.5 %collective-permute-start.8 = (bf16[3,32,1024]{2,1,0:T(8,128)(2,1)S(1)}, bf16[3,32,1024]{2,1,0:T(8,128)(2,1)S(1)}, u32[]{:S(2)}, u32[]{:S(2)}) collective-permute-start(bf16[3,32,1024]{2,1,0:T(8,128)(2,1)S(1)} %get-tuple-element.39), channel_id=1, source_target_pairs={{0,1},{1,0},{2,3},{3,2},{4,5},{5,4},{6,7},{7,6},{8,9},{9,8},{10,11... | collective-permute-start | bytes 589832 | tf_op jit(solution)/shard_map/ppermute | solution.py:76
  25.5 7.2 %collective-permute-start.6 = (bf16[3,32,1024]{2,1,0:T(8,128)(2,1)S(1)}, bf16[3,32,1024]{2,1,0:T(8,128)(2,1)S(1)}, u32[]{:S(2)}, u32[]{:S(2)}) collective-permute-start(bf16[3,32,1024]{2,1,0:T(8,128)(2,1)S(1)} %get-tuple-element.68.rest_0_), channel_id=1, source_target_pairs={{0,2},{1,3},{2,0},{3,1},{4,6},{5,7},{6,4},{7,5},{8,10},{9,11},{10,... | collective-permute-start | bytes 589832 | tf_op jit(solution)/shard_map/ppermute | solution.py:80
  30.3 1.5 %collective-permute-start.10 = (bf16[3,32,1024]{2,1,0:T(8,128)(2,1)S(1)}, bf16[3,32,1024]{2,1,0:T(8,128)(2,1)S(1)}, u32[]{:S(2)}, u32[]{:S(2)}) collective-permute-start(bf16[3,32,1024]{2,1,0:T(8,128)(2,1)S(1)} %get-tuple-element.41), channel_id=1, source_target_pairs={{0,1},{1,0},{2,3},{3,2},{4,5},{5,4},{6,7},{7,6},{8,9},{9,8},{10,11... | collective-permute-start | bytes 589832 | tf_op jit(solution)/shard_map/ppermute | solution.py:76
  30.4 10.8 %collective-permute-start.9 = (bf16[3,32,1024]{2,1,0:T(8,128)(2,1)S(1)}, bf16[3,32,1024]{2,1,0:T(8,128)(2,1)S(1)}, u32[]{:S(2)}, u32[]{:S(2)}) collective-permute-start(bf16[3,32,1024]{2,1,0:T(8,128)(2,1)S(1)} %get-tuple-element.66), channel_id=1, source_target_pairs={{0,2},{1,3},{2,0},{3,1},{4,6},{5,7},{6,4},{7,5},{8,10},{9,11},{10,... | collective-permute-start | bytes 589832 | tf_op jit(solution)/shard_map/ppermute | solution.py:80
  31.8 10.2 %collective-permute-start.12 = (bf16[3,32,1024]{2,1,0:T(8,128)(2,1)S(1)}, bf16[3,32,1024]{2,1,0:T(8,128)(2,1)S(1)}, u32[]{:S(2)}, u32[]{:S(2)}) collective-permute-start(bf16[3,32,1024]{2,1,0:T(8,128)(2,1)S(1)} %get-tuple-element.64.refs_2_), channel_id=1, source_target_pairs={{0,2},{1,3},{2,0},{3,1},{4,6},{5,7},{6,4},{7,5},{8,10},{9,11},{10,... | collective-permute-start | bytes 589832 | tf_op jit(solution)/shard_map/ppermute | solution.py:80
  32.8 9.4 %collective-permute-start.7 = (bf16[2,32,1024]{2,1,0:T(8,128)(2,1)S(1)}, bf16[2,32,1024]{2,1,0:T(8,128)(2,1)S(1)}, u32[]{:S(2)}, u32[]{:S(2)}) collective-permute-start(bf16[2,32,1024]{2,1,0:T(8,128)(2,1)S(1)} %get-tuple-element.37.refs_0_), channel_id=1, source_target_pairs={{0,1},{1,0},{2,3},{3,2},{4,5},{5,4},{6,7},{7,6},{8,9},{9,8},{10,11... | collective-permute-start | bytes 393224 | tf_op jit(solution)/shard_map/ppermute | solution.py:76
  41.3 1.5 %collective-permute-start.11 = (bf16[2,32,1024]{2,1,0:T(8,128)(2,1)S(1)}, bf16[2,32,1024]{2,1,0:T(8,128)(2,1)S(1)}, u32[]{:S(2)}, u32[]{:S(2)}) collective-permute-start(bf16[2,32,1024]{2,1,0:T(8,128)(2,1)S(1)} %get-tuple-element.43.refs_2_), channel_id=1, source_target_pairs={{0,1},{1,0},{2,3},{3,2},{4,5},{5,4},{6,7},{7,6},{8,9},{9,8},{10,11... | collective-permute-start | bytes 393224 | tf_op jit(solution)/shard_map/ppermute | solution.py:76
  42.1 1.4 %collective-permute-start.13 = (bf16[2,32,1024]{2,1,0:T(8,128)(2,1)S(1)}, bf16[2,32,1024]{2,1,0:T(8,128)(2,1)S(1)}, u32[]{:S(2)}, u32[]{:S(2)}) collective-permute-start(bf16[2,32,1024]{2,1,0:T(8,128)(2,1)S(1)} %get-tuple-element.44.refs_4_), channel_id=1, source_target_pairs={{0,1},{1,0},{2,3},{3,2},{4,5},{5,4},{6,7},{7,6},{8,9},{9,8},{10,11... | collective-permute-start | bytes 393224 | tf_op jit(solution)/shard_map/ppermute | solution.py:76
  45.7 5.6 %collective-permute-start.14 = (bf16[2,2,64,256]{3,2,1,0:T(8,128)(2,1)S(1)}, bf16[2,2,64,256]{3,2,1,0:T(8,128)(2,1)S(1)}, u32[]{:S(2)}, u32[]{:S(2)}) collective-permute-start(bf16[2,2,64,256]{3,2,1,0:T(8,128)(2,1)S(1)} %get-tuple-element.47), channel_id=1, source_target_pairs={{0,4},{4,0},{8,12},{12,8},{16,20},{20,16},{24,28},{28,24},{1,5},{5... | collective-permute-start | bytes 393224 | tf_op jit(solution)/shard_map/ppermute | solution.py:533
  47.3 17.0 %copy-start = (bf16[64,2048]{1,0:T(8,128)(2,1)S(1)}, bf16[64,2048]{1,0:T(8,128)(2,1)}, u32[]{:S(2)}) copy-start(bf16[64,2048]{1,0:T(8,128)(2,1)} %target_ref.1) | copy-start | bytes 786436
  47.3 5.3 %collective-permute-start.16 = (bf16[2,2,64,256]{3,2,1,0:T(8,128)(2,1)S(1)}, bf16[2,2,64,256]{3,2,1,0:T(8,128)(2,1)S(1)}, u32[]{:S(2)}, u32[]{:S(2)}) collective-permute-start(bf16[2,2,64,256]{3,2,1,0:T(8,128)(2,1)S(1)} %get-tuple-element.49), channel_id=1, source_target_pairs={{0,8},{4,12},{8,0},{12,4},{16,24},{20,28},{24,16},{28,20},{1,9},{5... | collective-permute-start | bytes 393224 | tf_op jit(solution)/shard_map/ppermute | solution.py:533
  51.3 4.3 %collective-permute-start.15 = (bf16[2,64,256]{2,1,0:T(8,128)(2,1)S(1)}, bf16[2,64,256]{2,1,0:T(8,128)(2,1)S(1)}, u32[]{:S(2)}, u32[]{:S(2)}) collective-permute-start(bf16[2,64,256]{2,1,0:T(8,128)(2,1)S(1)} %fusion.4), channel_id=1, source_target_pairs={{0,8},{4,12},{8,0},{12,4},{16,24},{20,28},{24,16},{28,20},{1,9},{5... | collective-permute-start | bytes 196616 | tf_op jit(solution)/shard_map/ppermute | solution.py:533
  52.6 4.3 %collective-permute-start.17 = (bf16[2,64,256]{2,1,0:T(8,128)(2,1)S(1)}, bf16[2,64,256]{2,1,0:T(8,128)(2,1)S(1)}, u32[]{:S(2)}, u32[]{:S(2)}) collective-permute-start(bf16[2,64,256]{2,1,0:T(8,128)(2,1)S(1)} %fusion.5), channel_id=1, source_target_pairs={{0,4},{4,0},{8,12},{12,8},{16,20},{20,16},{24,28},{28,24},{1,5},{5... | collective-permute-start | bytes 196616 | tf_op jit(solution)/shard_map/ppermute | solution.py:533
  57.0 7.3 %collective-permute-start.18 = (bf16[2,2,64,256]{3,2,1,0:T(8,128)(2,1)S(1)}, bf16[2,2,64,256]{3,2,1,0:T(8,128)(2,1)S(1)}, u32[]{:S(2)}, u32[]{:S(2)}) collective-permute-start(bf16[2,2,64,256]{3,2,1,0:T(8,128)(2,1)S(1)} %fusion.6), channel_id=1, source_target_pairs={{0,16},{4,20},{8,24},{12,28},{16,0},{20,4},{24,8},{28,12},{1,17},{... | collective-permute-start | bytes 393224 | tf_op jit(solution)/shard_map/ppermute | solution.py:533
  64.3 4.8 %collective-permute-start.20 = (bf16[2,64,256]{2,1,0:T(8,128)(2,1)S(1)}, bf16[2,64,256]{2,1,0:T(8,128)(2,1)S(1)}, u32[]{:S(2)}, u32[]{:S(2)}) collective-permute-start(bf16[2,64,256]{2,1,0:T(8,128)(2,1)S(1)} %get-tuple-element.51), channel_id=1, source_target_pairs={{0,4},{4,0},{8,12},{12,8},{16,20},{20,16},{24,28},{28,24},{1,5},{5... | collective-permute-start | bytes 196616 | tf_op jit(solution)/shard_map/ppermute | solution.py:533
  65.8 4.3 %collective-permute-start.19 = (bf16[2,64,256]{2,1,0:T(8,128)(2,1)S(1)}, bf16[2,64,256]{2,1,0:T(8,128)(2,1)S(1)}, u32[]{:S(2)}, u32[]{:S(2)}) collective-permute-start(bf16[2,64,256]{2,1,0:T(8,128)(2,1)S(1)} %get-tuple-element.50), channel_id=1, source_target_pairs={{0,8},{4,12},{8,0},{12,4},{16,24},{20,28},{24,16},{28,20},{1,9},{5... | collective-permute-start | bytes 196616 | tf_op jit(solution)/shard_map/ppermute | solution.py:533
  69.1 5.7 %collective-permute-start.22 = (bf16[2,2,64,256]{3,2,1,0:T(8,128)(2,1)S(1)}, bf16[2,2,64,256]{3,2,1,0:T(8,128)(2,1)S(1)}, u32[]{:S(2)}, u32[]{:S(2)}) collective-permute-start(bf16[2,2,64,256]{3,2,1,0:T(8,128)(2,1)S(1)} %pad_maximum_fusion.2.b_ref), channel_id=1, source_target_pairs={{0,8},{4,12},{8,0},{12,4},{16,24},{20,28},{24,16},{28,20},{1,9},{5... | collective-permute-start | bytes 393224 | tf_op jit(solution)/shard_map/ppermute | solution.py:533
  70.1 5.0 %collective-permute-start.21 = (bf16[2,2,64,256]{3,2,1,0:T(8,128)(2,1)S(1)}, bf16[2,2,64,256]{3,2,1,0:T(8,128)(2,1)S(1)}, u32[]{:S(2)}, u32[]{:S(2)}) collective-permute-start(bf16[2,2,64,256]{3,2,1,0:T(8,128)(2,1)S(1)} %pad_maximum_fusion.1.a_ref), channel_id=1, source_target_pairs={{0,4},{4,0},{8,12},{12,8},{16,20},{20,16},{24,28},{28,24},{1,5},{5... | collective-permute-start | bytes 393224 | tf_op jit(solution)/shard_map/ppermute | solution.py:533
  77.4 3.0 %collective-permute-start.26 = (bf16[2,32,1536]{2,1,0:T(8,128)(2,1)S(1)}, bf16[2,32,1536]{2,1,0:T(8,128)(2,1)S(1)}, u32[]{:S(2)}, u32[]{:S(2)}) collective-permute-start(bf16[2,32,1536]{2,1,0:T(8,128)(2,1)S(1)} %get-tuple-element.59), channel_id=1, source_target_pairs={{0,1},{1,0},{2,3},{3,2},{4,5},{5,4},{6,7},{7,6},{8,9},{9,8},{10,11... | collective-permute-start | bytes 589832 | tf_op jit(solution)/shard_map/ppermute | solution.py:76
  79.8 1.9 %collective-permute-start.23 = (bf16[2,32,1536]{2,1,0:T(8,128)(2,1)S(1)}, bf16[2,32,1536]{2,1,0:T(8,128)(2,1)S(1)}, u32[]{:S(2)}, u32[]{:S(2)}) collective-permute-start(bf16[2,32,1536]{2,1,0:T(8,128)(2,1)S(1)} %get-tuple-element.53), channel_id=1, source_target_pairs={{0,1},{1,0},{2,3},{3,2},{4,5},{5,4},{6,7},{7,6},{8,9},{9,8},{10,11... | collective-permute-start | bytes 589832 | tf_op jit(solution)/shard_map/ppermute | solution.py:76
  80.4 7.8 %collective-permute-start.27 = (bf16[2,32,1536]{2,1,0:T(8,128)(2,1)S(1)}, bf16[2,32,1536]{2,1,0:T(8,128)(2,1)S(1)}, u32[]{:S(2)}, u32[]{:S(2)}) collective-permute-start(bf16[2,32,1536]{2,1,0:T(8,128)(2,1)S(1)} %get-tuple-element.60), channel_id=1, source_target_pairs={{0,2},{1,3},{2,0},{3,1},{4,6},{5,7},{6,4},{7,5},{8,10},{9,11},{10,... | collective-permute-start | bytes 589832 | tf_op jit(solution)/shard_map/ppermute | solution.py:80
  81.7 9.8 %collective-permute-start.24 = (bf16[2,32,1536]{2,1,0:T(8,128)(2,1)S(1)}, bf16[2,32,1536]{2,1,0:T(8,128)(2,1)S(1)}, u32[]{:S(2)}, u32[]{:S(2)}) collective-permute-start(bf16[2,32,1536]{2,1,0:T(8,128)(2,1)S(1)} %get-tuple-element.62), channel_id=1, source_target_pairs={{0,2},{1,3},{2,0},{3,1},{4,6},{5,7},{6,4},{7,5},{8,10},{9,11},{10,... | collective-permute-start | bytes 589832 | tf_op jit(solution)/shard_map/ppermute | solution.py:80
  88.2 4.7 %slice-start = ((s8[12582912]{0:T(1024)(128)(4,1)}), s8[4194304]{0:T(1024)(128)(4,1)S(1)}, s32[]{:S(2)}) async-start(s8[12582912]{0:T(1024)(128)(4,1)} %bitcast.26), calls=%async_computation | async-start | bytes 8388608
  88.2 4.7 %slice-start.1 = ((s8[12582912]{0:T(1024)(128)(4,1)}), s8[4194304]{0:T(1024)(128)(4,1)S(1)}, s32[]{:S(2)}) async-start(s8[12582912]{0:T(1024)(128)(4,1)} %bitcast.26), calls=%async_computation.1 | async-start | bytes 8388608
  88.3 3.4 %collective-permute-start.28 = (bf16[32,1536]{1,0:T(8,128)(2,1)S(1)}, bf16[32,1536]{1,0:T(8,128)(2,1)S(1)}, u32[]{:S(2)}, u32[]{:S(2)}) collective-permute-start(bf16[32,1536]{1,0:T(8,128)(2,1)S(1)} %combined.3.rest_2_), channel_id=1, source_target_pairs={{0,1},{1,0},{2,3},{3,2},{4,5},{5,4},{6,7},{7,6},{8,9},{9,8},{10,11... | collective-permute-start | bytes 294920 | tf_op jit(solution)/shard_map/ppermute | solution.py:76
  91.5 2.2 %slice-start.2 = ((s8[12582912]{0:T(1024)(128)(4,1)}), s8[4194304]{0:T(1024)(128)(4,1)S(1)}, s32[]{:S(2)}) async-start(s8[12582912]{0:T(1024)(128)(4,1)} %bitcast.26), calls=%async_computation.2 | async-start | bytes 8388608
  91.6 1.4 %collective-permute-start.25 = (bf16[32,1536]{1,0:T(8,128)(2,1)S(1)}, bf16[32,1536]{1,0:T(8,128)(2,1)S(1)}, u32[]{:S(2)}, u32[]{:S(2)}) collective-permute-start(bf16[32,1536]{1,0:T(8,128)(2,1)S(1)} %combined.2.rest_0_), channel_id=1, source_target_pairs={{0,1},{1,0},{2,3},{3,2},{4,5},{5,4},{6,7},{7,6},{8,9},{9,8},{10,11... | collective-permute-start | bytes 294920 | tf_op jit(solution)/shard_map/ppermute | solution.py:76

commit v6 on v5

--- a/solution.py
+++ b/solution.py
@@ -445,35 +445,37 @@
     )(*hiddens, residuals, held(v_down))
 
 
-def combine_call(chip_sum, arrived, factors, chunk, after):
-    half, width = chip_sum.shape[1:]
-    part = factors[0].shape[2]
-    block = block_of(math.gcd(width, part), 512)
-    n = len(factors)
-
-    def body(sum_ref, arrived_ref, *rest):
-        factor_refs, out_ref = rest[:n], rest[-1]
-        for j in range(width // block):
-            span = slice(j * block, (j + 1) * block)
+def combine_call(sums, arrived, factors, after):
+    n, m = len(sums), len(factors)
+    half, part = sums[0].shape[1:]
+    width = n * part
+    factor_part = factors[0].shape[2]
+    block = block_of(math.gcd(part, factor_part), 512)
+
+    def body(*refs):
+        sum_refs, arrived_refs, factor_refs = refs[:n], refs[n : 2 * n], refs[2 * n : 2 * n + m]
+        out_ref = refs[-1]
+        for at in range(0, width, block):
+            span = slice(at % part, at % part + block)
             back_grad, back_tangent = [
-                sum_ref[i, :, span] + arrived_ref[i, :, span].astype(f32) for i in range(2)
+                sum_refs[at // part][i, :, span] + arrived_refs[at // part][i, :, span].astype(f32)
+                for i in range(2)
             ]
-            at = chunk * width + j * block
-            factor_ref, start = factor_refs[at // part], at % part
-            taken = slice(start, start + block)
-            out_ref[:, span] = (
+            factor_ref = factor_refs[at // factor_part]
+            taken = slice(at % factor_part, at % factor_part + block)
+            out_ref[:, at : at + block] = (
                 back_tangent * factor_ref[0, :, taken] + back_grad * factor_ref[1, :, taken]
             ).astype(bf16)
 
     return pl.pallas_call(
         body,
-        in_specs=[IN_VMEM] * (n + 2) + [pl.BlockSpec(memory_space=pl.ANY)],
+        in_specs=[IN_VMEM] * (2 * n + m) + [pl.BlockSpec(memory_space=pl.ANY)],
         out_specs=IN_VMEM,
         out_shape=jax.ShapeDtypeStruct((half, width), bf16),
         compiler_params=params(8),
         cost_estimate=cost(0, 22 * half * width),
         name="combined",
-    )(chip_sum, arrived, *factors, kept_out(after))
+    )(*sums, *arrived, *factors, kept_out(after))
 
 
 def gate_score_call(normed, combined, v_gate):
@@ -533,17 +535,19 @@
     return lax.ppermute(value, "dp", [(i, i ^ bit) for i in range(8)])
 
 
-def piece_call(hiddens, w_down, v_down, away, dtype):
+def piece_call(hiddens, w_down, v_down, away, dtype, groups, after=None):
     count = 2 * hiddens[0].shape[1]
     rows, features = w_down.shape
     n = len(hiddens)
     piece = features // 8
 
     def body(*refs):
-        w_ref, v_ref, a_ref, b_ref, left = refs[n:]
+        w_ref, v_ref = refs[n : n + 2]
+        out_refs, left = refs[-1 - len(groups) : -1], refs[-1]
         y, z = bits()
         join_hidden(refs[:n], left)
-        for out_ref, base, outer, inner in ((a_ref, 0, y, z), (b_ref, 4, z, y)):
+        for out_ref, kind in zip(out_refs, groups):
+            base, outer, inner = ((0, y, z), (4, z, y))[kind]
             group = 1 - outer if away else outer
             for k, low in enumerate((1 - inner, inner)):
                 first = pl.multiple_of((base + 2 * group + low) * piece, piece)
@@ -553,16 +557,18 @@
                 out_ref[k, 1] = tangent.astype(dtype)
 
     shape = jax.ShapeDtypeStruct((2, 2, count, piece), dtype)
-    return pl.pallas_call(
-        body,
-        in_specs=[IN_VMEM] * (n + 2),
-        out_specs=[IN_VMEM] * 2,
-        out_shape=[shape, shape],
+    operands, in_specs = [*hiddens, held(w_down), held(v_down)], [IN_VMEM] * (n + 2)
+    order(operands, in_specs, after)
+    return pl.pallas_call(
+        body,
+        in_specs=in_specs,
+        out_specs=[IN_VMEM] * len(groups),
+        out_shape=[shape] * len(groups),
         scratch_shapes=[pltpu.VMEM((2 * count, rows), bf16)],
         compiler_params=params(8),
         cost_estimate=cost(3 * count * rows * features, 2 * rows * features),
         name="pieces_away" if away else "pieces_home",
-    )(*hiddens, held(w_down), held(v_down))
+    )(*operands)
 
 
 def residual_call(sums, arrived, target):
@@ -689,9 +695,10 @@
 
 
 def middle_tree(hiddens, target, w_down, v_down, chunks):
-    a_send, b_send = piece_call(hiddens, w_down, v_down, True, bf16)
+    (a_send,) = piece_call(hiddens, w_down, v_down, True, bf16, (0,))
+    (b_send,) = piece_call(hiddens, w_down, v_down, True, bf16, (1,), a_send)
     a_recv, b_recv = swap_dp(a_send, 1), swap_dp(b_send, 2)
-    a_home, b_home = piece_call(hiddens, w_down, v_down, False, f32)
+    a_home, b_home = piece_call(hiddens, w_down, v_down, False, f32, (0, 1))
     a_sum = a_home + a_recv.astype(f32)
     b_sum = b_home + b_recv.astype(f32)
     a_recv, b_recv = swap_dp(a_sum[0].astype(bf16), 2), swap_dp(b_sum[0].astype(bf16), 1)
@@ -773,10 +780,8 @@
         sums, residuals = middle_direct(dp, hiddens, target, w_down, v_down)
     arrived = [swap_chip(send) for _, send in sums]
     down_score = down_score_call(hiddens, residuals, v_down)
-    combined = []
-    for chunk, ((chip_sum, _), came) in enumerate(zip(sums, arrived)):
-        mine = combine_call(chip_sum, came, factors, chunk, down_score)
-        combined += [mine, swap_core(mine)]
+    mine = combine_call([chip_sum for chip_sum, _ in sums], arrived, factors, down_score)
+    combined = [mine, swap_core(mine)]
     gate_score = gate_score_call(normed, combined, v_gate)
     return (gate_score, down_score)
 

time: 99.4 us -> 99.1 us (level)
  Pallas kernels: 45.1 us -> 46.7 us
  starting transfers between devices: 28 us -> 26.5 us
    ppermute x14, starting transfers between devices: 20.6 us -> 19.1 us  [swap_dp(): return lax.ppermute(value, 'dp', [(i, i ^ bit) for i in range(8)])]
    pallas_call x1, Pallas kernels: 5.36 us -> 6.77 us  [down_score_call(): pl.pallas_call(body, in_specs=[IN_VMEM] * (n + 2), out_specs=IN_HBM, out_...]
    ppermute x5, waiting for transfers between devices: 3.4 us -> 2.12 us  [swap_chip(): return lax.ppermute(value, 'mp', [(i, i ^ 2) for i in range(4)])]
    ppermute x10 -> x9, waiting for transfers between devices: 3.37 us -> 3.53 us  [swap_core(): return lax.ppermute(value, 'mp', [(i, i ^ 1) for i in range(4)])]
    ppermute x10 -> x9, starting transfers between devices: 2.16 us -> 2.1 us  [swap_core(): return lax.ppermute(value, 'mp', [(i, i ^ 1) for i in range(4)])]
  transfers between devices with their start and end apart: 29 -> 28, of which waited for: 18 -> 14; matrix products, arithmetic and copies ran while one was open for 0% -> 0% of each run, Pallas kernels for 32% -> 35%
where the time goes in v6:
time: 99.1 us; the launch traced here: 98.9 us
  Pallas kernels  46.7 us (47%)
  starting transfers between devices  26.5 us (27%)
  waiting for transfers between devices  23.4 us (24%)
  between operations  1.25 us (1%)
    ppermute x14, starting transfers between devices, swap_dp(): return lax.ppermute(value, 'dp', [(i, i ^ bit) for i in range(8)])  19.1 us
    ppermute x14, waiting for transfers between devices, swap_dp(): return lax.ppermute(value, 'dp', [(i, i ^ bit) for i in range(8)])  17.7 us
    pallas_call x2, Pallas kernels, load_call(): pl.pallas_call(body, in_specs=[IN_HBM] * n + [pl.BlockSpec(memory_space=p...  11.3 us
    pallas_call x3, Pallas kernels, gate_held_call(): pl.pallas_call(body, in_specs=in_specs, out_specs=[IN_VMEM] * 2, out_shap...  8.79 us
    pallas_call x1, Pallas kernels, down_score_call(): pl.pallas_call(body, in_specs=[IN_VMEM] * (n + 2), out_specs=IN_HBM, out_...  6.77 us
    pallas_call x1, Pallas kernels, gate_score_call(): pl.pallas_call(body, in_specs=[IN_VMEM] * (n + 2), out_specs=IN_HBM, out_...  5.36 us
    ppermute x5, starting transfers between devices, swap_chip(): return lax.ppermute(value, 'mp', [(i, i ^ 2) for i in range(4)])  5.22 us
    pallas_call x2, Pallas kernels, back_second_call(): pl.pallas_call(body, in_specs=[IN_VMEM] * 7, out_specs=[IN_VMEM] * len(ou...  4.62 us
  transfers between devices with their start and end apart: 28, of which 14 were waited for; matrix products, arithmetic and copies ran while one was open for 0% of the time, Pallas kernels for 35%

profile of v6, /device:TPU:0, one launch (start us, length us, event | category | flops | bytes accessed | tf_op | source)
XLA Modules:
  0.0 98.9 jit_solution(9612008368713112178)
XLA Ops:
  0.6 1.1 %norm_rows.1.refs_0_ = bf16[1,8,2048]{2,1,0:T(8,128)(2,1)S(1)} custom-call(bf16[8,8192]{1,0:T(8,128)(2,1)} %tokens_ref.1, f32[1,8192]{1,0:T(1,128)} %bitcast.40), custom_call_target="tpu_custom_call" | custom-call | flops 15000000512 | bytes 262144 | tf_op jit(solution)/shard_map/norm_rows/pallas_call | solution.py:138
  1.8 4.1 %collective-permute-start = (bf16[1,8,2048]{2,1,0:T(8,128)(2,1)S(1)}, bf16[1,8,2048]{2,1,0:T(8,128)(2,1)S(1)}, u32[]{:S(2)}, u32[]{:S(2)}) collective-permute-start(bf16[1,8,2048]{2,1,0:T(8,128)(2,1)S(1)} %norm_rows.1.refs_0_), channel_id=1, source_target_pairs={{0,16},{4,20},{8,24},{12,28},{16,0},{20,4},{24,8},{28,12},{1,17},{... | collective-permute-start | bytes 98312 | tf_op jit(solution)/shard_map/ppermute | solution.py:535
  5.9 2.2 %collective-permute-done.refs_1_ = bf16[1,8,2048]{2,1,0:T(8,128)(2,1)S(1)} collective-permute-done((bf16[1,8,2048]{2,1,0:T(8,128)(2,1)S(1)}, bf16[1,8,2048]{2,1,0:T(8,128)(2,1)S(1)}, u32[]{:S(2)}, u32[]{:S(2)}) %collective-permute-start) | collective-permute-done | bytes 32800 | tf_op jit(solution)/shard_map/ppermute | solution.py:535
  8.1 1.6 %collective-permute-start.1 = (bf16[2,8,1024]{2,1,0:T(8,128)(2,1)S(1)}, bf16[2,8,1024]{2,1,0:T(8,128)(2,1)S(1)}, u32[]{:S(2)}, u32[]{:S(2)}) collective-permute-start(bf16[2,8,1024]{2,1,0:T(8,128)(2,1)S(1)} %get-tuple-element.29.refs_0_), channel_id=1, source_target_pairs={{0,8},{4,12},{8,0},{12,4},{16,24},{20,28},{24,16},{28,20},{1,9},{5... | collective-permute-start | bytes 98312 | tf_op jit(solution)/shard_map/ppermute | solution.py:535
  9.7 1.6 %collective-permute-start.2 = (bf16[2,8,1024]{2,1,0:T(8,128)(2,1)S(1)}, bf16[2,8,1024]{2,1,0:T(8,128)(2,1)S(1)}, u32[]{:S(2)}, u32[]{:S(2)}) collective-permute-start(bf16[2,8,1024]{2,1,0:T(8,128)(2,1)S(1)} %get-tuple-element.30.refs_1_), channel_id=1, source_target_pairs={{0,4},{4,0},{8,12},{12,8},{16,20},{20,16},{24,28},{28,24},{1,5},{5... | collective-permute-start | bytes 98312 | tf_op jit(solution)/shard_map/ppermute | solution.py:535
  11.3 0.7 collective-permute-done.1.refs_2_
  12.0 1.7 %collective-permute-done.2.refs_3_ = bf16[2,8,1024]{2,1,0:T(8,128)(2,1)S(1)} collective-permute-done((bf16[2,8,1024]{2,1,0:T(8,128)(2,1)S(1)}, bf16[2,8,1024]{2,1,0:T(8,128)(2,1)S(1)}, u32[]{:S(2)}, u32[]{:S(2)}) %collective-permute-start.2) | collective-permute-done | bytes 32800 | tf_op jit(solution)/shard_map/ppermute | solution.py:535
  13.7 0.5 collective-permute-start.4
  14.2 1.7 %collective-permute-start.3 = (bf16[4,8,1024]{2,1,0:T(8,128)(2,1)S(1)}, bf16[4,8,1024]{2,1,0:T(8,128)(2,1)S(1)}, u32[]{:S(2)}, u32[]{:S(2)}) collective-permute-start(bf16[4,8,1024]{2,1,0:T(8,128)(2,1)S(1)} %get-tuple-element.31.refs_1_.a0), channel_id=1, source_target_pairs={{0,4},{4,0},{8,12},{12,8},{16,20},{20,16},{24,28},{28,24},{1,5},{5... | collective-permute-start | bytes 196616 | tf_op jit(solution)/shard_map/ppermute | solution.py:535
  15.9 3.0 %load_first.1.after_ref.tan_ref = bf16[2048,1024]{1,0:T(8,128)(2,1)S(1)} custom-call(bf16[2048,3072]{1,0:T(8,128)(2,1)} %rest_2_.1, bf16[4,8,1024]{2,1,0:T(8,128)(2,1)S(1)} %get-tuple-element.31.refs_1_.a0), custom_call_target="tpu_custom_call" | custom-call | bytes 8388608 | tf_op jit(solution)/shard_map/load_first/pallas_call | solution.py:106
  19.0 0.1 slice-done.8
  19.2 2.3 %gate_products.3 = (f32[3,32,1024]{2,1,0:T(8,128)S(1)}, bf16[3,32,1024]{2,1,0:T(8,128)(2,1)S(1)}) custom-call(bf16[64,2048]{1,0:T(8,128)(2,1)S(1)} %bitcast.32, bf16[2048,3072]{1,0:T(8,128)(2,1)S(1)} %bitcast.29, bf16[2048,3072]{1,0:T(8,128)(2,1)S(1)} %bitcast.31, bf16[2048,1024]{1,0:T(8,128)(2,1)S(1)} %load_first.1.after_ref.tan_ref), custom_call_target="tpu_custom_call" | custom-call | flops 805306368 | bytes 12582912 | tf_op jit(solution)/shard_map/gate_products/pallas_call | solution.py:293
  21.5 0.1 collective-permute-start.5
  21.6 3.2 %gate_products.4 = (f32[3,32,1024]{2,1,0:T(8,128)S(1)}, bf16[3,32,1024]{2,1,0:T(8,128)(2,1)S(1)}) custom-call(bf16[64,2048]{1,0:T(8,128)(2,1)S(1)} %bitcast.33, bf16[2048,3072]{1,0:T(8,128)(2,1)S(1)} %bitcast.29, bf16[2048,3072]{1,0:T(8,128)(2,1)S(1)} %bitcast.31, bf16[2048,3072]{1,0:T(8,128)(2,1)} %rest_2_.1), custom_call_target="tpu_custom_call" | custom-call | flops 805306368 | bytes 12582912 | tf_op jit(solution)/shard_map/gate_products/pallas_call | solution.py:293
  24.8 0.6 collective-permute-start.8
  25.5 1.6 %collective-permute-start.6 = (bf16[3,32,1024]{2,1,0:T(8,128)(2,1)S(1)}, bf16[3,32,1024]{2,1,0:T(8,128)(2,1)S(1)}, u32[]{:S(2)}, u32[]{:S(2)}) collective-permute-start(bf16[3,32,1024]{2,1,0:T(8,128)(2,1)S(1)} %get-tuple-element.64.rest_0_), channel_id=1, source_target_pairs={{0,2},{1,3},{2,0},{3,1},{4,6},{5,7},{6,4},{7,5},{8,10},{9,11},{10,... | collective-permute-start | bytes 589832 | tf_op jit(solution)/shard_map/ppermute | solution.py:80
  27.0 3.2 %gate_products.5 = (f32[3,32,1024]{2,1,0:T(8,128)S(1)}, bf16[3,32,1024]{2,1,0:T(8,128)(2,1)S(1)}) custom-call(bf16[64,2048]{1,0:T(8,128)(2,1)S(1)} %bitcast.34, bf16[2048,3072]{1,0:T(8,128)(2,1)S(1)} %bitcast.29, bf16[2048,3072]{1,0:T(8,128)(2,1)S(1)} %bitcast.31, bf16[2048,3072]{1,0:T(8,128)(2,1)} %rest_2_.1, bf16[3,32,1024]{2,1,0:T(8,128)(2,1)S(1)} %get-tuple-element.64.rest_0_), custom_call_target="tpu_custom_call" | custom-call | flops 805306368 | bytes 12582912 | tf_op jit(solution)/shard_map/gate_products/pallas_call | solution.py:293
  30.3 0.1 collective-permute-start.10
  30.4 0.6 collective-permute-start.9
  31.0 0.8 collective-permute-done.10
  31.8 0.1 fusion.9
  31.8 0.8 collective-permute-start.12
  32.6 0.1 hidden_units.3
  32.8 0.1 collective-permute-start.7
  32.8 8.3 %load_down.1 = (bf16[3072,2048]{1,0:T(8,128)(2,1)S(1)}, bf16[3072,2048]{1,0:T(8,128)(2,1)S(1)}) custom-call(bf16[3072,2048]{1,0:T(8,128)(2,1)} %refs_0_.3, bf16[3072,2048]{1,0:T(8,128)(2,1)} %refs_1_.1, bf16[3,32,1024]{2,1,0:T(8,128)(2,1)S(1)} %get-tuple-element.60.refs_2_), custom_call_target="tpu_custom_call" | custom-call | bytes 50331648 | tf_op jit(solution)/shard_map/load_down/pallas_call | solution.py:106
  41.2 0.1 hidden_units.4
  41.3 0.6 collective-permute-start.11
  41.9 0.1 collective-permute-done.12.arrived_ref
  42.0 0.1 hidden_units.5
  42.1 0.1 collective-permute-start.13
  42.2 0.6 collective-permute-done.11.refs_3_
  42.8 0.7 collective-permute-done.13.refs_5_
  43.5 1.1 %pieces_away.2.refs_8_ = bf16[2,2,64,256]{3,2,1,0:T(8,128)(2,1)S(1)} custom-call(bf16[2,32,1024]{2,1,0:T(8,128)(2,1)S(1)} %get-tuple-element.35.refs_0_, bf16[2,32,1024]{2,1,0:T(8,128)(2,1)S(1)} %collective-permute-done.7.refs_1_, bf16[2,32,1024]{2,1,0:T(8,128)(2,1)S(1)} %get-tuple-element.41.refs_2_, ...), custom_call_target="tpu_custom_call" | custom-call | flops 1207959552 | bytes 12582912 | tf_op jit(solution)/shard_map/pieces_away/pallas_call | solution.py:562
  44.7 1.6 %collective-permute-start.14 = (bf16[2,2,64,256]{3,2,1,0:T(8,128)(2,1)S(1)}, bf16[2,2,64,256]{3,2,1,0:T(8,128)(2,1)S(1)}, u32[]{:S(2)}, u32[]{:S(2)}) collective-permute-start(bf16[2,2,64,256]{3,2,1,0:T(8,128)(2,1)S(1)} %pieces_away.2.refs_8_), channel_id=1, source_target_pairs={{0,4},{4,0},{8,12},{12,8},{16,20},{20,16},{24,28},{28,24},{1,5},{5... | collective-permute-start | bytes 393224 | tf_op jit(solution)/shard_map/ppermute | solution.py:535
  46.2 1.1 %pieces_away.3 = bf16[2,2,64,256]{3,2,1,0:T(8,128)(2,1)S(1)} custom-call(bf16[2,32,1024]{2,1,0:T(8,128)(2,1)S(1)} %get-tuple-element.35.refs_0_, bf16[2,32,1024]{2,1,0:T(8,128)(2,1)S(1)} %collective-permute-done.7.refs_1_, bf16[2,32,1024]{2,1,0:T(8,128)(2,1)S(1)} %get-tuple-element.41.refs_2_, bf16[2,32,1024]{2,1,0:T(8,128)(2,1)S(1)} %collective-permute-done.11.refs_3_, ...), custom_call_target="tpu_custom_call" | custom-call | flops 1207959552 | bytes 12582912 | tf_op jit(solution)/shard_map/pieces_away/pallas_call | solution.py:562
  47.4 1.0 %collective-permute-start.16 = (bf16[2,2,64,256]{3,2,1,0:T(8,128)(2,1)S(1)}, bf16[2,2,64,256]{3,2,1,0:T(8,128)(2,1)S(1)}, u32[]{:S(2)}, u32[]{:S(2)}) collective-permute-start(bf16[2,2,64,256]{3,2,1,0:T(8,128)(2,1)S(1)} %pieces_away.3), channel_id=1, source_target_pairs={{0,8},{4,12},{8,0},{12,4},{16,24},{20,28},{24,16},{28,20},{1,9},{5... | collective-permute-start | bytes 393224 | tf_op jit(solution)/shard_map/ppermute | solution.py:535
  48.4 2.1 %pieces_home.1 = (f32[2,2,64,256]{3,2,1,0:T(8,128)S(1)}, f32[2,2,64,256]{3,2,1,0:T(8,128)S(1)}) custom-call(bf16[2,32,1024]{2,1,0:T(8,128)(2,1)S(1)} %get-tuple-element.35.refs_0_, bf16[2,32,1024]{2,1,0:T(8,128)(2,1)S(1)} %collective-permute-done.7.refs_1_, bf16[2,32,1024]{2,1,0:T(8,128)(2,1)S(1)} %get-tuple-element.41.refs_2_, ...), custom_call_target="tpu_custom_call" | custom-call | flops 1207959552 | bytes 12582912 | tf_op jit(solution)/shard_map/pieces_home/pallas_call | solution.py:562
  50.6 1.2 %collective-permute-start.15 = (bf16[2,64,256]{2,1,0:T(8,128)(2,1)S(1)}, bf16[2,64,256]{2,1,0:T(8,128)(2,1)S(1)}, u32[]{:S(2)}, u32[]{:S(2)}) collective-permute-start(bf16[2,64,256]{2,1,0:T(8,128)(2,1)S(1)} %fusion.4), channel_id=1, source_target_pairs={{0,8},{4,12},{8,0},{12,4},{16,24},{20,28},{24,16},{28,20},{1,9},{5... | collective-permute-start | bytes 196616 | tf_op jit(solution)/shard_map/ppermute | solution.py:535
  51.8 1.0 collective-permute-done.16
  52.8 0.6 collective-permute-start.17
  53.4 1.6 %collective-permute-done.15 = bf16[2,64,256]{2,1,0:T(8,128)(2,1)S(1)} collective-permute-done((bf16[2,64,256]{2,1,0:T(8,128)(2,1)S(1)}, bf16[2,64,256]{2,1,0:T(8,128)(2,1)S(1)}, u32[]{:S(2)}, u32[]{:S(2)}) %collective-permute-start.15) | collective-permute-done | bytes 65568 | tf_op jit(solution)/shard_map/ppermute | solution.py:535
  55.0 2.2 %collective-permute-done.17 = bf16[2,64,256]{2,1,0:T(8,128)(2,1)S(1)} collective-permute-done((bf16[2,64,256]{2,1,0:T(8,128)(2,1)S(1)}, bf16[2,64,256]{2,1,0:T(8,128)(2,1)S(1)}, u32[]{:S(2)}, u32[]{:S(2)}) %collective-permute-start.17) | collective-permute-done | bytes 65568 | tf_op jit(solution)/shard_map/ppermute | solution.py:535
  57.1 2.9 %collective-permute-start.18 = (bf16[2,2,64,256]{3,2,1,0:T(8,128)(2,1)S(1)}, bf16[2,2,64,256]{3,2,1,0:T(8,128)(2,1)S(1)}, u32[]{:S(2)}, u32[]{:S(2)}) collective-permute-start(bf16[2,2,64,256]{3,2,1,0:T(8,128)(2,1)S(1)} %fusion.6), channel_id=1, source_target_pairs={{0,16},{4,20},{8,24},{12,28},{16,0},{20,4},{24,8},{28,12},{1,17},{... | collective-permute-start | bytes 393224 | tf_op jit(solution)/shard_map/ppermute | solution.py:535
  60.1 4.4 %collective-permute-done.18.arrived_ref = bf16[2,2,64,256]{3,2,1,0:T(8,128)(2,1)S(1)} collective-permute-done((bf16[2,2,64,256]{3,2,1,0:T(8,128)(2,1)S(1)}, bf16[2,2,64,256]{3,2,1,0:T(8,128)(2,1)S(1)}, u32[]{:S(2)}, u32[]{:S(2)}) %collective-permute-start.18) | collective-permute-done | bytes 131104 | tf_op jit(solution)/shard_map/ppermute | solution.py:535
  64.5 0.8 collective-permute-start.20
  65.3 0.2 collective-permute-start.19
  65.5 4.0 %collective-permute-done.20 = bf16[2,64,256]{2,1,0:T(8,128)(2,1)S(1)} collective-permute-done((bf16[2,64,256]{2,1,0:T(8,128)(2,1)S(1)}, bf16[2,64,256]{2,1,0:T(8,128)(2,1)S(1)}, u32[]{:S(2)}, u32[]{:S(2)}) %collective-permute-start.20) | collective-permute-done | bytes 65568 | tf_op jit(solution)/shard_map/ppermute | solution.py:535
  69.5 0.1 collective-permute-start.22
  69.6 1.3 %collective-permute-start.21 = (bf16[2,2,64,256]{3,2,1,0:T(8,128)(2,1)S(1)}, bf16[2,2,64,256]{3,2,1,0:T(8,128)(2,1)S(1)}, u32[]{:S(2)}, u32[]{:S(2)}) collective-permute-start(bf16[2,2,64,256]{3,2,1,0:T(8,128)(2,1)S(1)} %pad_maximum_fusion.1.a_ref), channel_id=1, source_target_pairs={{0,4},{4,0},{8,12},{12,8},{16,20},{20,16},{24,28},{28,24},{1,5},{5... | collective-permute-start | bytes 393224 | tf_op jit(solution)/shard_map/ppermute | solution.py:535
  71.0 3.8 %back_first.1.part_ref = f32[3072,128]{1,0:T(8,128)S(1)} custom-call(bf16[2,2,64,256]{3,2,1,0:T(8,128)(2,1)S(1)} %pad_maximum_fusion.1.a_ref, bf16[2,2,64,256]{3,2,1,0:T(8,128)(2,1)S(1)} %pad_maximum_fusion.2.b_ref, bf16[3072,2048]{1,0:T(8,128)(2,1)S(1)} %get-tuple-element.40.rest_0_.refs_6_.w_ref, bf16[3072,2048]{1,0:T(8,128)(2,1)S(1)} %get-tuple-element.43.refs_7_.v_ref), custom_call_target="tpu_custom_call" | custom-call | flops 603979776 | bytes 6291456 | tf_op jit(solution)/shard_map/back_first/pallas_call | solution.py:629
  74.8 2.3 %back_second.3 = (f32[2,32,1536]{2,1,0:T(8,128)S(1)}, bf16[2,32,1536]{2,1,0:T(8,128)(2,1)S(1)}) custom-call(bf16[2,2,64,256]{3,2,1,0:T(8,128)(2,1)S(1)} %pad_maximum_fusion.1.a_ref, bf16[2,2,64,256]{3,2,1,0:T(8,128)(2,1)S(1)} %pad_maximum_fusion.2.b_ref, bf16[2,2,64,256]{3,2,1,0:T(8,128)(2,1)S(1)} %collective-permute-done.21.a_far_ref, ...), custom_call_target="tpu_custom_call" | custom-call | flops 301989888 | bytes 3145728 | tf_op jit(solution)/shard_map/back_second/pallas_call | solution.py:685
  77.1 0.1 collective-permute-start.24
  77.2 2.3 %back_second.2 = (f32[2,32,1536]{2,1,0:T(8,128)S(1)}, bf16[2,32,1536]{2,1,0:T(8,128)(2,1)S(1)}, bf16[2,64,2048]{2,1,0:T(8,128)(2,1)S(1)}) custom-call(bf16[2,2,64,256]{3,2,1,0:T(8,128)(2,1)S(1)} %pad_maximum_fusion.1.a_ref, bf16[2,2,64,256]{3,2,1,0:T(8,128)(2,1)S(1)} %pad_maximum_fusion.2.b_ref, ...), custom_call_target="tpu_custom_call" | custom-call | flops 301989888 | bytes 3145728 | tf_op jit(solution)/shard_map/back_second/pallas_call | solution.py:685
  79.5 0.6 collective-permute-start.23
  80.1 1.2 %collective-permute-start.26 = (bf16[2,32,1536]{2,1,0:T(8,128)(2,1)S(1)}, bf16[2,32,1536]{2,1,0:T(8,128)(2,1)S(1)}, u32[]{:S(2)}, u32[]{:S(2)}) collective-permute-start(bf16[2,32,1536]{2,1,0:T(8,128)(2,1)S(1)} %get-tuple-element.56), channel_id=1, source_target_pairs={{0,2},{1,3},{2,0},{3,1},{4,6},{5,7},{6,4},{7,5},{8,10},{9,11},{10,... | collective-permute-start | bytes 589832 | tf_op jit(solution)/shard_map/ppermute | solution.py:80
  81.4 0.1 fusion.8
  81.4 1.0 %collective-permute-start.25 = (bf16[2,32,1536]{2,1,0:T(8,128)(2,1)S(1)}, bf16[2,32,1536]{2,1,0:T(8,128)(2,1)S(1)}, u32[]{:S(2)}, u32[]{:S(2)}) collective-permute-start(bf16[2,32,1536]{2,1,0:T(8,128)(2,1)S(1)} %get-tuple-element.58), channel_id=1, source_target_pairs={{0,2},{1,3},{2,0},{3,1},{4,6},{5,7},{6,4},{7,5},{8,10},{9,11},{10,... | collective-permute-start | bytes 589832 | tf_op jit(solution)/shard_map/ppermute | solution.py:80
  82.5 6.8 %down_score.1.refs_7_ = bf16[3072,2048]{1,0:T(8,128)(2,1)} custom-call(bf16[2,32,1024]{2,1,0:T(8,128)(2,1)S(1)} %get-tuple-element.35.refs_0_, bf16[2,32,1024]{2,1,0:T(8,128)(2,1)S(1)} %collective-permute-done.7.refs_1_, bf16[2,32,1024]{2,1,0:T(8,128)(2,1)S(1)} %get-tuple-element.41.refs_2_, bf16[2,32,1024]{2,1,0:T(8,128)(2,1)S(1)} %collective-permute-done.11.refs_3_, ...), custom_call_target="tpu_custom_call" | custom-call | flops 1610612736 | bytes 25165824 | tf_op jit(solution)/shard_map/down_score/pallas_call | solution.py:431
  89.2 2.0 %collective-permute-done.25.refs_2_ = bf16[2,32,1536]{2,1,0:T(8,128)(2,1)S(1)} collective-permute-done((bf16[2,32,1536]{2,1,0:T(8,128)(2,1)S(1)}, bf16[2,32,1536]{2,1,0:T(8,128)(2,1)S(1)}, u32[]{:S(2)}, u32[]{:S(2)}) %collective-permute-start.25) | collective-permute-done | bytes 196640 | tf_op jit(solution)/shard_map/ppermute | solution.py:80
  91.2 0.1 combined.1.rest_0_
  91.3 0.1 collective-permute-start.27
  91.4 1.4 %collective-permute-done.27.rest_1_ = bf16[32,3072]{1,0:T(8,128)(2,1)S(1)} collective-permute-done((bf16[32,3072]{1,0:T(8,128)(2,1)S(1)}, bf16[32,3072]{1,0:T(8,128)(2,1)S(1)}, u32[]{:S(2)}, u32[]{:S(2)}) %collective-permute-start.27) | collective-permute-done | bytes 196640 | tf_op jit(solution)/shard_map/ppermute | solution.py:76
  92.9 0.6 slice-done.2
  93.4 5.4 %gate_score.1 = bf16[2048,3072]{1,0:T(8,128)(2,1)} custom-call(bf16[64,2048]{1,0:T(8,128)(2,1)S(1)} %bitcast.35, bf16[32,3072]{1,0:T(8,128)(2,1)S(1)} %combined.1.rest_0_, bf16[32,3072]{1,0:T(8,128)(2,1)S(1)} %collective-permute-done.27.rest_1_, bf16[2048,3072]{1,0:T(8,128)(2,1)S(1)} %bitcast.27), custom_call_target="tpu_custom_call" | custom-call | flops 805306368 | bytes 25165824 | tf_op jit(solution)/shard_map/gate_score/pallas_call | solution.py:514
  (52 shorter events, 0.5 us)
Async XLA Ops:
  1.8 6.3 %collective-permute-start = (bf16[1,8,2048]{2,1,0:T(8,128)(2,1)S(1)}, bf16[1,8,2048]{2,1,0:T(8,128)(2,1)S(1)}, u32[]{:S(2)}, u32[]{:S(2)}) collective-permute-start(bf16[1,8,2048]{2,1,0:T(8,128)(2,1)S(1)} %norm_rows.1.refs_0_), channel_id=1, source_target_pairs={{0,16},{4,20},{8,24},{12,28},{16,0},{20,4},{24,8},{28,12},{1,17},{... | collective-permute-start | bytes 98312 | tf_op jit(solution)/shard_map/ppermute | solution.py:535
  8.1 3.9 %collective-permute-start.1 = (bf16[2,8,1024]{2,1,0:T(8,128)(2,1)S(1)}, bf16[2,8,1024]{2,1,0:T(8,128)(2,1)S(1)}, u32[]{:S(2)}, u32[]{:S(2)}) collective-permute-start(bf16[2,8,1024]{2,1,0:T(8,128)(2,1)S(1)} %get-tuple-element.29.refs_0_), channel_id=1, source_target_pairs={{0,8},{4,12},{8,0},{12,4},{16,24},{20,28},{24,16},{28,20},{1,9},{5... | collective-permute-start | bytes 98312 | tf_op jit(solution)/shard_map/ppermute | solution.py:535
  9.7 9.3 %slice-start.3 = ((s8[12582912]{0:T(1024)(128)(4,1)}), s8[4194304]{0:T(1024)(128)(4,1)S(1)}, s32[]{:S(2)}) async-start(s8[12582912]{0:T(1024)(128)(4,1)} %bitcast.28), calls=%async_computation.3 | async-start | bytes 8388608
  9.7 9.3 %slice-start.6 = ((s8[12582912]{0:T(1024)(128)(4,1)}), s8[4194304]{0:T(1024)(128)(4,1)S(1)}, s32[]{:S(2)}) async-start(s8[12582912]{0:T(1024)(128)(4,1)} %bitcast.30), calls=%async_computation.6 | async-start | bytes 8388608
  9.7 9.3 %slice-start.4 = ((s8[12582912]{0:T(1024)(128)(4,1)}), s8[4194304]{0:T(1024)(128)(4,1)S(1)}, s32[]{:S(2)}) async-start(s8[12582912]{0:T(1024)(128)(4,1)} %bitcast.28), calls=%async_computation.4 | async-start | bytes 8388608
  9.7 9.4 %slice-start.5 = ((s8[12582912]{0:T(1024)(128)(4,1)}), s8[4194304]{0:T(1024)(128)(4,1)S(1)}, s32[]{:S(2)}) async-start(s8[12582912]{0:T(1024)(128)(4,1)} %bitcast.28), calls=%async_computation.5 | async-start | bytes 8388608
  9.7 9.4 %slice-start.7 = ((s8[12582912]{0:T(1024)(128)(4,1)}), s8[4194304]{0:T(1024)(128)(4,1)S(1)}, s32[]{:S(2)}) async-start(s8[12582912]{0:T(1024)(128)(4,1)} %bitcast.30), calls=%async_computation.7 | async-start | bytes 8388608
  9.7 9.5 %slice-start.8 = ((s8[12582912]{0:T(1024)(128)(4,1)}), s8[4194304]{0:T(1024)(128)(4,1)S(1)}, s32[]{:S(2)}) async-start(s8[12582912]{0:T(1024)(128)(4,1)} %bitcast.30), calls=%async_computation.8 | async-start | bytes 8388608
  9.7 4.0 %collective-permute-start.2 = (bf16[2,8,1024]{2,1,0:T(8,128)(2,1)S(1)}, bf16[2,8,1024]{2,1,0:T(8,128)(2,1)S(1)}, u32[]{:S(2)}, u32[]{:S(2)}) collective-permute-start(bf16[2,8,1024]{2,1,0:T(8,128)(2,1)S(1)} %get-tuple-element.30.refs_1_), channel_id=1, source_target_pairs={{0,4},{4,0},{8,12},{12,8},{16,20},{20,16},{24,28},{28,24},{1,5},{5... | collective-permute-start | bytes 98312 | tf_op jit(solution)/shard_map/ppermute | solution.py:535
  13.7 5.2 %collective-permute-start.4 = (bf16[4,8,1024]{2,1,0:T(8,128)(2,1)S(1)}, bf16[4,8,1024]{2,1,0:T(8,128)(2,1)S(1)}, u32[]{:S(2)}, u32[]{:S(2)}) collective-permute-start(bf16[4,8,1024]{2,1,0:T(8,128)(2,1)S(1)} %get-tuple-element.32.b0), channel_id=1, source_target_pairs={{0,8},{4,12},{8,0},{12,4},{16,24},{20,28},{24,16},{28,20},{1,9},{5... | collective-permute-start | bytes 196616 | tf_op jit(solution)/shard_map/ppermute | solution.py:535
  14.2 4.7 %collective-permute-start.3 = (bf16[4,8,1024]{2,1,0:T(8,128)(2,1)S(1)}, bf16[4,8,1024]{2,1,0:T(8,128)(2,1)S(1)}, u32[]{:S(2)}, u32[]{:S(2)}) collective-permute-start(bf16[4,8,1024]{2,1,0:T(8,128)(2,1)S(1)} %get-tuple-element.31.refs_1_.a0), channel_id=1, source_target_pairs={{0,4},{4,0},{8,12},{12,8},{16,20},{20,16},{24,28},{28,24},{1,5},{5... | collective-permute-start | bytes 196616 | tf_op jit(solution)/shard_map/ppermute | solution.py:535
  21.5 3.9 %collective-permute-start.5 = (bf16[3,32,1024]{2,1,0:T(8,128)(2,1)S(1)}, bf16[3,32,1024]{2,1,0:T(8,128)(2,1)S(1)}, u32[]{:S(2)}, u32[]{:S(2)}) collective-permute-start(bf16[3,32,1024]{2,1,0:T(8,128)(2,1)S(1)} %get-tuple-element.34), channel_id=1, source_target_pairs={{0,1},{1,0},{2,3},{3,2},{4,5},{5,4},{6,7},{7,6},{8,9},{9,8},{10,11... | collective-permute-start | bytes 589832 | tf_op jit(solution)/shard_map/ppermute | solution.py:76
  24.8 5.5 %collective-permute-start.8 = (bf16[3,32,1024]{2,1,0:T(8,128)(2,1)S(1)}, bf16[3,32,1024]{2,1,0:T(8,128)(2,1)S(1)}, u32[]{:S(2)}, u32[]{:S(2)}) collective-permute-start(bf16[3,32,1024]{2,1,0:T(8,128)(2,1)S(1)} %get-tuple-element.37), channel_id=1, source_target_pairs={{0,1},{1,0},{2,3},{3,2},{4,5},{5,4},{6,7},{7,6},{8,9},{9,8},{10,11... | collective-permute-start | bytes 589832 | tf_op jit(solution)/shard_map/ppermute | solution.py:76
  25.5 7.2 %collective-permute-start.6 = (bf16[3,32,1024]{2,1,0:T(8,128)(2,1)S(1)}, bf16[3,32,1024]{2,1,0:T(8,128)(2,1)S(1)}, u32[]{:S(2)}, u32[]{:S(2)}) collective-permute-start(bf16[3,32,1024]{2,1,0:T(8,128)(2,1)S(1)} %get-tuple-element.64.rest_0_), channel_id=1, source_target_pairs={{0,2},{1,3},{2,0},{3,1},{4,6},{5,7},{6,4},{7,5},{8,10},{9,11},{10,... | collective-permute-start | bytes 589832 | tf_op jit(solution)/shard_map/ppermute | solution.py:80
  30.3 1.5 %collective-permute-start.10 = (bf16[3,32,1024]{2,1,0:T(8,128)(2,1)S(1)}, bf16[3,32,1024]{2,1,0:T(8,128)(2,1)S(1)}, u32[]{:S(2)}, u32[]{:S(2)}) collective-permute-start(bf16[3,32,1024]{2,1,0:T(8,128)(2,1)S(1)} %get-tuple-element.39), channel_id=1, source_target_pairs={{0,1},{1,0},{2,3},{3,2},{4,5},{5,4},{6,7},{7,6},{8,9},{9,8},{10,11... | collective-permute-start | bytes 589832 | tf_op jit(solution)/shard_map/ppermute | solution.py:76
  30.4 10.8 %collective-permute-start.9 = (bf16[3,32,1024]{2,1,0:T(8,128)(2,1)S(1)}, bf16[3,32,1024]{2,1,0:T(8,128)(2,1)S(1)}, u32[]{:S(2)}, u32[]{:S(2)}) collective-permute-start(bf16[3,32,1024]{2,1,0:T(8,128)(2,1)S(1)} %get-tuple-element.62), channel_id=1, source_target_pairs={{0,2},{1,3},{2,0},{3,1},{4,6},{5,7},{6,4},{7,5},{8,10},{9,11},{10,... | collective-permute-start | bytes 589832 | tf_op jit(solution)/shard_map/ppermute | solution.py:80
  31.8 10.1 %collective-permute-start.12 = (bf16[3,32,1024]{2,1,0:T(8,128)(2,1)S(1)}, bf16[3,32,1024]{2,1,0:T(8,128)(2,1)S(1)}, u32[]{:S(2)}, u32[]{:S(2)}) collective-permute-start(bf16[3,32,1024]{2,1,0:T(8,128)(2,1)S(1)} %get-tuple-element.60.refs_2_), channel_id=1, source_target_pairs={{0,2},{1,3},{2,0},{3,1},{4,6},{5,7},{6,4},{7,5},{8,10},{9,11},{10,... | collective-permute-start | bytes 589832 | tf_op jit(solution)/shard_map/ppermute | solution.py:80
  32.8 9.4 %collective-permute-start.7 = (bf16[2,32,1024]{2,1,0:T(8,128)(2,1)S(1)}, bf16[2,32,1024]{2,1,0:T(8,128)(2,1)S(1)}, u32[]{:S(2)}, u32[]{:S(2)}) collective-permute-start(bf16[2,32,1024]{2,1,0:T(8,128)(2,1)S(1)} %get-tuple-element.35.refs_0_), channel_id=1, source_target_pairs={{0,1},{1,0},{2,3},{3,2},{4,5},{5,4},{6,7},{7,6},{8,9},{9,8},{10,11... | collective-permute-start | bytes 393224 | tf_op jit(solution)/shard_map/ppermute | solution.py:76
  41.3 1.5 %collective-permute-start.11 = (bf16[2,32,1024]{2,1,0:T(8,128)(2,1)S(1)}, bf16[2,32,1024]{2,1,0:T(8,128)(2,1)S(1)}, u32[]{:S(2)}, u32[]{:S(2)}) collective-permute-start(bf16[2,32,1024]{2,1,0:T(8,128)(2,1)S(1)} %get-tuple-element.41.refs_2_), channel_id=1, source_target_pairs={{0,1},{1,0},{2,3},{3,2},{4,5},{5,4},{6,7},{7,6},{8,9},{9,8},{10,11... | collective-permute-start | bytes 393224 | tf_op jit(solution)/shard_map/ppermute | solution.py:76
  42.1 1.4 %collective-permute-start.13 = (bf16[2,32,1024]{2,1,0:T(8,128)(2,1)S(1)}, bf16[2,32,1024]{2,1,0:T(8,128)(2,1)S(1)}, u32[]{:S(2)}, u32[]{:S(2)}) collective-permute-start(bf16[2,32,1024]{2,1,0:T(8,128)(2,1)S(1)} %get-tuple-element.42.refs_4_), channel_id=1, source_target_pairs={{0,1},{1,0},{2,3},{3,2},{4,5},{5,4},{6,7},{7,6},{8,9},{9,8},{10,11... | collective-permute-start | bytes 393224 | tf_op jit(solution)/shard_map/ppermute | solution.py:76
  44.7 5.9 %collective-permute-start.14 = (bf16[2,2,64,256]{3,2,1,0:T(8,128)(2,1)S(1)}, bf16[2,2,64,256]{3,2,1,0:T(8,128)(2,1)S(1)}, u32[]{:S(2)}, u32[]{:S(2)}) collective-permute-start(bf16[2,2,64,256]{3,2,1,0:T(8,128)(2,1)S(1)} %pieces_away.2.refs_8_), channel_id=1, source_target_pairs={{0,4},{4,0},{8,12},{12,8},{16,20},{20,16},{24,28},{28,24},{1,5},{5... | collective-permute-start | bytes 393224 | tf_op jit(solution)/shard_map/ppermute | solution.py:535
  47.4 17.1 %copy-start = (bf16[64,2048]{1,0:T(8,128)(2,1)S(1)}, bf16[64,2048]{1,0:T(8,128)(2,1)}, u32[]{:S(2)}) copy-start(bf16[64,2048]{1,0:T(8,128)(2,1)} %target_ref.1) | copy-start | bytes 786436
  47.4 5.3 %collective-permute-start.16 = (bf16[2,2,64,256]{3,2,1,0:T(8,128)(2,1)S(1)}, bf16[2,2,64,256]{3,2,1,0:T(8,128)(2,1)S(1)}, u32[]{:S(2)}, u32[]{:S(2)}) collective-permute-start(bf16[2,2,64,256]{3,2,1,0:T(8,128)(2,1)S(1)} %pieces_away.3), channel_id=1, source_target_pairs={{0,8},{4,12},{8,0},{12,4},{16,24},{20,28},{24,16},{28,20},{1,9},{5... | collective-permute-start | bytes 393224 | tf_op jit(solution)/shard_map/ppermute | solution.py:535
  50.6 4.3 %collective-permute-start.15 = (bf16[2,64,256]{2,1,0:T(8,128)(2,1)S(1)}, bf16[2,64,256]{2,1,0:T(8,128)(2,1)S(1)}, u32[]{:S(2)}, u32[]{:S(2)}) collective-permute-start(bf16[2,64,256]{2,1,0:T(8,128)(2,1)S(1)} %fusion.4), channel_id=1, source_target_pairs={{0,8},{4,12},{8,0},{12,4},{16,24},{20,28},{24,16},{28,20},{1,9},{5... | collective-permute-start | bytes 196616 | tf_op jit(solution)/shard_map/ppermute | solution.py:535
  52.8 4.3 %collective-permute-start.17 = (bf16[2,64,256]{2,1,0:T(8,128)(2,1)S(1)}, bf16[2,64,256]{2,1,0:T(8,128)(2,1)S(1)}, u32[]{:S(2)}, u32[]{:S(2)}) collective-permute-start(bf16[2,64,256]{2,1,0:T(8,128)(2,1)S(1)} %fusion.5), channel_id=1, source_target_pairs={{0,4},{4,0},{8,12},{12,8},{16,20},{20,16},{24,28},{28,24},{1,5},{5... | collective-permute-start | bytes 196616 | tf_op jit(solution)/shard_map/ppermute | solution.py:535
  57.1 7.3 %collective-permute-start.18 = (bf16[2,2,64,256]{3,2,1,0:T(8,128)(2,1)S(1)}, bf16[2,2,64,256]{3,2,1,0:T(8,128)(2,1)S(1)}, u32[]{:S(2)}, u32[]{:S(2)}) collective-permute-start(bf16[2,2,64,256]{3,2,1,0:T(8,128)(2,1)S(1)} %fusion.6), channel_id=1, source_target_pairs={{0,16},{4,20},{8,24},{12,28},{16,0},{20,4},{24,8},{28,12},{1,17},{... | collective-permute-start | bytes 393224 | tf_op jit(solution)/shard_map/ppermute | solution.py:535
  64.5 5.0 %collective-permute-start.20 = (bf16[2,64,256]{2,1,0:T(8,128)(2,1)S(1)}, bf16[2,64,256]{2,1,0:T(8,128)(2,1)S(1)}, u32[]{:S(2)}, u32[]{:S(2)}) collective-permute-start(bf16[2,64,256]{2,1,0:T(8,128)(2,1)S(1)} %get-tuple-element.47), channel_id=1, source_target_pairs={{0,4},{4,0},{8,12},{12,8},{16,20},{20,16},{24,28},{28,24},{1,5},{5... | collective-permute-start | bytes 196616 | tf_op jit(solution)/shard_map/ppermute | solution.py:535
  65.3 4.3 %collective-permute-start.19 = (bf16[2,64,256]{2,1,0:T(8,128)(2,1)S(1)}, bf16[2,64,256]{2,1,0:T(8,128)(2,1)S(1)}, u32[]{:S(2)}, u32[]{:S(2)}) collective-permute-start(bf16[2,64,256]{2,1,0:T(8,128)(2,1)S(1)} %get-tuple-element.46), channel_id=1, source_target_pairs={{0,8},{4,12},{8,0},{12,4},{16,24},{20,28},{24,16},{28,20},{1,9},{5... | collective-permute-start | bytes 196616 | tf_op jit(solution)/shard_map/ppermute | solution.py:535
  69.5 5.3 %collective-permute-start.22 = (bf16[2,2,64,256]{3,2,1,0:T(8,128)(2,1)S(1)}, bf16[2,2,64,256]{3,2,1,0:T(8,128)(2,1)S(1)}, u32[]{:S(2)}, u32[]{:S(2)}) collective-permute-start(bf16[2,2,64,256]{3,2,1,0:T(8,128)(2,1)S(1)} %pad_maximum_fusion.2.b_ref), channel_id=1, source_target_pairs={{0,8},{4,12},{8,0},{12,4},{16,24},{20,28},{24,16},{28,20},{1,9},{5... | collective-permute-start | bytes 393224 | tf_op jit(solution)/shard_map/ppermute | solution.py:535
  69.6 5.2 %collective-permute-start.21 = (bf16[2,2,64,256]{3,2,1,0:T(8,128)(2,1)S(1)}, bf16[2,2,64,256]{3,2,1,0:T(8,128)(2,1)S(1)}, u32[]{:S(2)}, u32[]{:S(2)}) collective-permute-start(bf16[2,2,64,256]{3,2,1,0:T(8,128)(2,1)S(1)} %pad_maximum_fusion.1.a_ref), channel_id=1, source_target_pairs={{0,4},{4,0},{8,12},{12,8},{16,20},{20,16},{24,28},{28,24},{1,5},{5... | collective-permute-start | bytes 393224 | tf_op jit(solution)/shard_map/ppermute | solution.py:535
  77.1 3.0 %collective-permute-start.24 = (bf16[2,32,1536]{2,1,0:T(8,128)(2,1)S(1)}, bf16[2,32,1536]{2,1,0:T(8,128)(2,1)S(1)}, u32[]{:S(2)}, u32[]{:S(2)}) collective-permute-start(bf16[2,32,1536]{2,1,0:T(8,128)(2,1)S(1)} %get-tuple-element.51), channel_id=1, source_target_pairs={{0,1},{1,0},{2,3},{3,2},{4,5},{5,4},{6,7},{7,6},{8,9},{9,8},{10,11... | collective-permute-start | bytes 589832 | tf_op jit(solution)/shard_map/ppermute | solution.py:76
  79.5 1.9 %collective-permute-start.23 = (bf16[2,32,1536]{2,1,0:T(8,128)(2,1)S(1)}, bf16[2,32,1536]{2,1,0:T(8,128)(2,1)S(1)}, u32[]{:S(2)}, u32[]{:S(2)}) collective-permute-start(bf16[2,32,1536]{2,1,0:T(8,128)(2,1)S(1)} %get-tuple-element.49), channel_id=1, source_target_pairs={{0,1},{1,0},{2,3},{3,2},{4,5},{5,4},{6,7},{7,6},{8,9},{9,8},{10,11... | collective-permute-start | bytes 589832 | tf_op jit(solution)/shard_map/ppermute | solution.py:76
  80.1 9.1 %collective-permute-start.26 = (bf16[2,32,1536]{2,1,0:T(8,128)(2,1)S(1)}, bf16[2,32,1536]{2,1,0:T(8,128)(2,1)S(1)}, u32[]{:S(2)}, u32[]{:S(2)}) collective-permute-start(bf16[2,32,1536]{2,1,0:T(8,128)(2,1)S(1)} %get-tuple-element.56), channel_id=1, source_target_pairs={{0,2},{1,3},{2,0},{3,1},{4,6},{5,7},{6,4},{7,5},{8,10},{9,11},{10,... | collective-permute-start | bytes 589832 | tf_op jit(solution)/shard_map/ppermute | solution.py:80
  81.4 9.8 %collective-permute-start.25 = (bf16[2,32,1536]{2,1,0:T(8,128)(2,1)S(1)}, bf16[2,32,1536]{2,1,0:T(8,128)(2,1)S(1)}, u32[]{:S(2)}, u32[]{:S(2)}) collective-permute-start(bf16[2,32,1536]{2,1,0:T(8,128)(2,1)S(1)} %get-tuple-element.58), channel_id=1, source_target_pairs={{0,2},{1,3},{2,0},{3,1},{4,6},{5,7},{6,4},{7,5},{8,10},{9,11},{10,... | collective-permute-start | bytes 589832 | tf_op jit(solution)/shard_map/ppermute | solution.py:80
  82.5 10.4 %slice-start = ((s8[12582912]{0:T(1024)(128)(4,1)}), s8[4194304]{0:T(1024)(128)(4,1)S(1)}, s32[]{:S(2)}) async-start(s8[12582912]{0:T(1024)(128)(4,1)} %bitcast.26), calls=%async_computation | async-start | bytes 8388608
  82.5 10.4 %slice-start.1 = ((s8[12582912]{0:T(1024)(128)(4,1)}), s8[4194304]{0:T(1024)(128)(4,1)S(1)}, s32[]{:S(2)}) async-start(s8[12582912]{0:T(1024)(128)(4,1)} %bitcast.26), calls=%async_computation.1 | async-start | bytes 8388608
  91.2 2.2 %slice-start.2 = ((s8[12582912]{0:T(1024)(128)(4,1)}), s8[4194304]{0:T(1024)(128)(4,1)S(1)}, s32[]{:S(2)}) async-start(s8[12582912]{0:T(1024)(128)(4,1)} %bitcast.26), calls=%async_computation.2 | async-start | bytes 8388608
  91.3 1.5 %collective-permute-start.27 = (bf16[32,3072]{1,0:T(8,128)(2,1)S(1)}, bf16[32,3072]{1,0:T(8,128)(2,1)S(1)}, u32[]{:S(2)}, u32[]{:S(2)}) collective-permute-start(bf16[32,3072]{1,0:T(8,128)(2,1)S(1)} %combined.1.rest_0_), channel_id=1, source_target_pairs={{0,1},{1,0},{2,3},{3,2},{4,5},{5,4},{6,7},{7,6},{8,9},{9,8},{10,11... | collective-permute-start | bytes 589832 | tf_op jit(solution)/shard_map/ppermute | solution.py:76
